TPU v7x, 256 devices: a whole 4x4x8 slice. The times are simulated.
256 devices in a mesh: depth: 4 (over x), col: 64 (over z, y, core).
Axes of the slice: x: 4, y: 4, z: 8, core: 2. Of those that a mesh axis runs over, the one named last changes fastest.
Arguments:
- raw_views: bfloat16 [8, 32, 8, 8192], P('depth', None, None, 'col'), may hold values from -48 to 48
- feat_weight: bfloat16 [9, 32, 32], replicated, may hold values from -0.375 to 0.375
- shifts: int32 [8, 96], replicated, may hold values from 0 to 127, as said below
- frame_range: int32 [8, 2], replicated, may hold values from 0 to 8192, as said below
- cost_weight: bfloat16 [27, 8, 32], replicated, may hold values from -0.21875 to 0.21875
- mid_weight: bfloat16 [27, 8, 8], replicated, may hold values from -0.4375 to 0.4375
- final_weight: bfloat16 [27, 8], replicated, may hold values from -17 to 17
Outputs:
- estimate: float32 [8, 8192], P(None, 'col')
Inputs may be any that keep to these rules, and one draw needn't show every extreme that they name: `shifts`: shifts of view 0 are all zero; the largest shift is exactly 127. `frame_range`: row v holds the first and one past the last valid column of view v, the first below the second; view 0 is valid over all 8192 columns.
All inputs are finite; a program needn't handle non-finite values.
Results may differ from a plain program's by a relative error of at most 0.007.
The roundings to bfloat16 on the way count: a program that leaves them out, or rounds other values in their place, can miss the bound.
Values may be sent and summed in bfloat16 or wider, within the bound.
No kernel may reach another device: no remote copies, remote signals or barrier semaphores. Data moves between devices by JAX's collectives and lax.ppermute only.
A program may use at most 64 MiB of HBM per device.

v0:
```python
import jax
import jax.numpy as jnp
from jax import lax
from jax.sharding import PartitionSpec as P

norm_eps = 1e-05


def extended_2(x, sides, width):
    for axis, dim in sides:
        peers, length = (lax.axis_size(axis), x.shape[dim])
        up = [(i, (i + 1) % peers) for i in range(peers - 1)]
        down = [(j, i) for i, j in up]
        last = lax.slice_in_dim(x, length - width, length, axis=dim)
        initial = lax.slice_in_dim(x, 0, width, axis=dim)
        before = lax.ppermute(last, axis, up)
        after = lax.ppermute(initial, axis, down)
        x = jnp.concatenate([before, x, after], axis=dim)
    return x


def shifted(x, axis, by):
    peers = lax.axis_size(axis)
    pairs = [(i, i + by) for i in range(peers) if 0 <= i + by < peers]
    return lax.ppermute(x, axis, pairs)


def merged_2(x, axis, combine):
    everything = jax.tree.map(lambda part: lax.all_gather(part, axis), x)
    initial = jax.tree.map(lambda part: part[0], everything)

    def hop(k, so_far):
        return combine(so_far, jax.tree.map(lambda part: part[k], everything))

    return lax.fori_loop(1, lax.axis_size(axis), hop, initial)


def conv_block(window, weights):
    taps, out_count, in_count = weights.shape
    kernel = weights.reshape(3, 3, 3, out_count, in_count)
    numbers = lax.ConvDimensionNumbers(
        lhs_spec=(0, 2, 1, 3, 4), rhs_spec=(3, 4, 0, 1, 2), out_spec=(0, 2, 1, 3, 4)
    )
    result = lax.conv_general_dilated(
        window[None],
        kernel,
        (1, 1, 1),
        ((0, 0), (1, 1), (0, 0)),
        dimension_numbers=numbers,
        preferred_element_type=jnp.float32,
    )
    return result[0]


def with_rim(values):
    return extended_2(values, (("depth", 0), ("col", 3)), 1)


def normalize(values, voxels):
    average = lax.psum(jnp.sum(values, axis=(0, 2, 3)), ("depth", "col")) / voxels
    centered = values - average[None, :, None, None]
    spread = lax.psum(jnp.sum(centered * centered, axis=(0, 2, 3)), ("depth", "col")) / voxels
    return jnp.maximum(centered * lax.rsqrt(spread + norm_eps)[None, :, None, None], 0.0).astype(
        jnp.bfloat16
    )


def local(raw_views, feat_weight, shifts, frame_range, cost_weight, mid_weight, final_weight):
    view_local, channels, row_count, col_count = raw_views.shape
    depths_all = shifts.shape[1]
    depth_local = depths_all // lax.axis_size("depth")
    first_depth = lax.axis_index("depth") * depth_local
    first_col = lax.axis_index("col") * col_count
    total_cols = col_count * lax.axis_size("col")
    widened_views = extended_2(raw_views, (("col", 3),), 1)
    padded_views = jnp.pad(widened_views, ((0, 0), (0, 0), (1, 1), (0, 0)))
    summed = None
    for kernel_tap in range(9):
        row_off = kernel_tap // 3
        col_off = kernel_tap % 3
        window = padded_views[:, :, row_off : row_off + row_count, col_off : col_off + col_count]
        term = jnp.einsum(
            "oi,vihw->vohw", feat_weight[kernel_tap], window, preferred_element_type=jnp.float32
        )
        summed = term if summed is None else summed + term
    features = summed.astype(jnp.bfloat16)
    all_views = lax.all_gather(features, "depth", axis=0, tiled=True)
    left_strip = shifted(all_views, "col", 1)
    extended = jnp.concatenate([left_strip, all_views], axis=3)

    def one_depth(depth_step):
        depth_idx = first_depth + depth_step
        clipped = jnp.clip(depth_idx, 0, depths_all - 1)
        view_shift = lax.dynamic_index_in_dim(shifts, clipped, axis=1, keepdims=False)

        def slide(view_plane, shift_one):
            return lax.dynamic_slice_in_dim(view_plane, col_count - shift_one, col_count, axis=2)

        moved = jax.vmap(slide)(extended, view_shift)
        columns = first_col + jnp.arange(col_count, dtype=jnp.int32)
        src_cols = columns[None, :] - view_shift[:, None]
        inside = (src_cols >= frame_range[:, 0:1]) & (src_cols < frame_range[:, 1:2])
        weight_mask = inside.astype(jnp.float32)[:, None, None, :]
        tally = jnp.sum(weight_mask, axis=0)
        values = moved.astype(jnp.float32)
        average = jnp.sum(weight_mask * values, axis=0) / tally
        deviation = values - average
        spread = jnp.sum(weight_mask * deviation * deviation, axis=0) / tally
        keep = (depth_idx >= 0) & (depth_idx < depths_all) & (columns >= 0) & (columns < total_cols)
        return jnp.where(keep[None, None, :], spread, 0.0).astype(jnp.bfloat16)

    volume = lax.map(one_depth, jnp.arange(depth_local, dtype=jnp.int32))
    framed = extended_2(volume, (("depth", 0), ("col", 3)), 1)
    voxels = float(
        depth_local * row_count * col_count * lax.axis_size("depth") * lax.axis_size("col")
    )
    first_conv = conv_block(framed, cost_weight)
    first_act = normalize(first_conv, voxels)
    second_conv = conv_block(with_rim(first_act), mid_weight)
    second_act = normalize(second_conv, voxels)
    score = conv_block(with_rim(second_act), final_weight[:, None, :])[:, 0]
    depth_value = (first_depth + jnp.arange(depth_local, dtype=jnp.int32)).astype(jnp.float32) / (
        depths_all - 1
    )
    peak_value = jnp.max(score, axis=0)
    exponent = jnp.exp(score - peak_value[None])
    local_total = jnp.sum(exponent, axis=0)
    local_weighted = jnp.sum(exponent * depth_value[:, None, None], axis=0)

    def combine(earlier, later):
        highest = jnp.maximum(earlier[0], later[0])
        scale_early = jnp.exp(earlier[0] - highest)
        scale_late = jnp.exp(later[0] - highest)
        return (
            highest,
            earlier[1] * scale_early + later[1] * scale_late,
            earlier[2] * scale_early + later[2] * scale_late,
        )

    merged = merged_2((peak_value, local_total, local_weighted), "depth", combine)
    return merged[2] / merged[1]


def solution(mesh):
    in_specs = (P("depth", None, None, "col"), P(), P(), P(), P(), P(), P())
    out_specs = P(None, "col")
    return jax.shard_map(local, mesh=mesh, in_specs=in_specs, out_specs=out_specs, check_vma=False)
```

profile of v0, /device:TPU:2, one launch (start us, length us, event | category | flops | bytes accessed | tf_op | source)
XLA Modules:
  0.0 845.5 jit_solution(18421079025314636510)
XLA Ops:
  5.2 2.2 collective-permute-done.1
  15.1 12.8 %all_gather.21 = bf16[8,32,8,128]{3,2,1,0:T(8,128)(2,1)S(1)} all-gather(bf16[2,32,8,128]{3,2,1,0:T(8,128)(2,1)S(1)} %copy.111), channel_id=1, replica_groups=mesh['depth'=4,'col'=64] {'depth'}, dimensions={0}, use_global_device_ids=true | all-gather | bytes 655360 | tf_op jit(solution)/shard_map/all_gather | solution.py:87
  28.0 3.9 collective-permute-start.2
  33.5 7.2 copy.113
  40.7 218.3 %while.31 = (s32[]{:T(128)}, bf16[24,32,8,128]{3,2,1,0:T(8,128)(2,1)}, s32[24]{0:T(128)S(1)}, s32[]{:T(128)}, s32[]{:T(128)}, /*index=5*/s32[8,96]{0,1:T(8,128)S...) while((s32[]{:T(128)}, ...), condition=%wide.region_4.5_spmd, body=%wide.region_0.4_spmd.sunk | while | flops 2174672 | bytes 3228135 | solution.py:112
  42.0 3.5 gather_fusion
  51.1 3.5 gather_fusion
  60.2 3.5 gather_fusion
  69.3 3.5 gather_fusion
  78.4 3.5 gather_fusion
  87.5 3.5 gather_fusion
  96.6 3.5 gather_fusion
  105.7 3.5 gather_fusion
  114.8 3.5 gather_fusion
  123.8 3.5 gather_fusion
  132.9 3.5 gather_fusion
  142.0 3.5 gather_fusion
  151.1 3.5 gather_fusion
  160.2 3.5 gather_fusion
  169.3 3.5 gather_fusion
  178.4 3.5 gather_fusion
  187.5 3.5 gather_fusion
  196.6 3.5 gather_fusion
  205.7 3.5 gather_fusion
  214.8 3.5 gather_fusion
  223.9 3.5 gather_fusion
  233.0 3.5 gather_fusion
  242.1 3.5 gather_fusion
  251.2 3.5 gather_fusion
  261.9 3.9 collective-permute-start.4
  266.1 2.5 collective-permute-done.4
  270.3 6.1 copy.117
  277.2 7.5 collective-permute-start.5
  286.2 4.8 collective-permute-done.6
  291.0 7.5 maximum_bitcast_fusion
  298.5 4.9 pad.9
  303.4 4.1 copy.121
  308.9 24.7 %select_reduce_fusion.1 = (f32[8]{0:T(128)S(1)}, f32[24,8,8,17,8]{4,2,3,1,0:T(8,128)}) fusion(pred[8,17]{0,1:T(8,128)(4,1)S(1)} %copy-done.6, bf16[3,3,3,8,32]{4,3,2,1,0:T(8,128)(2,1)S(1)} %bitcast.195, bf16[26,32,8,1,7,2]{1,4,5,2,0,3:T(8,128)(2,1)S(1)} %slice.180, bf16[26,32,8,1,8,17]{1,4,5,2,0,3:T(8,128)(2,1)} %copy.121), kind=kOutput, calls=%fused_computation.42 | convolution fusion | flops 337588224 | bytes 2846376 | tf_op jit(solution)/shard_map/conv_general_dilated | solution.py:44
  333.7 13.8 %copy.122 = f32[24,8,8,17,8]{3,2,4,1,0:T(8,128)} copy(f32[24,8,8,17,8]{4,2,3,1,0:T(8,128)} %get-tuple-element.381) | data formatting | bytes 1671168 | tf_op jit(solution)/shard_map/conv_general_dilated | solution.py:44
  347.5 4.2 reshape.192
  351.7 90.8 %psum.28 = f32[8]{0:T(128)S(1)} all-reduce(f32[8]{0:T(128)S(1)} %get-tuple-element.380), channel_id=1, replica_groups=mesh['depth'=4,'col'=64] {'depth','col'}, use_global_device_ids=true, to_apply=%region_6.7 | all-reduce | flops 8 | bytes 64 | tf_op jit(solution)/shard_map/psum | solution.py:60
  442.9 73.4 %psum.29 = f32[8]{0:T(128)S(1)} all-reduce(f32[8]{0:T(128)S(1)} %multiply_reduce_fusion.1), channel_id=1, replica_groups=mesh['depth'=4,'col'=64] {'depth','col'}, use_global_device_ids=true, to_apply=%region_8.9 | all-reduce | flops 8 | bytes 64 | tf_op jit(solution)/shard_map/psum | solution.py:62
  516.5 2.2 collective-permute-start.7
  518.7 3.7 collective-permute-start.8
  522.4 2.3 collective-permute-done.8
  526.3 3.1 collective-permute-start.9
  532.3 3.8 reshape.250
  536.1 11.8 %copy.125 = bf16[26,8,8,1,8,17]{1,4,5,2,0,3:T(8,128)(2,1)} copy(bf16[26,8,8,1,8,17]{5,4,1,2,0,3:T(8,128)(2,1)S(1)} %reshape.250) | data formatting | bytes 905216 | tf_op jit(solution)/shard_map/conv_general_dilated | solution.py:44
  549.4 20.1 %select_reduce_fusion = (f32[8]{0:T(128)S(1)}, f32[24,8,8,17,8]{4,2,3,1,0:T(8,128)}) fusion(pred[8,17]{0,1:T(8,128)(4,1)S(1)} %copy-done.6, bf16[3,3,3,8,8]{4,3,2,1,0:T(8,128)(2,1)S(1)} %bitcast.200, bf16[26,8,8,1,7,2]{1,4,5,2,0,3:T(8,128)(2,1)S(1)} %slice.186, bf16[26,8,8,1,8,17]{1,4,5,2,0,3:T(8,128)(2,1)} %copy.125), kind=kOutput, calls=%fused_computation.41 | convolution fusion | flops 84867064 | bytes 1338408 | tf_op jit(solution)/shard_map/conv_general_dilated | solution.py:44
  569.5 13.8 %copy.127 = f32[24,8,8,17,8]{3,2,4,1,0:T(8,128)} copy(f32[24,8,8,17,8]{4,2,3,1,0:T(8,128)} %get-tuple-element.383) | data formatting | bytes 1671168 | tf_op jit(solution)/shard_map/conv_general_dilated | solution.py:44
  583.3 4.2 reshape.200
  587.5 81.0 %psum.30 = f32[8]{0:T(128)S(1)} all-reduce(f32[8]{0:T(128)S(1)} %get-tuple-element.382), channel_id=1, replica_groups=mesh['depth'=4,'col'=64] {'depth','col'}, use_global_device_ids=true, to_apply=%region_10.11 | all-reduce | flops 8 | bytes 64 | tf_op jit(solution)/shard_map/psum | solution.py:60
  668.9 75.0 %psum.31 = f32[8]{0:T(128)S(1)} all-reduce(f32[8]{0:T(128)S(1)} %multiply_reduce_fusion), channel_id=1, replica_groups=mesh['depth'=4,'col'=64] {'depth','col'}, use_global_device_ids=true, to_apply=%region_12.13 | all-reduce | flops 8 | bytes 64 | tf_op jit(solution)/shard_map/psum | solution.py:62
  744.1 2.1 collective-permute-start.11
  746.3 3.7 collective-permute-start.12
  750.0 2.3 collective-permute-done.12
  755.3 3.5 collective-permute-done.14
  760.5 3.8 reshape.251
  764.3 11.8 %copy.130 = bf16[26,8,8,1,8,17]{1,4,5,2,0,3:T(8,128)(2,1)} copy(bf16[26,8,8,1,8,17]{5,4,1,2,0,3:T(8,128)(2,1)S(1)} %reshape.251) | data formatting | bytes 905216 | tf_op jit(solution)/shard_map/conv_general_dilated | solution.py:44
  777.6 19.8 %convolution_select_fusion = f32[24,8,8,17,1]{4,2,3,1,0:T(8,128)} fusion(bf16[3,3,3,1,8]{4,3,2,1,0:T(2,128)(2,1)S(1)} %reshape_broadcast_in_dim.4, bf16[26,8,8,1,7,2]{1,4,5,2,0,3:T(8,128)(2,1)S(1)} %slice.192, bf16[26,8,8,1,8,17]{1,4,5,2,0,3:T(8,128)(2,1)} %copy.130, pred[8,17]{0,1:T(8,128)(4,1)S(1)} %copy-done.6), kind=kOutput, calls=%fused_computation.43 | convolution fusion | flops 11884032 | bytes 604216 | tf_op jit(solution)/shard_map/conv_general_dilated | solution.py:44
  797.4 11.9 %copy.133 = f32[24,8,8,17,1]{3,2,1,0,4:T(8,128)S(1)} copy(f32[24,8,8,17,1]{4,2,3,1,0:T(8,128)} %convolution_select_fusion) | data formatting | bytes 208896 | tf_op jit(solution)/shard_map/conv_general_dilated | solution.py:44
  809.6 10.7 %all-gather = f32[32,128]{1,0:T(8,128)S(1)} all-gather(f32[8,128]{1,0:T(8,128)S(1)} %slice_reduce_fusion), channel_id=2, replica_groups=mesh['depth'=4,'col'=64] {'depth'}, dimensions={0}, use_global_device_ids=true | all-gather | bytes 20480 | tf_op jit(solution)/shard_map/all_gather | solution.py:29
  820.4 11.9 %all-gather.1 = f32[32,128]{1,0:T(8,128)S(1)} all-gather(f32[8,128]{1,0:T(8,128)S(1)} %get-tuple-element.327), channel_id=3, replica_groups=mesh['depth'=4,'col'=64] {'depth'}, dimensions={0}, use_global_device_ids=true | all-gather | bytes 20480 | tf_op jit(solution)/shard_map/all_gather | solution.py:29
  832.3 11.9 %all-gather.2 = f32[32,128]{1,0:T(8,128)S(1)} all-gather(f32[8,128]{1,0:T(8,128)S(1)} %get-tuple-element.326), channel_id=4, replica_groups=mesh['depth'=4,'col'=64] {'depth'}, dimensions={0}, use_global_device_ids=true | all-gather | bytes 20480 | tf_op jit(solution)/shard_map/all_gather | solution.py:29
  (380 shorter events, 155.5 us)
Async XLA Ops:
  0.0 308.9 %copy-start = (bf16[27,8,32]{2,1,0:T(8,128)(2,1)S(1)}, bf16[27,8,32]{2,1,0:T(8,128)(2,1)}, u32[]{:S(2)}) copy-start(bf16[27,8,32]{2,1,0:T(8,128)(2,1)} %param.15) | copy-start | bytes 41476
  0.0 31.9 %copy-start.4 = (s32[8,96]{1,0:T(8,128)S(1)}, s32[8,96]{1,0:T(8,128)}, u32[]{:S(2)}) copy-start(s32[8,96]{1,0:T(8,128)} %param.13) | copy-start | bytes 9220
  1.1 4.1 collective-permute-start
  2.8 4.6 collective-permute-start.1
  10.3 30.4 %copy-start.2 = (s32[8,2]{0,1:T(2,128)S(1)}, s32[8,2]{0,1:T(2,128)}, u32[]{:S(2)}) copy-start(s32[8,2]{0,1:T(2,128)} %param.14) | copy-start | bytes 196
  28.0 5.4 collective-permute-start.2
  259.9 6.2 collective-permute-start.3
  261.9 6.8 collective-permute-start.4
  277.2 9.0 %collective-permute-start.5 = (bf16[26,32,8,1]{1,2,3,0:T(8,128)(2,1)S(1)}, bf16[26,32,8,1]{1,2,3,0:T(8,128)(2,1)S(1)}, u32[]{:S(2)}, u32[]{:S(2)}) collective-permute-start(bf16[26,32,8,1]{1,2,3,0:T(8,128)(2,1)S(1)} %get-tuple-element.366), channel_id=1, source_target_pairs={{0,1},{1,2},{2,3},{3,4},{4,5},{5,6},{6,7},{7,8},{8,9},{9,10},{10,1... | collective-permute-start | bytes 39944 | tf_op jit(solution)/shard_map/ppermute | solution.py:16
  284.7 6.3 collective-permute-start.6
  303.4 5.5 copy-start.6
  347.5 181.9 %copy-start.3 = (bf16[27,8,8]{0,2,1:T(8,128)(2,1)S(1)}, bf16[27,8,8]{0,2,1:T(8,128)(2,1)}, u32[]{:S(2)}) copy-start(bf16[27,8,8]{0,2,1:T(8,128)(2,1)} %param.16) | copy-start | bytes 10372
  516.5 5.9 collective-permute-start.7
  518.7 6.0 collective-permute-start.8
  525.0 4.5 collective-permute-start.10
  526.3 4.4 collective-permute-start.9
  583.3 171.9 %copy-start.5 = (bf16[27,8]{0,1:T(8,128)(2,1)S(1)}, bf16[27,8]{0,1:T(8,128)(2,1)}, u32[]{:S(2)}) copy-start(bf16[27,8]{0,1:T(8,128)(2,1)} %param.17) | copy-start | bytes 1300
  744.1 5.9 collective-permute-start.11
  746.3 6.0 collective-permute-start.12
  752.6 2.8 collective-permute-start.13
  753.9 5.0 collective-permute-start.14
  777.6 67.5 %copy-start.1 = (bf16[27,8,32]{2,1,0:T(8,128)(2,1)S(1)}, bf16[27,8,32]{2,1,0:T(8,128)(2,1)}, u32[]{:S(2)}) copy-start(bf16[27,8,32]{2,1,0:T(8,128)(2,1)} %param.15) | copy-start | bytes 41476
where the time goes:
time: 861 us; the launch traced here: 845 us
  blocking collectives  368 us (43%)
  local copies, waits for them, and re-layouts  231 us (27%)
  other arithmetic  96.8 us (11%)
  matrix products  73.1 us (8%)
  starting transfers between devices  40.3 us (5%)
  waiting for transfers between devices  20.5 us (2%)
  loops' own time  15.4 us (2%)
    psum x2, blocking collectives, normalize(): lax.psum(jnp.sum(values, axis=(0, 2, 3)), ('depth', 'col')) / voxels  172 us
    psum x2, blocking collectives, normalize(): lax.psum(jnp.sum(centered * centered, axis=(0, 2, 3)), ('depth', 'col'))  148 us
    conv_general_dilated x14, local copies, waits for them, and re-layouts, conv_block(): lax.conv_general_dilated(window[None], kernel, (1, 1, 1), ((0, 0), (1, 1)...  87.8 us
    gather x24, local copies, waits for them, and re-layouts, slide(): lax.dynamic_slice_in_dim(view_plane, col_count - shift_one, col_count, ax...  84.9 us
    conv_general_dilated x3, matrix products, conv_block(): lax.conv_general_dilated(window[None], kernel, (1, 1, 1), ((0, 0), (1, 1)...  64.7 us
    all_gather x3, blocking collectives, merged_2(): everything = jax.tree.map(lambda part: lax.all_gather(part, axis), x)  34.6 us
    reduce_sum x24, other arithmetic, one_depth(): spread = jnp.sum(weight_mask * deviation * deviation, axis=0) / tally  33.4 us
    reduce_sum x24, other arithmetic, one_depth(): average = jnp.sum(weight_mask * values, axis=0) / tally  33.1 us
  transfers between devices with their start and end apart: 15, of which 9 were waited for; matrix products, arithmetic and copies ran while one was open for 0% of the time, Pallas kernels for 0%

commit v1 on v0

v1 whole, which is shorter than its diff:
```python
import jax
import jax.numpy as jnp
from jax import lax
from jax.experimental import pallas as pl
from jax.experimental.pallas import tpu as pltpu
from jax.sharding import PartitionSpec as P

norm_eps = 1e-05

F32 = jnp.float32
BF16 = jnp.bfloat16
I32 = jnp.int32

VIEWS = 8
CHAN = 32
HID = 8
ROWS = 8
DEPTHS = 96
STRIP = 128
OWN = 32
GROUP = 42
HALO = 5
TILES = 32
LEFT = 136
CR = CHAN * ROWS
HR = HID * ROWS
DEVICES = 256
COUNT = DEPTHS * ROWS * OWN

VMEM = pl.BlockSpec(memory_space=pltpu.VMEM)
SMEM = pl.BlockSpec(memory_space=pltpu.SMEM)
PARAMS = pltpu.CompilerParams(vmem_limit_bytes=48 * 1024 * 1024)


def iota(shape, axis):
    return lax.broadcasted_iota(I32, shape, axis)


def mm(a, b):
    return jnp.dot(a, b, preferred_element_type=F32)


def spread_rows(count):
    return ((iota((8 * count, count), 0) >> 3) == iota((8 * count, count), 1)).astype(F32).astype(BF16)


def spread_cols(count):
    return (iota((count, 8 * count), 0) == (iota((count, 8 * count), 1) >> 3)).astype(F32).astype(BF16)


def banded(taps, left, right):
    total = None
    for b, w in enumerate(taps):
        t = w if left is None else mm(left, w).astype(BF16)
        u = mm(t, right)
        rows, cols = u.shape
        band = ((iota((rows, cols), 1) & 7) - (iota((rows, cols), 0) & 7)) == (b - 1)
        u = jnp.where(band, u, 0.0)
        total = u if total is None else total + u
    return total


def weights_kernel(fw, cw, mw, lw, wf, w1, w2, w3):
    ro32, ro8 = spread_rows(CHAN), spread_rows(HID)
    ci32, ci8 = spread_cols(CHAN), spread_cols(HID)
    for b in range(3):
        wf[b * CR : (b + 1) * CR, :] = banded([fw[3 * a + b] for a in range(3)], ro32, ci32).astype(BF16)
    for a in range(3):
        for e in range(3):
            taps = [9 * a + 3 * b + e for b in range(3)]
            w1[e * HR : (e + 1) * HR, a * CR : (a + 1) * CR] = banded(
                [cw[t] for t in taps], ro8, ci32
            ).astype(BF16)
    second, last = [], []
    for e in range(3):
        row2, row3 = [], []
        for a in range(3):
            taps = [9 * a + 3 * b + e for b in range(3)]
            row2.append(banded([mw[t] for t in taps], ro8, ci8))
            row3.append(
                banded([jnp.broadcast_to(lw[t], (ROWS, HID)).astype(BF16) for t in taps], None, ci8)
            )
        second.append(jnp.concatenate(row2, axis=1))
        last.append(jnp.concatenate(row3, axis=1))
    w2[...] = jnp.concatenate(second, axis=0).astype(BF16)
    w3[...] = jnp.concatenate(last, axis=0).astype(BF16)


def make_weights(feat_weight, cost_weight, mid_weight, final_weight):
    return pl.pallas_call(
        weights_kernel,
        out_shape=(
            jax.ShapeDtypeStruct((3 * CR, CR), BF16),
            jax.ShapeDtypeStruct((3 * HR, 3 * CR), BF16),
            jax.ShapeDtypeStruct((3 * HR, 3 * HR), BF16),
            jax.ShapeDtypeStruct((3 * ROWS, 3 * HR), BF16),
        ),
        in_specs=[VMEM] * 4,
        out_specs=(VMEM,) * 4,
        compiler_params=PARAMS,
        cost_estimate=pl.CostEstimate(flops=2_000_000_000, bytes_accessed=1_000_000, transcendentals=0),
        name="banded_weights",
    )(feat_weight, cost_weight, mid_weight, final_weight.astype(F32).reshape(27, 1, HID))


def features_kernel(pos, s2, s1, s0, sp, wf, *outs):
    depth = pos[0]
    for u in range(2):
        x = jnp.concatenate([s2[u], s1[u], s0[u], sp[u]], axis=1)
        y = mm(wf[...], x)
        f = (
            y[CR : 2 * CR]
            + pltpu.roll(y[:CR], 1, axis=1)
            + pltpu.roll(y[2 * CR :], 4 * STRIP - 1, axis=1)
        )
        f = f.astype(BF16).astype(F32)
        for k in range(4):
            target = depth ^ k
            start = OWN * target + 2 * STRIP - LEFT
            outs[k][u] = pltpu.roll(f, 4 * STRIP - start, axis=1)[:, : 2 * STRIP].astype(BF16)


def make_features(pos, strips, wf):
    return pl.pallas_call(
        features_kernel,
        out_shape=tuple(jax.ShapeDtypeStruct((2, CR, 2 * STRIP), BF16) for _ in range(4)),
        in_specs=[SMEM] + [VMEM] * 5,
        out_specs=(VMEM,) * 4,
        compiler_params=PARAMS,
        name="features",
    )(pos, *strips, wf)


def lane_places(width):
    lane = iota((1, width), 1) & (STRIP - 1)
    group = (lane >= GROUP).astype(I32) + (lane >= 2 * GROUP).astype(I32)
    return lane, group, lane - GROUP * group - HALO


def wrap_tiles(ref, size):
    lane = iota((1, STRIP), 1)
    last = ref[TILES * size : (TILES + 1) * size, :].astype(F32)
    first = ref[size : 2 * size, :].astype(F32)
    before = jnp.where(lane >= GROUP, pltpu.roll(last, GROUP, axis=1), 0.0)
    after = jnp.where(lane < 2 * GROUP, pltpu.roll(first, STRIP - GROUP, axis=1), 0.0)
    ref[0:size, :] = before.astype(BF16)
    ref[(TILES + 1) * size : (TILES + 2) * size, :] = after.astype(BF16)


def own_mask():
    lane, _, col = lane_places(STRIP)
    return ((col >= 0) & (col < OWN)).astype(F32)


def total_of(x):
    return jnp.sum(jnp.sum(x, axis=0, keepdims=True), axis=1, keepdims=True)


def conv_and_stats(w, ref, size, out, stats):
    mask = own_mask()

    def one(k, acc):
        rows = ref[pl.ds(pl.multiple_of(k * size, size), 3 * size), :]
        z = mm(w[...], rows)
        y = z[HR : 2 * HR] + pltpu.roll(z[:HR], 1, axis=1) + pltpu.roll(z[2 * HR :], STRIP - 1, axis=1)
        out[pl.ds(pl.multiple_of(k * HR, HR), HR), :] = y
        return acc + y

    acc = lax.fori_loop(0, TILES, one, jnp.zeros((HR, STRIP), F32), unroll=4) * mask
    means = [total_of(acc[ROWS * o : ROWS * (o + 1)]) * (1.0 / COUNT) for o in range(HID)]
    mean = jnp.concatenate([jnp.broadcast_to(m, (ROWS, STRIP)) for m in means], axis=0)

    def two(k, acc):
        dev = (out[pl.ds(pl.multiple_of(k * HR, HR), HR), :] - mean) * mask
        return acc + dev * dev

    acc = lax.fori_loop(0, TILES, two, jnp.zeros((HR, STRIP), F32), unroll=4)
    lane = iota((1, STRIP), 1)
    row = jnp.zeros((1, STRIP), F32)
    for o in range(HID):
        row = jnp.where(lane == o, means[o], row)
        row = jnp.where(lane == HID + o, total_of(acc[ROWS * o : ROWS * (o + 1)]), row)
    stats[...] = jnp.broadcast_to(row, (DEVICES, STRIP))


def normalized(pos, stats, values, act):
    lane = iota((1, STRIP), 1)
    rows = stats[...]
    center = jnp.sum(rows, axis=0, keepdims=True) * (1.0 / DEVICES)
    dev = rows - center
    between = jnp.sum(dev * dev, axis=0, keepdims=True)

    def pick(row, at):
        return jnp.sum(jnp.where(lane == at, row, 0.0), axis=1, keepdims=True)

    means, scales = [], []
    for o in range(HID):
        spread = pick(center, HID + o) * (1.0 / COUNT) + pick(between, o) * (1.0 / DEVICES)
        means.append(jnp.broadcast_to(pick(center, o), (ROWS, STRIP)))
        scales.append(jnp.broadcast_to(lax.rsqrt(spread + norm_eps), (ROWS, STRIP)))
    mean = jnp.concatenate(means, axis=0)
    scale = jnp.concatenate(scales, axis=0)
    _, _, col = lane_places(STRIP)
    col = col + (STRIP * pos[1] + OWN * pos[0])
    inside = (col >= 0) & (col < STRIP * pos[2])

    def one(k, carry):
        x = values[pl.ds(pl.multiple_of(k * HR, HR), HR), :]
        y = jnp.where(inside, jnp.maximum((x - mean) * scale, 0.0), 0.0)
        act[pl.ds(pl.multiple_of((k + 1) * HR, HR), HR), :] = y.astype(BF16)
        return carry

    lax.fori_loop(0, TILES, one, 0, unroll=4)
    wrap_tiles(act, HR)


def volume_kernel(pos, shifts, frame, f0, f1, f2, f3, w1, out, stats, moved, vol):
    depth = pos[0]
    base = STRIP * pos[1] + OWN * depth
    wide = 2 * STRIP
    _, group, col = lane_places(wide)
    half = iota((1, wide), 1) >= STRIP
    glob = base + col
    valid = (glob >= 0) & (glob < STRIP * pos[2])
    places = iota((wide, wide), 0)
    sources = (f0, f1, f2, f3)

    def pair(kk, carry):
        masks = []
        for n in range(VIEWS):
            v = 2 * (depth ^ (n // 2)) + n % 2
            at = [[shifts[v, TILES * j + 2 * kk + s] for j in range(3)] for s in range(2)]
            one, two = (
                jnp.where(group == 0, t[0], jnp.where(group == 1, t[1], t[2])) for t in at
            )
            shift = jnp.where(half, two, one)
            source = glob - shift
            inside = (source >= frame[v, 0]) & (source < frame[v, 1])
            index = jnp.where(inside, col - shift + LEFT, -1)
            hot = jnp.where(places == index, 1.0, 0.0).astype(BF16)
            moved[n] = mm(sources[n // 2][n % 2], hot)
            masks.append(inside.astype(F32))
        tally = masks[0]
        for m in masks[1:]:
            tally = tally + m
        inverse = 1.0 / tally
        for r in range(0, CR, 16):
            parts = [moved[n, r : r + 16, :] for n in range(VIEWS)]
            total = parts[0]
            for p in parts[1:]:
                total = total + p
            average = total * inverse
            spread = None
            for p, m in zip(parts, masks):
                dev = (p - average) * m
                spread = dev * dev if spread is None else spread + dev * dev
            value = jnp.where(valid, spread * inverse, 0.0).astype(BF16)
            for s in range(2):
                row = pl.multiple_of((2 * kk + s + 1) * CR + r, 16)
                vol[pl.ds(row, 16), :] = value[:, s * STRIP : (s + 1) * STRIP]
        return carry

    lax.fori_loop(0, TILES // 2, pair, 0)
    wrap_tiles(vol, CR)
    conv_and_stats(w1, vol, CR, out, stats)


def cost_and_conv(pos, shifts, frame, feats, w1):
    return pl.pallas_call(
        volume_kernel,
        out_shape=(
            jax.ShapeDtypeStruct((TILES * HR, STRIP), F32),
            jax.ShapeDtypeStruct((DEVICES, STRIP), F32),
        ),
        in_specs=[SMEM] * 3 + [VMEM] * 5,
        out_specs=(VMEM,) * 2,
        scratch_shapes=[
            pltpu.VMEM((VIEWS, CR, 2 * STRIP), F32),
            pltpu.VMEM(((TILES + 2) * CR, STRIP), BF16),
        ],
        compiler_params=PARAMS,
        name="cost_volume",
    )(pos, shifts, frame, *feats, w1)


def middle_kernel(pos, stats_in, values, w2, out, stats, act):
    normalized(pos, stats_in, values, act)
    conv_and_stats(w2, act, HR, out, stats)


def second_conv(pos, stats, values, w2):
    return pl.pallas_call(
        middle_kernel,
        out_shape=(
            jax.ShapeDtypeStruct((TILES * HR, STRIP), F32),
            jax.ShapeDtypeStruct((DEVICES, STRIP), F32),
        ),
        in_specs=[SMEM] + [VMEM] * 3,
        out_specs=(VMEM,) * 2,
        scratch_shapes=[pltpu.VMEM(((TILES + 2) * HR, STRIP), BF16)],
        compiler_params=PARAMS,
        name="second_conv",
    )(pos, stats, values, w2)


def last_kernel(pos, stats_in, values, w3, out, act, score):
    normalized(pos, stats_in, values, act)

    def one(k, peak):
        z = mm(w3[...], act[pl.ds(pl.multiple_of(k * HR, HR), 3 * HR), :])
        y = (
            z[ROWS : 2 * ROWS]
            + pltpu.roll(z[:ROWS], 1, axis=1)
            + pltpu.roll(z[2 * ROWS :], STRIP - 1, axis=1)
        )
        score[k] = y
        return jnp.maximum(peak, y)

    peak = lax.fori_loop(0, TILES, one, jnp.full((ROWS, STRIP), -jnp.inf, F32), unroll=4)
    _, group, _ = lane_places(STRIP)

    def two(k, sums):
        e = jnp.exp(score[k] - peak)
        value = (TILES * group + k).astype(F32) / (DEPTHS - 1)
        return sums[0] + e, sums[1] + e * value

    zero = jnp.zeros((ROWS, STRIP), F32)
    total, weighted = lax.fori_loop(0, TILES, two, (zero, zero), unroll=4)

    def turned(x):
        return [x] + [pltpu.roll(x, STRIP - j * GROUP, axis=1) for j in (1, 2)]

    peaks, totals, weights = turned(peak), turned(total), turned(weighted)
    top = jnp.maximum(jnp.maximum(peaks[0], peaks[1]), peaks[2])
    scales = [jnp.exp(p - top) for p in peaks]
    whole = sum(t * s for t, s in zip(totals, scales))
    mean = sum(t * s for t, s in zip(weights, scales)) / whole
    first = OWN * pos[0]
    lane = iota((1, STRIP), 1)
    moved = pltpu.roll(mean, (first + STRIP - HALO) & (STRIP - 1), axis=1)
    out[...] = jnp.where((lane >= first) & (lane < first + OWN), moved, 0.0)


def final_estimate(pos, stats, values, w3):
    return pl.pallas_call(
        last_kernel,
        out_shape=jax.ShapeDtypeStruct((ROWS, STRIP), F32),
        in_specs=[SMEM] + [VMEM] * 3,
        out_specs=VMEM,
        scratch_shapes=[
            pltpu.VMEM(((TILES + 2) * HR, STRIP), BF16),
            pltpu.VMEM((TILES, ROWS, STRIP), F32),
        ],
        compiler_params=PARAMS,
        name="final_estimate",
    )(pos, stats, values, w3)


def beside(x, by):
    peers = lax.axis_size("col")
    return lax.ppermute(x, "col", [(i, i + by) for i in range(peers) if 0 <= i + by < peers])


def everyones(stats):
    return lax.all_to_all(stats, ("depth", "col"), 0, 0, tiled=True)


def local(raw_views, feat_weight, shifts, frame_range, cost_weight, mid_weight, final_weight):
    pos = jnp.stack([lax.axis_index("depth"), lax.axis_index("col"), jnp.int32(lax.axis_size("col"))])
    pos = pos.astype(I32)
    own = raw_views.reshape(2, CR, STRIP)
    with jax.named_scope("strips"):
        strips = (beside(own, 2), beside(own, 1), own, beside(own, -1))
    wf, w1, w2, w3 = make_weights(feat_weight, cost_weight, mid_weight, final_weight)
    windows = make_features(pos, strips, wf)
    with jax.named_scope("views"):
        feats = [windows[0]] + [
            lax.ppermute(windows[k], "depth", [(i, i ^ k) for i in range(4)]) for k in (1, 2, 3)
        ]
    first, stats = cost_and_conv(pos, shifts, frame_range, feats, w1)
    second, stats = second_conv(pos, everyones(stats), first, w2)
    part = final_estimate(pos, everyones(stats), second, w3)
    return lax.psum(part, "depth")


def solution(mesh):
    in_specs = (P("depth", None, None, "col"), P(), P(), P(), P(), P(), P())
    out_specs = P(None, "col")
    return jax.shard_map(local, mesh=mesh, in_specs=in_specs, out_specs=out_specs, check_vma=False)
```

time: 861 us -> 114 us (0.13); the launches traced: 845 us -> 113 us
  blocking collectives: 368 us -> 54.8 us
  local copies, waits for them, and re-layouts: 231 us -> 1.14 us
  other arithmetic: 96.8 us -> 0.76 us
  matrix products: 73.1 us -> 0 us
  Pallas kernels: 0 us -> 31.4 us
  starting transfers between devices: 40.3 us -> 11.5 us
  loops' own time: 15.4 us -> 0 us
    psum x4 -> x1, blocking collectives: 320 us -> 9.74 us  [local(): return lax.psum(part, 'depth')]
    conv_general_dilated x14 -> x0, local copies, waits for them, and re-layouts: 87.8 us -> none  [conv_block(): lax.conv_general_dilated(window[None], kernel, (1, 1, 1), ((0, 0), (1, 1)...]
    gather x24 -> x0, local copies, waits for them, and re-layouts: 84.9 us -> none  [slide(): lax.dynamic_slice_in_dim(view_plane, col_count - shift_one, col_count, ax...]
    reduce_sum x75 -> x0, other arithmetic: 69.4 us -> none  [the longest x24 33.4 us: one_depth(): spread = jnp.sum(weight_mask * deviation * deviation, axis=0) / tally]
    conv_general_dilated x3 -> x0, matrix products: 64.7 us -> none  [conv_block(): lax.conv_general_dilated(window[None], kernel, (1, 1, 1), ((0, 0), (1, 1)...]
    all_gather x4 -> x0, blocking collectives: 47.4 us -> none  [the longest x3 34.6 us: merged_2(): everything = jax.tree.map(lambda part: lax.all_gather(part, axis), x)]
    all_to_all x0 -> x2, blocking collectives: none -> 45 us  [everyones(): return lax.all_to_all(stats, ('depth', 'col'), 0, 0, tiled=True)]
    pallas_call x0 -> x5, Pallas kernels: none -> 31.4 us  [the longest x1 18 us: cost_and_conv(): pl.pallas_call(volume_kernel, out_shape=(jax.ShapeDtypeStruct((TILES * HR...]
  transfers between devices with their start and end apart: 15 -> 6, of which waited for: 9 -> 3; matrix products, arithmetic and copies ran while one was open for 0% -> 1% of each run, Pallas kernels for 0% -> 4%
where the time goes in v1:
time: 114 us; the launch traced here: 113 us
  blocking collectives  54.8 us (48%)
  Pallas kernels  31.4 us (28%)
  waiting for transfers between devices  13.6 us (12%)
  starting transfers between devices  11.5 us (10%)
    all_to_all x2, blocking collectives, everyones(): return lax.all_to_all(stats, ('depth', 'col'), 0, 0, tiled=True)  45 us
    pallas_call x1, Pallas kernels, cost_and_conv(): pl.pallas_call(volume_kernel, out_shape=(jax.ShapeDtypeStruct((TILES * HR...  18 us
    ppermute x3, waiting for transfers between devices, local(): lax.ppermute(windows[k], 'depth', [(i, i ^ k) for i in range(4)])  13.6 us
    psum x1, blocking collectives, local(): return lax.psum(part, 'depth')  9.74 us
    ppermute x3, starting transfers between devices, beside(): lax.ppermute(x, 'col', [(i, i + by) for i in range(peers) if 0 <= i + by...  7.94 us
    pallas_call x1, Pallas kernels, make_weights(): pl.pallas_call(weights_kernel, out_shape=(jax.ShapeDtypeStruct((3 * CR, C...  4.05 us
    pallas_call x1, Pallas kernels, second_conv(): pl.pallas_call(middle_kernel, out_shape=(jax.ShapeDtypeStruct((TILES * HR...  3.99 us
    ppermute x3, starting transfers between devices, local(): lax.ppermute(windows[k], 'depth', [(i, i ^ k) for i in range(4)])  3.58 us
  transfers between devices with their start and end apart: 6, of which 3 were waited for; matrix products, arithmetic and copies ran while one was open for 1% of the time, Pallas kernels for 4%

profile of v1, /device:TPU:2, one launch (start us, length us, event | category | flops | bytes accessed | tf_op | source)
XLA Modules:
  0.0 113.3 jit_solution(13534133469262052776)
XLA Ops:
  0.0 0.0 copy-start.4
  0.0 0.0 copy-start.2
  0.0 1.4 %collective-permute-start.2 = (bf16[2,256,128]{2,1,0:T(8,128)(2,1)}, bf16[2,256,128]{2,1,0:T(8,128)(2,1)S(1)}, u32[]{:S(2)}, u32[]{:S(2)}) collective-permute-start(bf16[2,256,128]{2,1,0:T(8,128)(2,1)} %bitcast.16), channel_id=1, source_target_pairs={{1,0},{2,1},{3,2},{4,3},{5,4},{6,5},{7,6},{8,7},{9,8},{10,9},{11,1... | collective-permute-start | bytes 393224 | tf_op jit(solution)/shard_map/strips/ppermute | solution.py:361
  1.4 3.0 %collective-permute-start.1 = (bf16[2,256,128]{2,1,0:T(8,128)(2,1)}, bf16[2,256,128]{2,1,0:T(8,128)(2,1)S(1)}, u32[]{:S(2)}, u32[]{:S(2)}) collective-permute-start(bf16[2,256,128]{2,1,0:T(8,128)(2,1)} %bitcast.17), channel_id=1, source_target_pairs={{0,1},{1,2},{2,3},{3,4},{4,5},{5,6},{6,7},{7,8},{8,9},{9,10},{10,1... | collective-permute-start | bytes 393224 | tf_op jit(solution)/shard_map/strips/ppermute | solution.py:361
  4.5 3.5 %collective-permute-start = (bf16[2,256,128]{2,1,0:T(8,128)(2,1)}, bf16[2,256,128]{2,1,0:T(8,128)(2,1)S(1)}, u32[]{:S(2)}, u32[]{:S(2)}) collective-permute-start(bf16[2,256,128]{2,1,0:T(8,128)(2,1)} %bitcast.18), channel_id=1, source_target_pairs={{0,2},{1,3},{2,4},{3,5},{4,6},{5,7},{6,8},{7,9},{8,10},{9,11},{10,... | collective-permute-start | bytes 393224 | tf_op jit(solution)/shard_map/strips/ppermute | solution.py:361
  8.0 0.7 bitcast_convert_fusion
  8.7 0.1 copy.15.lw
  8.7 0.0 copy-done.4
  8.7 0.1 copy.14.mw
  8.9 0.0 copy-done.2
  8.9 0.0 copy-start.3
  8.9 0.8 copy-done.3
  9.7 0.0 copy-start
  9.7 4.0 %banded_weights.1 = (bf16[768,256]{1,0:T(8,128)(2,1)S(1)}, bf16[192,768]{1,0:T(8,128)(2,1)S(1)}, bf16[192,192]{1,0:T(8,128)(2,1)S(1)}, bf16[24,192]{1,0:T(8,128)(2,1)S(1)}) custom-call(bf16[9,32,32]{2,1,0:T(8,128)(2,1)S(1)} %copy-done.2, bf16[27,8,32]{2,1,0:T(8,128)(2,1)S(1)} %copy-done.3, bf16[27,8,8]{2,1,0:T(8,128)(2,1)S(1)} %copy.14.mw, ...), custom_call_target="tpu_custom_call" | custom-call | flops 2000000000 | bytes 1000000 | tf_op jit(solution)/shard_map/banded_weights/pallas_call | solution.py:90
  13.8 0.1 pad_add_fusion.pos
  13.9 0.0 collective-permute-done.2.sp
  13.9 0.0 collective-permute-done.1.s1
  13.9 0.0 collective-permute-done.s2
  13.9 0.0 copy-done
  13.9 2.0 %features.1 = (bf16[2,256,256]{2,1,0:T(8,128)(2,1)S(1)}, bf16[2,256,256]{2,1,0:T(8,128)(2,1)S(1)}, bf16[2,256,256]{2,1,0:T(8,128)(2,1)S(1)}, bf16[2,256,256]{2,1,0:T(8,128)(2,1)S(1)}) custom-call(s32[3]{0:T(128)S(1)} %pad_add_fusion.pos, bf16[2,256,128]{2,1,0:T(8,128)(2,1)S(1)} %collective-permute-done.s2, ...), custom_call_target="tpu_custom_call" | custom-call | tf_op jit(solution)/shard_map/features/pallas_call | solution.py:124
  15.9 0.6 collective-permute-start.3
  16.6 0.0 copy-start.5
  16.6 2.4 %collective-permute-start.4 = (bf16[2,256,256]{2,1,0:T(8,128)(2,1)S(1)}, bf16[2,256,256]{2,1,0:T(8,128)(2,1)S(1)}, u32[]{:S(2)}, u32[]{:S(2)}) collective-permute-start(bf16[2,256,256]{2,1,0:T(8,128)(2,1)S(1)} %get-tuple-element.20), channel_id=1, source_target_pairs={{0,128},{64,192},{128,0},{192,64},{1,129},{65,193},{129,1},{193,65... | collective-permute-start | bytes 786440 | tf_op jit(solution)/shard_map/views/ppermute | solution.py:378
  19.0 0.0 copy-start.1
  19.0 0.5 collective-permute-start.5
  19.5 0.0 copy-done.5
  19.5 0.1 copy.16.frame
  19.6 5.6 %collective-permute-done.3.f1 = bf16[2,256,256]{2,1,0:T(8,128)(2,1)S(1)} collective-permute-done((bf16[2,256,256]{2,1,0:T(8,128)(2,1)S(1)}, bf16[2,256,256]{2,1,0:T(8,128)(2,1)S(1)}, u32[]{:S(2)}, u32[]{:S(2)}) %collective-permute-start.3) | collective-permute-done | bytes 262176 | tf_op jit(solution)/shard_map/views/ppermute | solution.py:378
  25.2 6.6 %collective-permute-done.4.f2 = bf16[2,256,256]{2,1,0:T(8,128)(2,1)S(1)} collective-permute-done((bf16[2,256,256]{2,1,0:T(8,128)(2,1)S(1)}, bf16[2,256,256]{2,1,0:T(8,128)(2,1)S(1)}, u32[]{:S(2)}, u32[]{:S(2)}) %collective-permute-start.4) | collective-permute-done | bytes 262176 | tf_op jit(solution)/shard_map/views/ppermute | solution.py:378
  31.8 1.4 %collective-permute-done.5.f3 = bf16[2,256,256]{2,1,0:T(8,128)(2,1)S(1)} collective-permute-done((bf16[2,256,256]{2,1,0:T(8,128)(2,1)S(1)}, bf16[2,256,256]{2,1,0:T(8,128)(2,1)S(1)}, u32[]{:S(2)}, u32[]{:S(2)}) %collective-permute-start.5) | collective-permute-done | bytes 262176 | tf_op jit(solution)/shard_map/views/ppermute | solution.py:378
  33.2 0.0 copy-done.1
  33.2 18.0 %cost_volume.1 = (f32[2048,128]{1,0:T(8,128)S(1)}, f32[256,128]{1,0:T(8,128)S(1)}) custom-call(s32[3]{0:T(128)S(1)} %pad_add_fusion.pos, s32[8,96]{1,0:T(8,128)S(1)} %copy-done.1, s32[8,2]{1,0:T(8,128)S(1)} %copy.16.frame, bf16[2,256,256]{2,1,0:T(8,128)(2,1)S(1)} %get-tuple-element.18.f0, bf16[2,256,256]{2,1,0:T(8,128)(2,1)S(1)} %collective-permute-done.3.f1, ...), custom_call_target="tpu_custom_call" | custom-call | tf_op jit(solution)/shard_map/cost_volume/pallas_call | solution.py:269
  51.2 26.9 %all_to_all.22 = f32[256,1,128]{2,1,0:T(1,128)S(1)} all-to-all(f32[256,1,128]{2,1,0:T(1,128)S(1)} %bitcast.20), channel_id=1, replica_groups=mesh['depth'=4,'col'=64] {'depth','col'}, dimensions={0} | all-to-all | bytes 262144 | tf_op jit(solution)/shard_map/all_to_all | solution.py:365
  78.1 4.0 %second_conv.1 = (f32[2048,128]{1,0:T(8,128)S(1)}, f32[256,128]{1,0:T(8,128)S(1)}) custom-call(s32[3]{0:T(128)S(1)} %pad_add_fusion.pos, f32[256,128]{1,0:T(8,128)S(1)} %bitcast.14, f32[2048,128]{1,0:T(8,128)S(1)} %get-tuple-element.24.values, bf16[192,192]{1,0:T(8,128)(2,1)S(1)} %get-tuple-element.25.w2), custom_call_target="tpu_custom_call" | custom-call | tf_op jit(solution)/shard_map/second_conv/pallas_call | solution.py:292
  82.1 18.1 %all_to_all.23 = f32[256,1,128]{2,1,0:T(1,128)S(1)} all-to-all(f32[256,1,128]{2,1,0:T(1,128)S(1)} %bitcast.21), channel_id=1, replica_groups=mesh['depth'=4,'col'=64] {'depth','col'}, dimensions={0} | all-to-all | bytes 262144 | tf_op jit(solution)/shard_map/all_to_all | solution.py:365
  100.3 3.3 %final_estimate.1 = f32[8,128]{1,0:T(8,128)S(1)} custom-call(s32[3]{0:T(128)S(1)} %pad_add_fusion.pos, f32[256,128]{1,0:T(8,128)S(1)} %bitcast.15, f32[2048,128]{1,0:T(8,128)S(1)} %get-tuple-element.27.values, bf16[24,192]{1,0:T(8,128)(2,1)S(1)} %get-tuple-element.28.w3), custom_call_target="tpu_custom_call" | custom-call | tf_op jit(solution)/shard_map/final_estimate/pallas_call | solution.py:345
  103.5 9.7 %psum.7 = f32[8,128]{1,0:T(8,128)} all-reduce(f32[8,128]{1,0:T(8,128)S(1)} %final_estimate.1), channel_id=1, replica_groups=mesh['depth'=4,'col'=64] {'depth'}, use_global_device_ids=true, to_apply=%region_0.0 | all-reduce | flops 1024 | bytes 8192 | tf_op jit(solution)/shard_map/psum | solution.py:383
Async XLA Ops:
  0.0 8.7 %copy-start.4 = (bf16[27,8,8]{0,2,1:T(8,128)(2,1)S(1)}, bf16[27,8,8]{0,2,1:T(8,128)(2,1)}, u32[]{:S(2)}) copy-start(bf16[27,8,8]{0,2,1:T(8,128)(2,1)} %param.12) | copy-start | bytes 10372
  0.0 8.9 %copy-start.2 = (bf16[9,32,32]{2,1,0:T(8,128)(2,1)S(1)}, bf16[9,32,32]{2,1,0:T(8,128)(2,1)}, u32[]{:S(2)}) copy-start(bf16[9,32,32]{2,1,0:T(8,128)(2,1)} %fw.1) | copy-start | bytes 55300
  0.0 13.8 %collective-permute-start.2 = (bf16[2,256,128]{2,1,0:T(8,128)(2,1)}, bf16[2,256,128]{2,1,0:T(8,128)(2,1)S(1)}, u32[]{:S(2)}, u32[]{:S(2)}) collective-permute-start(bf16[2,256,128]{2,1,0:T(8,128)(2,1)} %bitcast.16), channel_id=1, source_target_pairs={{1,0},{2,1},{3,2},{4,3},{5,4},{6,5},{7,6},{8,7},{9,8},{10,9},{11,1... | collective-permute-start | bytes 393224 | tf_op jit(solution)/shard_map/strips/ppermute | solution.py:361
  1.4 12.4 %collective-permute-start.1 = (bf16[2,256,128]{2,1,0:T(8,128)(2,1)}, bf16[2,256,128]{2,1,0:T(8,128)(2,1)S(1)}, u32[]{:S(2)}, u32[]{:S(2)}) collective-permute-start(bf16[2,256,128]{2,1,0:T(8,128)(2,1)} %bitcast.17), channel_id=1, source_target_pairs={{0,1},{1,2},{2,3},{3,4},{4,5},{5,6},{6,7},{7,8},{8,9},{9,10},{10,1... | collective-permute-start | bytes 393224 | tf_op jit(solution)/shard_map/strips/ppermute | solution.py:361
  4.5 9.4 %collective-permute-start = (bf16[2,256,128]{2,1,0:T(8,128)(2,1)}, bf16[2,256,128]{2,1,0:T(8,128)(2,1)S(1)}, u32[]{:S(2)}, u32[]{:S(2)}) collective-permute-start(bf16[2,256,128]{2,1,0:T(8,128)(2,1)} %bitcast.18), channel_id=1, source_target_pairs={{0,2},{1,3},{2,4},{3,5},{4,6},{5,7},{6,8},{7,9},{8,10},{9,11},{10,... | collective-permute-start | bytes 393224 | tf_op jit(solution)/shard_map/strips/ppermute | solution.py:361
  8.9 0.8 copy-start.3
  9.7 4.2 %copy-start = (bf16[2,32,8,128]{3,2,1,0:T(8,128)(2,1)S(1)}, bf16[2,32,8,128]{3,2,1,0:T(8,128)(2,1)}, u32[]{:S(2)}) copy-start(bf16[2,32,8,128]{3,2,1,0:T(8,128)(2,1)} %param.7) | copy-start | bytes 393220
  15.9 9.3 %collective-permute-start.3 = (bf16[2,256,256]{2,1,0:T(8,128)(2,1)S(1)}, bf16[2,256,256]{2,1,0:T(8,128)(2,1)S(1)}, u32[]{:S(2)}, u32[]{:S(2)}) collective-permute-start(bf16[2,256,256]{2,1,0:T(8,128)(2,1)S(1)} %get-tuple-element.19), channel_id=1, source_target_pairs={{0,64},{64,0},{128,192},{192,128},{1,65},{65,1},{129,193},{193,129... | collective-permute-start | bytes 786440 | tf_op jit(solution)/shard_map/views/ppermute | solution.py:378
  16.6 3.0 %copy-start.5 = (s32[8,2]{0,1:T(2,128)S(1)}, s32[8,2]{0,1:T(2,128)}, u32[]{:S(2)}) copy-start(s32[8,2]{0,1:T(2,128)} %param.10) | copy-start | bytes 196
  16.6 15.3 %collective-permute-start.4 = (bf16[2,256,256]{2,1,0:T(8,128)(2,1)S(1)}, bf16[2,256,256]{2,1,0:T(8,128)(2,1)S(1)}, u32[]{:S(2)}, u32[]{:S(2)}) collective-permute-start(bf16[2,256,256]{2,1,0:T(8,128)(2,1)S(1)} %get-tuple-element.20), channel_id=1, source_target_pairs={{0,128},{64,192},{128,0},{192,64},{1,129},{65,193},{129,1},{193,65... | collective-permute-start | bytes 786440 | tf_op jit(solution)/shard_map/views/ppermute | solution.py:378
  19.0 14.2 %copy-start.1 = (s32[8,96]{1,0:T(8,128)S(1)}, s32[8,96]{1,0:T(8,128)}, u32[]{:S(2)}) copy-start(s32[8,96]{1,0:T(8,128)} %shifts.1) | copy-start | bytes 9220
  19.0 14.2 %collective-permute-start.5 = (bf16[2,256,256]{2,1,0:T(8,128)(2,1)S(1)}, bf16[2,256,256]{2,1,0:T(8,128)(2,1)S(1)}, u32[]{:S(2)}, u32[]{:S(2)}) collective-permute-start(bf16[2,256,256]{2,1,0:T(8,128)(2,1)S(1)} %get-tuple-element.21), channel_id=1, source_target_pairs={{0,192},{64,128},{128,64},{192,0},{1,193},{65,129},{129,65},{193,1... | collective-permute-start | bytes 786440 | tf_op jit(solution)/shard_map/views/ppermute | solution.py:378

commit v2 on v1

--- a/solution.py
+++ b/solution.py
@@ -22,6 +22,7 @@
 HALO = 5
 TILES = 32
 LEFT = 136
+BASE = 176
 CR = CHAN * ROWS
 HR = HID * ROWS
 DEVICES = 256
@@ -214,21 +215,30 @@
     wrap_tiles(act, HR)
 
 
-def volume_kernel(pos, shifts, frame, f0, f1, f2, f3, w1, out, stats, moved, vol):
+def volume_kernel(pos, shifts, frame, f0, f1, f2, f3, w1, out, stats, feats, even, odd, vol):
     depth = pos[0]
     base = STRIP * pos[1] + OWN * depth
     wide = 2 * STRIP
+    lane = iota((1, wide), 1)
+    sources = (f0, f1, f2, f3)
+    for k in range(4):
+        for u in range(2):
+            feats[2 * (depth ^ k) + u] = sources[k][u]
+    zero_view = pltpu.roll(feats[0].astype(F32), BASE - (LEFT - HALO), axis=1)
+    own_lanes = (lane >= BASE) & (lane < BASE + GROUP)
+    for v in range(1, VIEWS):
+        feats[v] = jnp.where(own_lanes, zero_view, feats[v].astype(F32)).astype(BF16)
+
     _, group, col = lane_places(wide)
-    half = iota((1, wide), 1) >= STRIP
+    half = lane >= STRIP
     glob = base + col
     valid = (glob >= 0) & (glob < STRIP * pos[2])
-    places = iota((wide, wide), 0)
-    sources = (f0, f1, f2, f3)
-
-    def pair(kk, carry):
-        masks = []
-        for n in range(VIEWS):
-            v = 2 * (depth ^ (n // 2)) + n % 2
+    places = iota((BASE, wide), 0)
+    below = jnp.where(iota((wide - BASE, wide), 0) == col + HALO, -1.0, 0.0)
+
+    def move(kk, moved):
+        tally = jnp.ones((1, wide), F32)
+        for v in range(1, VIEWS):
             at = [[shifts[v, TILES * j + 2 * kk + s] for j in range(3)] for s in range(2)]
             one, two = (
                 jnp.where(group == 0, t[0], jnp.where(group == 1, t[1], t[2])) for t in at
@@ -238,29 +248,33 @@
             inside = (source >= frame[v, 0]) & (source < frame[v, 1])
             index = jnp.where(inside, col - shift + LEFT, -1)
             hot = jnp.where(places == index, 1.0, 0.0).astype(BF16)
-            moved[n] = mm(sources[n // 2][n % 2], hot)
-            masks.append(inside.astype(F32))
-        tally = masks[0]
-        for m in masks[1:]:
-            tally = tally + m
-        inverse = 1.0 / tally
+            mask = inside.astype(F32)
+            hot = jnp.concatenate([hot, (below * mask).astype(BF16)], axis=0)
+            moved[v - 1] = mm(feats[v], hot)
+            tally = tally + mask
+        return 1.0 / tally
+
+    def spread(kk, moved, inverse):
         for r in range(0, CR, 16):
-            parts = [moved[n, r : r + 16, :] for n in range(VIEWS)]
-            total = parts[0]
-            for p in parts[1:]:
-                total = total + p
+            total = squares = None
+            for v in range(VIEWS - 1):
+                p = moved[v, r : r + 16, :]
+                total = p if total is None else total + p
+                squares = p * p if squares is None else squares + p * p
             average = total * inverse
-            spread = None
-            for p, m in zip(parts, masks):
-                dev = (p - average) * m
-                spread = dev * dev if spread is None else spread + dev * dev
-            value = jnp.where(valid, spread * inverse, 0.0).astype(BF16)
+            value = jnp.where(valid, squares * inverse - average * average, 0.0)
+            value = jnp.maximum(value, 0.0).astype(BF16)
             for s in range(2):
                 row = pl.multiple_of((2 * kk + s + 1) * CR + r, 16)
                 vol[pl.ds(row, 16), :] = value[:, s * STRIP : (s + 1) * STRIP]
-        return carry
-
-    lax.fori_loop(0, TILES // 2, pair, 0)
+
+    def step(t, inverse):
+        spread(2 * t, even, inverse)
+        later = move(2 * t + 1, odd)
+        spread(2 * t + 1, odd, later)
+        return move(jnp.minimum(2 * t + 2, TILES // 2 - 1), even)
+
+    lax.fori_loop(0, TILES // 4, step, move(0, even))
     wrap_tiles(vol, CR)
     conv_and_stats(w1, vol, CR, out, stats)
 
@@ -275,7 +289,9 @@
         in_specs=[SMEM] * 3 + [VMEM] * 5,
         out_specs=(VMEM,) * 2,
         scratch_shapes=[
-            pltpu.VMEM((VIEWS, CR, 2 * STRIP), F32),
+            pltpu.VMEM((VIEWS, CR, 2 * STRIP), BF16),
+            pltpu.VMEM((VIEWS - 1, CR, 2 * STRIP), F32),
+            pltpu.VMEM((VIEWS - 1, CR, 2 * STRIP), F32),
             pltpu.VMEM(((TILES + 2) * CR, STRIP), BF16),
         ],
         compiler_params=PARAMS,
@@ -380,7 +396,9 @@
     first, stats = cost_and_conv(pos, shifts, frame_range, feats, w1)
     second, stats = second_conv(pos, everyones(stats), first, w2)
     part = final_estimate(pos, everyones(stats), second, w3)
-    return lax.psum(part, "depth")
+    with jax.named_scope("columns"):
+        others = [lax.ppermute(part, "depth", [(i, i ^ k) for i in range(4)]) for k in (1, 2, 3)]
+        return part + others[0] + others[1] + others[2]
 
 
 def solution(mesh):

time: 114 us -> 108 us (0.947)
  blocking collectives: 54.8 us -> 45 us
  starting transfers between devices: 11.5 us -> 15.6 us
  Pallas kernels: 31.4 us -> 27.9 us
  waiting for transfers between devices: 13.6 us -> 16.6 us
    psum x1 -> x0, blocking collectives: 9.74 us -> none  [local(): return lax.psum(part, 'depth')]
    ppermute x0 -> x3, starting transfers between devices: none -> 4.13 us  [local(): lax.ppermute(part, 'depth', [(i, i ^ k) for i in range(4)])]
    pallas_call x1, Pallas kernels: 18 us -> 14.5 us  [cost_and_conv(): pl.pallas_call(volume_kernel, out_shape=(jax.ShapeDtypeStruct((TILES * HR...]
    ppermute x0 -> x3, waiting for transfers between devices: none -> 3.03 us  [local(): lax.ppermute(part, 'depth', [(i, i ^ k) for i in range(4)])]
  transfers between devices with their start and end apart: 6 -> 9, of which waited for: 3 -> 5; matrix products, arithmetic and copies ran while one was open for 1% -> 1% of each run, Pallas kernels for 4% -> 4%
where the time goes in v2:
time: 108 us
  blocking collectives  45 us (42%)
  Pallas kernels  27.9 us (26%)
  waiting for transfers between devices  16.6 us (15%)
  starting transfers between devices  15.6 us (14%)
  other arithmetic  1.36 us (1%)
  local copies, waits for them, and re-layouts  1.14 us (1%)
    all_to_all x2, blocking collectives, everyones(): return lax.all_to_all(stats, ('depth', 'col'), 0, 0, tiled=True)  45 us
    pallas_call x1, Pallas kernels, cost_and_conv(): pl.pallas_call(volume_kernel, out_shape=(jax.ShapeDtypeStruct((TILES * HR...  14.5 us
    ppermute x3, waiting for transfers between devices, local(): lax.ppermute(windows[k], 'depth', [(i, i ^ k) for i in range(4)])  13.6 us
    ppermute x3, starting transfers between devices, beside(): lax.ppermute(x, 'col', [(i, i + by) for i in range(peers) if 0 <= i + by...  7.94 us
    ppermute x3, starting transfers between devices, local(): lax.ppermute(part, 'depth', [(i, i ^ k) for i in range(4)])  4.13 us
    pallas_call x1, Pallas kernels, make_weights(): pl.pallas_call(weights_kernel, out_shape=(jax.ShapeDtypeStruct((3 * CR, C...  4.05 us
    pallas_call x1, Pallas kernels, second_conv(): pl.pallas_call(middle_kernel, out_shape=(jax.ShapeDtypeStruct((TILES * HR...  3.99 us
    ppermute x3, starting transfers between devices, local(): lax.ppermute(windows[k], 'depth', [(i, i ^ k) for i in range(4)])  3.58 us
  transfers between devices with their start and end apart: 9, of which 5 were waited for; matrix products, arithmetic and copies ran while one was open for 1% of the time, Pallas kernels for 4%

profile of v2, /device:TPU:2, one launch (start us, length us, event | category | flops | bytes accessed | tf_op | source)
XLA Modules:
  0.0 107.7 jit_solution(6598658673808528508)
XLA Ops:
  0.0 0.0 copy-start.4
  0.0 0.0 copy-start.2
  0.0 1.4 %collective-permute-start.2 = (bf16[2,256,128]{2,1,0:T(8,128)(2,1)}, bf16[2,256,128]{2,1,0:T(8,128)(2,1)S(1)}, u32[]{:S(2)}, u32[]{:S(2)}) collective-permute-start(bf16[2,256,128]{2,1,0:T(8,128)(2,1)} %bitcast.16), channel_id=1, source_target_pairs={{1,0},{2,1},{3,2},{4,3},{5,4},{6,5},{7,6},{8,7},{9,8},{10,9},{11,1... | collective-permute-start | bytes 393224 | tf_op jit(solution)/shard_map/strips/ppermute | solution.py:377
  1.4 3.0 %collective-permute-start.1 = (bf16[2,256,128]{2,1,0:T(8,128)(2,1)}, bf16[2,256,128]{2,1,0:T(8,128)(2,1)S(1)}, u32[]{:S(2)}, u32[]{:S(2)}) collective-permute-start(bf16[2,256,128]{2,1,0:T(8,128)(2,1)} %bitcast.17), channel_id=1, source_target_pairs={{0,1},{1,2},{2,3},{3,4},{4,5},{5,6},{6,7},{7,8},{8,9},{9,10},{10,1... | collective-permute-start | bytes 393224 | tf_op jit(solution)/shard_map/strips/ppermute | solution.py:377
  4.5 3.5 %collective-permute-start = (bf16[2,256,128]{2,1,0:T(8,128)(2,1)}, bf16[2,256,128]{2,1,0:T(8,128)(2,1)S(1)}, u32[]{:S(2)}, u32[]{:S(2)}) collective-permute-start(bf16[2,256,128]{2,1,0:T(8,128)(2,1)} %bitcast.18), channel_id=1, source_target_pairs={{0,2},{1,3},{2,4},{3,5},{4,6},{5,7},{6,8},{7,9},{8,10},{9,11},{10,... | collective-permute-start | bytes 393224 | tf_op jit(solution)/shard_map/strips/ppermute | solution.py:377
  8.0 0.7 bitcast_convert_fusion
  8.7 0.1 copy.15.lw
  8.7 0.0 copy-done.4
  8.7 0.1 copy.14.mw
  8.9 0.0 copy-done.2
  8.9 0.0 copy-start.3
  8.9 0.8 copy-done.3
  9.7 0.0 copy-start
  9.7 4.0 %banded_weights.1 = (bf16[768,256]{1,0:T(8,128)(2,1)S(1)}, bf16[192,768]{1,0:T(8,128)(2,1)S(1)}, bf16[192,192]{1,0:T(8,128)(2,1)S(1)}, bf16[24,192]{1,0:T(8,128)(2,1)S(1)}) custom-call(bf16[9,32,32]{2,1,0:T(8,128)(2,1)S(1)} %copy-done.2, bf16[27,8,32]{2,1,0:T(8,128)(2,1)S(1)} %copy-done.3, bf16[27,8,8]{2,1,0:T(8,128)(2,1)S(1)} %copy.14.mw, ...), custom_call_target="tpu_custom_call" | custom-call | flops 2000000000 | bytes 1000000 | tf_op jit(solution)/shard_map/banded_weights/pallas_call | solution.py:91
  13.8 0.1 pad_add_fusion.pos
  13.9 0.0 collective-permute-done.2.sp
  13.9 0.0 collective-permute-done.1.s1
  13.9 0.0 collective-permute-done.s2
  13.9 0.0 copy-done
  13.9 2.0 %features.1 = (bf16[2,256,256]{2,1,0:T(8,128)(2,1)S(1)}, bf16[2,256,256]{2,1,0:T(8,128)(2,1)S(1)}, bf16[2,256,256]{2,1,0:T(8,128)(2,1)S(1)}, bf16[2,256,256]{2,1,0:T(8,128)(2,1)S(1)}) custom-call(s32[3]{0:T(128)S(1)} %pad_add_fusion.pos, bf16[2,256,128]{2,1,0:T(8,128)(2,1)S(1)} %collective-permute-done.s2, ...), custom_call_target="tpu_custom_call" | custom-call | tf_op jit(solution)/shard_map/features/pallas_call | solution.py:125
  15.9 0.6 collective-permute-start.3
  16.6 0.0 copy-start.5
  16.6 2.4 %collective-permute-start.4 = (bf16[2,256,256]{2,1,0:T(8,128)(2,1)S(1)}, bf16[2,256,256]{2,1,0:T(8,128)(2,1)S(1)}, u32[]{:S(2)}, u32[]{:S(2)}) collective-permute-start(bf16[2,256,256]{2,1,0:T(8,128)(2,1)S(1)} %get-tuple-element.20), channel_id=1, source_target_pairs={{0,128},{64,192},{128,0},{192,64},{1,129},{65,193},{129,1},{193,65... | collective-permute-start | bytes 786440 | tf_op jit(solution)/shard_map/views/ppermute | solution.py:394
  19.0 0.0 copy-start.1
  19.0 0.5 collective-permute-start.5
  19.5 0.0 copy-done.5
  19.5 0.1 copy.16.frame
  19.6 5.6 %collective-permute-done.3.f1 = bf16[2,256,256]{2,1,0:T(8,128)(2,1)S(1)} collective-permute-done((bf16[2,256,256]{2,1,0:T(8,128)(2,1)S(1)}, bf16[2,256,256]{2,1,0:T(8,128)(2,1)S(1)}, u32[]{:S(2)}, u32[]{:S(2)}) %collective-permute-start.3) | collective-permute-done | bytes 262176 | tf_op jit(solution)/shard_map/views/ppermute | solution.py:394
  25.2 6.6 %collective-permute-done.4.f2 = bf16[2,256,256]{2,1,0:T(8,128)(2,1)S(1)} collective-permute-done((bf16[2,256,256]{2,1,0:T(8,128)(2,1)S(1)}, bf16[2,256,256]{2,1,0:T(8,128)(2,1)S(1)}, u32[]{:S(2)}, u32[]{:S(2)}) %collective-permute-start.4) | collective-permute-done | bytes 262176 | tf_op jit(solution)/shard_map/views/ppermute | solution.py:394
  31.8 1.4 %collective-permute-done.5.f3 = bf16[2,256,256]{2,1,0:T(8,128)(2,1)S(1)} collective-permute-done((bf16[2,256,256]{2,1,0:T(8,128)(2,1)S(1)}, bf16[2,256,256]{2,1,0:T(8,128)(2,1)S(1)}, u32[]{:S(2)}, u32[]{:S(2)}) %collective-permute-start.5) | collective-permute-done | bytes 262176 | tf_op jit(solution)/shard_map/views/ppermute | solution.py:394
  33.2 0.0 copy-done.1
  33.2 14.5 %cost_volume.1 = (f32[2048,128]{1,0:T(8,128)S(1)}, f32[256,128]{1,0:T(8,128)S(1)}) custom-call(s32[3]{0:T(128)S(1)} %pad_add_fusion.pos, s32[8,96]{1,0:T(8,128)S(1)} %copy-done.1, s32[8,2]{1,0:T(8,128)S(1)} %copy.16.frame, bf16[2,256,256]{2,1,0:T(8,128)(2,1)S(1)} %get-tuple-element.18.f0, bf16[2,256,256]{2,1,0:T(8,128)(2,1)S(1)} %collective-permute-done.3.f1, ...), custom_call_target="tpu_custom_call" | custom-call | tf_op jit(solution)/shard_map/cost_volume/pallas_call | solution.py:283
  47.7 26.9 %all_to_all.22 = f32[256,1,128]{2,1,0:T(1,128)S(1)} all-to-all(f32[256,1,128]{2,1,0:T(1,128)S(1)} %bitcast.20), channel_id=1, replica_groups=mesh['depth'=4,'col'=64] {'depth','col'}, dimensions={0} | all-to-all | bytes 262144 | tf_op jit(solution)/shard_map/all_to_all | solution.py:381
  74.6 4.0 %second_conv.1 = (f32[2048,128]{1,0:T(8,128)S(1)}, f32[256,128]{1,0:T(8,128)S(1)}) custom-call(s32[3]{0:T(128)S(1)} %pad_add_fusion.pos, f32[256,128]{1,0:T(8,128)S(1)} %bitcast.14, f32[2048,128]{1,0:T(8,128)S(1)} %get-tuple-element.24.values, bf16[192,192]{1,0:T(8,128)(2,1)S(1)} %get-tuple-element.25.w2), custom_call_target="tpu_custom_call" | custom-call | tf_op jit(solution)/shard_map/second_conv/pallas_call | solution.py:308
  78.6 18.1 %all_to_all.23 = f32[256,1,128]{2,1,0:T(1,128)S(1)} all-to-all(f32[256,1,128]{2,1,0:T(1,128)S(1)} %bitcast.21), channel_id=1, replica_groups=mesh['depth'=4,'col'=64] {'depth','col'}, dimensions={0} | all-to-all | bytes 262144 | tf_op jit(solution)/shard_map/all_to_all | solution.py:381
  96.7 3.3 %final_estimate.1 = f32[8,128]{1,0:T(8,128)S(1)} custom-call(s32[3]{0:T(128)S(1)} %pad_add_fusion.pos, f32[256,128]{1,0:T(8,128)S(1)} %bitcast.15, f32[2048,128]{1,0:T(8,128)S(1)} %get-tuple-element.27.values, bf16[24,192]{1,0:T(8,128)(2,1)S(1)} %get-tuple-element.28.w3), custom_call_target="tpu_custom_call" | custom-call | tf_op jit(solution)/shard_map/final_estimate/pallas_call | solution.py:361
  100.0 0.4 collective-permute-start.8
  100.4 3.1 %collective-permute-start.7 = (f32[8,128]{1,0:T(8,128)S(1)}, f32[8,128]{1,0:T(8,128)S(1)}, u32[]{:S(2)}, u32[]{:S(2)}) collective-permute-start(f32[8,128]{1,0:T(8,128)S(1)} %final_estimate.1), channel_id=1, source_target_pairs={{0,128},{64,192},{128,0},{192,64},{1,129},{65,193},{129,1},{193,65... | collective-permute-start | bytes 12296 | tf_op jit(solution)/shard_map/columns/ppermute | solution.py:400
  103.5 0.6 collective-permute-start.6
  104.1 0.0 collective-permute-done.8
  104.1 1.4 %collective-permute-done.7 = f32[8,128]{1,0:T(8,128)S(1)} collective-permute-done((f32[8,128]{1,0:T(8,128)S(1)}, f32[8,128]{1,0:T(8,128)S(1)}, u32[]{:S(2)}, u32[]{:S(2)}) %collective-permute-start.7) | collective-permute-done | bytes 4128 | tf_op jit(solution)/shard_map/columns/ppermute | solution.py:400
  105.5 1.6 %collective-permute-done.6 = f32[8,128]{1,0:T(8,128)S(1)} collective-permute-done((f32[8,128]{1,0:T(8,128)S(1)}, f32[8,128]{1,0:T(8,128)S(1)}, u32[]{:S(2)}, u32[]{:S(2)}) %collective-permute-start.6) | collective-permute-done | bytes 4128 | tf_op jit(solution)/shard_map/columns/ppermute | solution.py:400
  107.1 0.6 add_add_fusion
Async XLA Ops:
  0.0 8.7 %copy-start.4 = (bf16[27,8,8]{0,2,1:T(8,128)(2,1)S(1)}, bf16[27,8,8]{0,2,1:T(8,128)(2,1)}, u32[]{:S(2)}) copy-start(bf16[27,8,8]{0,2,1:T(8,128)(2,1)} %param.12) | copy-start | bytes 10372
  0.0 8.9 %copy-start.2 = (bf16[9,32,32]{2,1,0:T(8,128)(2,1)S(1)}, bf16[9,32,32]{2,1,0:T(8,128)(2,1)}, u32[]{:S(2)}) copy-start(bf16[9,32,32]{2,1,0:T(8,128)(2,1)} %fw.1) | copy-start | bytes 55300
  0.0 13.8 %collective-permute-start.2 = (bf16[2,256,128]{2,1,0:T(8,128)(2,1)}, bf16[2,256,128]{2,1,0:T(8,128)(2,1)S(1)}, u32[]{:S(2)}, u32[]{:S(2)}) collective-permute-start(bf16[2,256,128]{2,1,0:T(8,128)(2,1)} %bitcast.16), channel_id=1, source_target_pairs={{1,0},{2,1},{3,2},{4,3},{5,4},{6,5},{7,6},{8,7},{9,8},{10,9},{11,1... | collective-permute-start | bytes 393224 | tf_op jit(solution)/shard_map/strips/ppermute | solution.py:377
  1.4 12.4 %collective-permute-start.1 = (bf16[2,256,128]{2,1,0:T(8,128)(2,1)}, bf16[2,256,128]{2,1,0:T(8,128)(2,1)S(1)}, u32[]{:S(2)}, u32[]{:S(2)}) collective-permute-start(bf16[2,256,128]{2,1,0:T(8,128)(2,1)} %bitcast.17), channel_id=1, source_target_pairs={{0,1},{1,2},{2,3},{3,4},{4,5},{5,6},{6,7},{7,8},{8,9},{9,10},{10,1... | collective-permute-start | bytes 393224 | tf_op jit(solution)/shard_map/strips/ppermute | solution.py:377
  4.5 9.4 %collective-permute-start = (bf16[2,256,128]{2,1,0:T(8,128)(2,1)}, bf16[2,256,128]{2,1,0:T(8,128)(2,1)S(1)}, u32[]{:S(2)}, u32[]{:S(2)}) collective-permute-start(bf16[2,256,128]{2,1,0:T(8,128)(2,1)} %bitcast.18), channel_id=1, source_target_pairs={{0,2},{1,3},{2,4},{3,5},{4,6},{5,7},{6,8},{7,9},{8,10},{9,11},{10,... | collective-permute-start | bytes 393224 | tf_op jit(solution)/shard_map/strips/ppermute | solution.py:377
  8.9 0.8 copy-start.3
  9.7 4.2 %copy-start = (bf16[2,32,8,128]{3,2,1,0:T(8,128)(2,1)S(1)}, bf16[2,32,8,128]{3,2,1,0:T(8,128)(2,1)}, u32[]{:S(2)}) copy-start(bf16[2,32,8,128]{3,2,1,0:T(8,128)(2,1)} %param.7) | copy-start | bytes 393220
  15.9 9.3 %collective-permute-start.3 = (bf16[2,256,256]{2,1,0:T(8,128)(2,1)S(1)}, bf16[2,256,256]{2,1,0:T(8,128)(2,1)S(1)}, u32[]{:S(2)}, u32[]{:S(2)}) collective-permute-start(bf16[2,256,256]{2,1,0:T(8,128)(2,1)S(1)} %get-tuple-element.19), channel_id=1, source_target_pairs={{0,64},{64,0},{128,192},{192,128},{1,65},{65,1},{129,193},{193,129... | collective-permute-start | bytes 786440 | tf_op jit(solution)/shard_map/views/ppermute | solution.py:394
  16.6 3.0 %copy-start.5 = (s32[8,2]{0,1:T(2,128)S(1)}, s32[8,2]{0,1:T(2,128)}, u32[]{:S(2)}) copy-start(s32[8,2]{0,1:T(2,128)} %param.10) | copy-start | bytes 196
  16.6 15.3 %collective-permute-start.4 = (bf16[2,256,256]{2,1,0:T(8,128)(2,1)S(1)}, bf16[2,256,256]{2,1,0:T(8,128)(2,1)S(1)}, u32[]{:S(2)}, u32[]{:S(2)}) collective-permute-start(bf16[2,256,256]{2,1,0:T(8,128)(2,1)S(1)} %get-tuple-element.20), channel_id=1, source_target_pairs={{0,128},{64,192},{128,0},{192,64},{1,129},{65,193},{129,1},{193,65... | collective-permute-start | bytes 786440 | tf_op jit(solution)/shard_map/views/ppermute | solution.py:394
  19.0 14.2 %copy-start.1 = (s32[8,96]{1,0:T(8,128)S(1)}, s32[8,96]{1,0:T(8,128)}, u32[]{:S(2)}) copy-start(s32[8,96]{1,0:T(8,128)} %shifts.1) | copy-start | bytes 9220
  19.0 14.2 %collective-permute-start.5 = (bf16[2,256,256]{2,1,0:T(8,128)(2,1)S(1)}, bf16[2,256,256]{2,1,0:T(8,128)(2,1)S(1)}, u32[]{:S(2)}, u32[]{:S(2)}) collective-permute-start(bf16[2,256,256]{2,1,0:T(8,128)(2,1)S(1)} %get-tuple-element.21), channel_id=1, source_target_pairs={{0,192},{64,128},{128,64},{192,0},{1,193},{65,129},{129,65},{193,1... | collective-permute-start | bytes 786440 | tf_op jit(solution)/shard_map/views/ppermute | solution.py:394
  100.0 4.1 %collective-permute-start.8 = (f32[8,128]{1,0:T(8,128)S(1)}, f32[8,128]{1,0:T(8,128)S(1)}, u32[]{:S(2)}, u32[]{:S(2)}) collective-permute-start(f32[8,128]{1,0:T(8,128)S(1)} %final_estimate.1), channel_id=1, source_target_pairs={{0,192},{64,128},{128,64},{192,0},{1,193},{65,129},{129,65},{193,1... | collective-permute-start | bytes 12296 | tf_op jit(solution)/shard_map/columns/ppermute | solution.py:400
  100.4 5.1 %collective-permute-start.7 = (f32[8,128]{1,0:T(8,128)S(1)}, f32[8,128]{1,0:T(8,128)S(1)}, u32[]{:S(2)}, u32[]{:S(2)}) collective-permute-start(f32[8,128]{1,0:T(8,128)S(1)} %final_estimate.1), channel_id=1, source_target_pairs={{0,128},{64,192},{128,0},{192,64},{1,129},{65,193},{129,1},{193,65... | collective-permute-start | bytes 12296 | tf_op jit(solution)/shard_map/columns/ppermute | solution.py:400
  103.5 3.6 %collective-permute-start.6 = (f32[8,128]{1,0:T(8,128)S(1)}, f32[8,128]{1,0:T(8,128)S(1)}, u32[]{:S(2)}, u32[]{:S(2)}) collective-permute-start(f32[8,128]{1,0:T(8,128)S(1)} %final_estimate.1), channel_id=1, source_target_pairs={{0,64},{64,0},{128,192},{192,128},{1,65},{65,1},{129,193},{193,129... | collective-permute-start | bytes 12296 | tf_op jit(solution)/shard_map/columns/ppermute | solution.py:400

commit v3 on v2

--- a/solution.py
+++ b/solution.py
@@ -22,6 +22,7 @@
 HALO = 5
 TILES = 32
 LEFT = 136
+EDGE = 8
 BASE = 176
 CR = CHAN * ROWS
 HR = HID * ROWS
@@ -104,32 +105,32 @@
     )(feat_weight, cost_weight, mid_weight, final_weight.astype(F32).reshape(27, 1, HID))
 
 
-def features_kernel(pos, s2, s1, s0, sp, wf, *outs):
+def views_kernel(pos, r0, r1, r2, r3, every, edge):
     depth = pos[0]
-    for u in range(2):
-        x = jnp.concatenate([s2[u], s1[u], s0[u], sp[u]], axis=1)
-        y = mm(wf[...], x)
-        f = (
-            y[CR : 2 * CR]
-            + pltpu.roll(y[:CR], 1, axis=1)
-            + pltpu.roll(y[2 * CR :], 4 * STRIP - 1, axis=1)
-        )
-        f = f.astype(BF16).astype(F32)
-        for k in range(4):
-            target = depth ^ k
-            start = OWN * target + 2 * STRIP - LEFT
-            outs[k][u] = pltpu.roll(f, 4 * STRIP - start, axis=1)[:, : 2 * STRIP].astype(BF16)
-
-
-def make_features(pos, strips, wf):
+    for k, r in enumerate((r0, r1, r2, r3)):
+        for u in range(2):
+            every[2 * (depth ^ k) + u] = r[u]
+    lane = iota((1, STRIP), 1)
+    turn = jnp.where(depth == 0, EDGE, 0)
+    packed = jnp.zeros((CR, STRIP), F32)
+    for v in range(VIEWS):
+        x = pltpu.roll(every[v].astype(F32), turn + EDGE * v, axis=1)
+        packed = jnp.where((lane >> 3) == v, x, packed)
+    edge[...] = packed.astype(BF16)
+
+
+def all_views(pos, parts):
     return pl.pallas_call(
-        features_kernel,
-        out_shape=tuple(jax.ShapeDtypeStruct((2, CR, 2 * STRIP), BF16) for _ in range(4)),
-        in_specs=[SMEM] + [VMEM] * 5,
-        out_specs=(VMEM,) * 4,
+        views_kernel,
+        out_shape=(
+            jax.ShapeDtypeStruct((VIEWS, CR, STRIP), BF16),
+            jax.ShapeDtypeStruct((CR, STRIP), BF16),
+        ),
+        in_specs=[SMEM] + [VMEM] * 4,
+        out_specs=(VMEM,) * 2,
         compiler_params=PARAMS,
-        name="features",
-    )(pos, *strips, wf)
+        name="all_views",
+    )(pos, *parts)
 
 
 def lane_places(width):
@@ -215,15 +216,44 @@
     wrap_tiles(act, HR)
 
 
-def volume_kernel(pos, shifts, frame, f0, f1, f2, f3, w1, out, stats, feats, even, odd, vol):
+def window_features(depth, every, left, edge, wf, feats):
+    lane = iota((1, STRIP), 1)
+    start = (OWN * depth + STRIP - EDGE) & (STRIP - 1)
+    back = STRIP - start
+    first = depth == 0
+
+    def one(v, carry):
+        own = every[v].astype(F32)
+        before = left[v].astype(F32)
+        far = pltpu.roll(edge[...].astype(F32), (3 * STRIP - EDGE * v - jnp.where(first, EDGE, 0)) & (STRIP - 1), axis=1)
+        a = jnp.where(first, far, before)
+        b = jnp.where(first, before, own)
+        c = jnp.where(first, own, far)
+        x = jnp.concatenate(
+            [
+                pltpu.roll(jnp.where(lane >= start, a, b), back, axis=1),
+                pltpu.roll(jnp.where(lane >= start, b, c), back, axis=1),
+            ],
+            axis=1,
+        ).astype(BF16)
+        y = mm(wf[...], x)
+        f = (
+            y[CR : 2 * CR]
+            + pltpu.roll(y[:CR], 1, axis=1)
+            + pltpu.roll(y[2 * CR :], 2 * STRIP - 1, axis=1)
+        )
+        feats[v] = f.astype(BF16)
+        return carry
+
+    lax.fori_loop(0, VIEWS, one, 0)
+
+
+def volume_kernel(pos, shifts, frame, every, left, edge, wf, w1, out, stats, feats, even, odd, vol):
     depth = pos[0]
     base = STRIP * pos[1] + OWN * depth
     wide = 2 * STRIP
     lane = iota((1, wide), 1)
-    sources = (f0, f1, f2, f3)
-    for k in range(4):
-        for u in range(2):
-            feats[2 * (depth ^ k) + u] = sources[k][u]
+    window_features(depth, every, left, edge, wf, feats)
     zero_view = pltpu.roll(feats[0].astype(F32), BASE - (LEFT - HALO), axis=1)
     own_lanes = (lane >= BASE) & (lane < BASE + GROUP)
     for v in range(1, VIEWS):
@@ -279,7 +309,7 @@
     conv_and_stats(w1, vol, CR, out, stats)
 
 
-def cost_and_conv(pos, shifts, frame, feats, w1):
+def cost_and_conv(pos, shifts, frame, every, left, edge, wf, w1):
     return pl.pallas_call(
         volume_kernel,
         out_shape=(
@@ -296,7 +326,7 @@
         ],
         compiler_params=PARAMS,
         name="cost_volume",
-    )(pos, shifts, frame, *feats, w1)
+    )(pos, shifts, frame, every, left, edge, wf, w1)
 
 
 def middle_kernel(pos, stats_in, values, w2, out, stats, act):
@@ -372,11 +402,6 @@
     )(pos, stats, values, w3)
 
 
-def beside(x, by):
-    peers = lax.axis_size("col")
-    return lax.ppermute(x, "col", [(i, i + by) for i in range(peers) if 0 <= i + by < peers])
-
-
 def everyones(stats):
     return lax.all_to_all(stats, ("depth", "col"), 0, 0, tiled=True)
 
@@ -385,15 +410,19 @@
     pos = jnp.stack([lax.axis_index("depth"), lax.axis_index("col"), jnp.int32(lax.axis_size("col"))])
     pos = pos.astype(I32)
     own = raw_views.reshape(2, CR, STRIP)
+    with jax.named_scope("views"):
+        parts = [own] + [lax.ppermute(own, "depth", [(i, i ^ k) for i in range(4)]) for k in (1, 2, 3)]
+        every, edge = all_views(pos, parts)
     with jax.named_scope("strips"):
-        strips = (beside(own, 2), beside(own, 1), own, beside(own, -1))
-    wf, w1, w2, w3 = make_weights(feat_weight, cost_weight, mid_weight, final_weight)
-    windows = make_features(pos, strips, wf)
-    with jax.named_scope("views"):
-        feats = [windows[0]] + [
-            lax.ppermute(windows[k], "depth", [(i, i ^ k) for i in range(4)]) for k in (1, 2, 3)
-        ]
-    first, stats = cost_and_conv(pos, shifts, frame_range, feats, w1)
+        cols = lax.axis_size("col")
+        far = [(i, i + 2) for i in range(cols - 2)] + [(3 * cols + i, 3 * cols + i - 1) for i in range(1, cols)]
+        left = lax.ppermute(every, "col", [(i, i + 1) for i in range(cols - 1)])
+        edge = lax.ppermute(edge, ("depth", "col"), far)
+    *weights, every = lax.optimization_barrier(
+        (feat_weight, cost_weight, mid_weight, final_weight, every)
+    )
+    wf, w1, w2, w3 = make_weights(*weights)
+    first, stats = cost_and_conv(pos, shifts, frame_range, every, left, edge, wf, w1)
     second, stats = second_conv(pos, everyones(stats), first, w2)
     part = final_estimate(pos, everyones(stats), second, w3)
     with jax.named_scope("columns"):

time: 108 us -> 101 us (0.935)
  waiting for transfers between devices: 16.6 us -> 8.7 us
  starting transfers between devices: 15.6 us -> 10.6 us
  blocking collectives: 45 us -> 49.2 us
  Pallas kernels: 27.9 us -> 30.7 us
    ppermute x6 -> x5, waiting for transfers between devices: 13.6 us -> 5.67 us  [the longest x3 5.67 us: local(): lax.ppermute(own, 'depth', [(i, i ^ k) for i in range(4)])]
    ppermute x6 -> x5, starting transfers between devices: 11.5 us -> 6.46 us  [the longest x3 4.34 us: local(): lax.ppermute(own, 'depth', [(i, i ^ k) for i in range(4)])]
    all_to_all x2, blocking collectives: 45 us -> 49.2 us  [everyones(): return lax.all_to_all(stats, ('depth', 'col'), 0, 0, tiled=True)]
    pallas_call x1, Pallas kernels: 14.5 us -> 18.6 us  [cost_and_conv(): pl.pallas_call(volume_kernel, out_shape=(jax.ShapeDtypeStruct((TILES * HR...]
    pallas_call x1, Pallas kernels: 2.04 us -> 0.78 us  [all_views(): pl.pallas_call(views_kernel, out_shape=(jax.ShapeDtypeStruct((VIEWS, CR,...]
  transfers between devices with their start and end apart: 9 -> 8, of which waited for: 5 -> 5; matrix products, arithmetic and copies ran while one was open for 1% -> 0% of each run, Pallas kernels for 4% -> 4%
where the time goes in v3:
time: 101 us
  blocking collectives  49.2 us (49%)
  Pallas kernels  30.7 us (30%)
  starting transfers between devices  10.6 us (10%)
  waiting for transfers between devices  8.7 us (9%)
  local copies, waits for them, and re-layouts  1.25 us (1%)
    all_to_all x2, blocking collectives, everyones(): return lax.all_to_all(stats, ('depth', 'col'), 0, 0, tiled=True)  49.2 us
    pallas_call x1, Pallas kernels, cost_and_conv(): pl.pallas_call(volume_kernel, out_shape=(jax.ShapeDtypeStruct((TILES * HR...  18.6 us
    ppermute x3, waiting for transfers between devices, local(): lax.ppermute(own, 'depth', [(i, i ^ k) for i in range(4)])  5.67 us
    ppermute x3, starting transfers between devices, local(): lax.ppermute(own, 'depth', [(i, i ^ k) for i in range(4)])  4.34 us
    ppermute x3, starting transfers between devices, local(): lax.ppermute(part, 'depth', [(i, i ^ k) for i in range(4)])  4.13 us
    pallas_call x1, Pallas kernels, make_weights(): pl.pallas_call(weights_kernel, out_shape=(jax.ShapeDtypeStruct((3 * CR, C...  4.07 us
    pallas_call x1, Pallas kernels, second_conv(): pl.pallas_call(middle_kernel, out_shape=(jax.ShapeDtypeStruct((TILES * HR...  3.98 us
    pallas_call x1, Pallas kernels, final_estimate(): pl.pallas_call(last_kernel, out_shape=jax.ShapeDtypeStruct((ROWS, STRIP),...  3.27 us
  transfers between devices with their start and end apart: 8, of which 5 were waited for; matrix products, arithmetic and copies ran while one was open for 0% of the time, Pallas kernels for 4%

profile of v3, /device:TPU:2, one launch (start us, length us, event | category | flops | bytes accessed | tf_op | source)
XLA Modules:
  0.0 101.3 jit_solution(10960079701939069784)
XLA Ops:
  0.0 1.5 %collective-permute-start.2 = (bf16[2,256,128]{2,1,0:T(8,128)(2,1)}, bf16[2,256,128]{2,1,0:T(8,128)(2,1)S(1)}, u32[]{:S(2)}, u32[]{:S(2)}) collective-permute-start(bf16[2,256,128]{2,1,0:T(8,128)(2,1)} %bitcast.16), channel_id=1, source_target_pairs={{0,192},{64,128},{128,64},{192,0},{1,193},{65,129},{129,65},{193,1... | collective-permute-start | bytes 393224 | tf_op jit(solution)/shard_map/views/ppermute | solution.py:414
  1.5 2.8 %collective-permute-start.1 = (bf16[2,256,128]{2,1,0:T(8,128)(2,1)}, bf16[2,256,128]{2,1,0:T(8,128)(2,1)S(1)}, u32[]{:S(2)}, u32[]{:S(2)}) collective-permute-start(bf16[2,256,128]{2,1,0:T(8,128)(2,1)} %bitcast.17), channel_id=1, source_target_pairs={{0,128},{64,192},{128,0},{192,64},{1,129},{65,193},{129,1},{193,65... | collective-permute-start | bytes 393224 | tf_op jit(solution)/shard_map/views/ppermute | solution.py:414
  4.3 0.0 collective-permute-start
  4.3 0.1 pad_add_fusion.pos
  4.4 2.4 %collective-permute-done.2.r3 = bf16[2,256,128]{2,1,0:T(8,128)(2,1)S(1)} collective-permute-done((bf16[2,256,128]{2,1,0:T(8,128)(2,1)}, bf16[2,256,128]{2,1,0:T(8,128)(2,1)S(1)}, u32[]{:S(2)}, u32[]{:S(2)}) %collective-permute-start.2) | collective-permute-done | bytes 131104 | tf_op jit(solution)/shard_map/views/ppermute | solution.py:414
  6.8 2.8 %collective-permute-done.1.r2 = bf16[2,256,128]{2,1,0:T(8,128)(2,1)S(1)} collective-permute-done((bf16[2,256,128]{2,1,0:T(8,128)(2,1)}, bf16[2,256,128]{2,1,0:T(8,128)(2,1)S(1)}, u32[]{:S(2)}, u32[]{:S(2)}) %collective-permute-start.1) | collective-permute-done | bytes 131104 | tf_op jit(solution)/shard_map/views/ppermute | solution.py:414
  9.6 0.5 collective-permute-done.r1
  10.1 0.0 copy-start
  10.1 0.9 copy-done
  11.0 0.0 copy-start.6
  11.0 0.0 copy-start.5
  11.0 0.0 copy-start.4
  11.0 0.0 copy-start.3
  11.0 0.8 all_views.1
  11.8 0.0 copy-start.2
  11.8 1.5 %collective-permute-start.3 = (bf16[8,256,128]{2,1,0:T(8,128)(2,1)S(1)}, bf16[8,256,128]{2,1,0:T(8,128)(2,1)S(1)}, u32[]{:S(2)}, u32[]{:S(2)}) collective-permute-start(bf16[8,256,128]{2,1,0:T(8,128)(2,1)S(1)} %get-tuple-element.21.every), channel_id=1, source_target_pairs={{0,1},{1,2},{2,3},{3,4},{4,5},{5,6},{6,7},{7,8},{8,9},{9,10},{10,1... | collective-permute-start | bytes 1572872 | tf_op jit(solution)/shard_map/strips/ppermute | solution.py:419
  13.3 0.0 copy-done.6
  13.3 0.1 copy.16.frame
  13.4 0.0 copy-done.5
  13.4 0.1 copy.15.lw
  13.5 0.0 copy-done.4
  13.5 0.1 copy.14.mw
  13.6 0.7 collective-permute-start.4
  14.3 0.0 copy-done.3
  14.3 0.0 copy-done.2
  14.3 0.0 copy-start.1
  14.3 4.1 %banded_weights.1 = (bf16[768,256]{1,0:T(8,128)(2,1)S(1)}, bf16[192,768]{1,0:T(8,128)(2,1)S(1)}, bf16[192,192]{1,0:T(8,128)(2,1)S(1)}, bf16[24,192]{1,0:T(8,128)(2,1)S(1)}) custom-call(bf16[9,32,32]{2,1,0:T(8,128)(2,1)S(1)} %copy-done.2, bf16[27,8,32]{2,1,0:T(8,128)(2,1)S(1)} %copy-done.3, bf16[27,8,8]{2,1,0:T(8,128)(2,1)S(1)} %copy.14.mw, ...), custom_call_target="tpu_custom_call" | custom-call | flops 2000000000 | bytes 1000000 | tf_op jit(solution)/shard_map/banded_weights/pallas_call | solution.py:92
  18.4 0.0 collective-permute-done.4.edge
  18.4 0.0 collective-permute-done.3.left
  18.4 0.0 copy-done.1
  18.4 18.6 %cost_volume.1 = (f32[2048,128]{1,0:T(8,128)S(1)}, f32[256,128]{1,0:T(8,128)S(1)}) custom-call(s32[3]{0:T(128)S(1)} %pad_add_fusion.pos, s32[8,96]{1,0:T(8,128)S(1)} %copy-done.1, s32[8,2]{1,0:T(8,128)S(1)} %copy.16.frame, bf16[8,256,128]{2,1,0:T(8,128)(2,1)S(1)} %get-tuple-element.21.every, bf16[8,256,128]{2,1,0:T(8,128)(2,1)S(1)} %collective-permute-done.3.left, ...), custom_call_target="tpu_custom_call" | custom-call | tf_op jit(solution)/shard_map/cost_volume/pallas_call | solution.py:313
  37.0 31.1 %all_to_all.22 = f32[256,1,128]{2,1,0:T(1,128)S(1)} all-to-all(f32[256,1,128]{2,1,0:T(1,128)S(1)} %bitcast.20), channel_id=1, replica_groups=mesh['depth'=4,'col'=64] {'depth','col'}, dimensions={0} | all-to-all | bytes 262144 | tf_op jit(solution)/shard_map/all_to_all | solution.py:406
  68.1 4.0 %second_conv.1 = (f32[2048,128]{1,0:T(8,128)S(1)}, f32[256,128]{1,0:T(8,128)S(1)}) custom-call(s32[3]{0:T(128)S(1)} %pad_add_fusion.pos, f32[256,128]{1,0:T(8,128)S(1)} %bitcast.14, f32[2048,128]{1,0:T(8,128)S(1)} %get-tuple-element.30.values, bf16[192,192]{1,0:T(8,128)(2,1)S(1)} %get-tuple-element.31.w2), custom_call_target="tpu_custom_call" | custom-call | tf_op jit(solution)/shard_map/second_conv/pallas_call | solution.py:338
  72.1 18.2 %all_to_all.23 = f32[256,1,128]{2,1,0:T(1,128)S(1)} all-to-all(f32[256,1,128]{2,1,0:T(1,128)S(1)} %bitcast.21), channel_id=1, replica_groups=mesh['depth'=4,'col'=64] {'depth','col'}, dimensions={0} | all-to-all | bytes 262144 | tf_op jit(solution)/shard_map/all_to_all | solution.py:406
  90.2 3.3 %final_estimate.1 = f32[8,128]{1,0:T(8,128)S(1)} custom-call(s32[3]{0:T(128)S(1)} %pad_add_fusion.pos, f32[256,128]{1,0:T(8,128)S(1)} %bitcast.15, f32[2048,128]{1,0:T(8,128)S(1)} %get-tuple-element.33.values, bf16[24,192]{1,0:T(8,128)(2,1)S(1)} %get-tuple-element.34.w3), custom_call_target="tpu_custom_call" | custom-call | tf_op jit(solution)/shard_map/final_estimate/pallas_call | solution.py:391
  93.5 0.4 collective-permute-start.7
  93.9 3.1 %collective-permute-start.6 = (f32[8,128]{1,0:T(8,128)S(1)}, f32[8,128]{1,0:T(8,128)S(1)}, u32[]{:S(2)}, u32[]{:S(2)}) collective-permute-start(f32[8,128]{1,0:T(8,128)S(1)} %final_estimate.1), channel_id=1, source_target_pairs={{0,128},{64,192},{128,0},{192,64},{1,129},{65,193},{129,1},{193,65... | collective-permute-start | bytes 12296 | tf_op jit(solution)/shard_map/columns/ppermute | solution.py:429
  97.0 0.6 collective-permute-start.5
  97.6 0.0 collective-permute-done.7
  97.6 1.4 %collective-permute-done.6 = f32[8,128]{1,0:T(8,128)S(1)} collective-permute-done((f32[8,128]{1,0:T(8,128)S(1)}, f32[8,128]{1,0:T(8,128)S(1)}, u32[]{:S(2)}, u32[]{:S(2)}) %collective-permute-start.6) | collective-permute-done | bytes 4128 | tf_op jit(solution)/shard_map/columns/ppermute | solution.py:429
  99.0 1.6 %collective-permute-done.5 = f32[8,128]{1,0:T(8,128)S(1)} collective-permute-done((f32[8,128]{1,0:T(8,128)S(1)}, f32[8,128]{1,0:T(8,128)S(1)}, u32[]{:S(2)}, u32[]{:S(2)}) %collective-permute-start.5) | collective-permute-done | bytes 4128 | tf_op jit(solution)/shard_map/columns/ppermute | solution.py:429
  100.7 0.6 add_add_fusion
  (1 shorter events, 0.0 us)
Async XLA Ops:
  0.0 6.8 %collective-permute-start.2 = (bf16[2,256,128]{2,1,0:T(8,128)(2,1)}, bf16[2,256,128]{2,1,0:T(8,128)(2,1)S(1)}, u32[]{:S(2)}, u32[]{:S(2)}) collective-permute-start(bf16[2,256,128]{2,1,0:T(8,128)(2,1)} %bitcast.16), channel_id=1, source_target_pairs={{0,192},{64,128},{128,64},{192,0},{1,193},{65,129},{129,65},{193,1... | collective-permute-start | bytes 393224 | tf_op jit(solution)/shard_map/views/ppermute | solution.py:414
  1.5 8.1 %collective-permute-start.1 = (bf16[2,256,128]{2,1,0:T(8,128)(2,1)}, bf16[2,256,128]{2,1,0:T(8,128)(2,1)S(1)}, u32[]{:S(2)}, u32[]{:S(2)}) collective-permute-start(bf16[2,256,128]{2,1,0:T(8,128)(2,1)} %bitcast.17), channel_id=1, source_target_pairs={{0,128},{64,192},{128,0},{192,64},{1,129},{65,193},{129,1},{193,65... | collective-permute-start | bytes 393224 | tf_op jit(solution)/shard_map/views/ppermute | solution.py:414
  4.3 5.7 %collective-permute-start = (bf16[2,256,128]{2,1,0:T(8,128)(2,1)}, bf16[2,256,128]{2,1,0:T(8,128)(2,1)S(1)}, u32[]{:S(2)}, u32[]{:S(2)}) collective-permute-start(bf16[2,256,128]{2,1,0:T(8,128)(2,1)} %bitcast.18), channel_id=1, source_target_pairs={{0,64},{64,0},{128,192},{192,128},{1,65},{65,1},{129,193},{193,129... | collective-permute-start | bytes 393224 | tf_op jit(solution)/shard_map/views/ppermute | solution.py:414
  10.1 0.9 copy-start
  11.0 2.3 %copy-start.6 = (s32[8,2]{0,1:T(2,128)S(1)}, s32[8,2]{0,1:T(2,128)}, u32[]{:S(2)}) copy-start(s32[8,2]{0,1:T(2,128)} %param.10) | copy-start | bytes 196
  11.0 2.4 %copy-start.5 = (bf16[27,8]{0,1:T(8,128)(2,1)S(1)}, bf16[27,8]{0,1:T(8,128)(2,1)}, u32[]{:S(2)}) copy-start(bf16[27,8]{0,1:T(8,128)(2,1)} %param.13) | copy-start | bytes 1300
  11.0 2.5 %copy-start.4 = (bf16[27,8,8]{0,2,1:T(8,128)(2,1)S(1)}, bf16[27,8,8]{0,2,1:T(8,128)(2,1)}, u32[]{:S(2)}) copy-start(bf16[27,8,8]{0,2,1:T(8,128)(2,1)} %param.12) | copy-start | bytes 10372
  11.0 3.3 %copy-start.3 = (bf16[27,8,32]{2,1,0:T(8,128)(2,1)S(1)}, bf16[27,8,32]{2,1,0:T(8,128)(2,1)}, u32[]{:S(2)}) copy-start(bf16[27,8,32]{2,1,0:T(8,128)(2,1)} %cw) | copy-start | bytes 41476
  11.8 2.5 %copy-start.2 = (bf16[9,32,32]{2,1,0:T(8,128)(2,1)S(1)}, bf16[9,32,32]{2,1,0:T(8,128)(2,1)}, u32[]{:S(2)}) copy-start(bf16[9,32,32]{2,1,0:T(8,128)(2,1)} %fw) | copy-start | bytes 55300
  11.8 6.6 %collective-permute-start.3 = (bf16[8,256,128]{2,1,0:T(8,128)(2,1)S(1)}, bf16[8,256,128]{2,1,0:T(8,128)(2,1)S(1)}, u32[]{:S(2)}, u32[]{:S(2)}) collective-permute-start(bf16[8,256,128]{2,1,0:T(8,128)(2,1)S(1)} %get-tuple-element.21.every), channel_id=1, source_target_pairs={{0,1},{1,2},{2,3},{3,4},{4,5},{5,6},{6,7},{7,8},{8,9},{9,10},{10,1... | collective-permute-start | bytes 1572872 | tf_op jit(solution)/shard_map/strips/ppermute | solution.py:419
  13.6 4.8 %collective-permute-start.4 = (bf16[256,128]{1,0:T(8,128)(2,1)S(1)}, bf16[256,128]{1,0:T(8,128)(2,1)S(1)}, u32[]{:S(2)}, u32[]{:S(2)}) collective-permute-start(bf16[256,128]{1,0:T(8,128)(2,1)S(1)} %get-tuple-element.22), channel_id=1, source_target_pairs={{0,2},{1,3},{2,4},{3,5},{4,6},{5,7},{6,8},{7,9},{8,10},{9,11},{10,... | collective-permute-start | bytes 196616 | tf_op jit(solution)/shard_map/strips/ppermute | solution.py:420
  14.3 4.1 %copy-start.1 = (s32[8,96]{1,0:T(8,128)S(1)}, s32[8,96]{1,0:T(8,128)}, u32[]{:S(2)}) copy-start(s32[8,96]{1,0:T(8,128)} %shifts.1) | copy-start | bytes 9220
  93.5 4.1 %collective-permute-start.7 = (f32[8,128]{1,0:T(8,128)S(1)}, f32[8,128]{1,0:T(8,128)S(1)}, u32[]{:S(2)}, u32[]{:S(2)}) collective-permute-start(f32[8,128]{1,0:T(8,128)S(1)} %final_estimate.1), channel_id=1, source_target_pairs={{0,192},{64,128},{128,64},{192,0},{1,193},{65,129},{129,65},{193,1... | collective-permute-start | bytes 12296 | tf_op jit(solution)/shard_map/columns/ppermute | solution.py:429
  93.9 5.1 %collective-permute-start.6 = (f32[8,128]{1,0:T(8,128)S(1)}, f32[8,128]{1,0:T(8,128)S(1)}, u32[]{:S(2)}, u32[]{:S(2)}) collective-permute-start(f32[8,128]{1,0:T(8,128)S(1)} %final_estimate.1), channel_id=1, source_target_pairs={{0,128},{64,192},{128,0},{192,64},{1,129},{65,193},{129,1},{193,65... | collective-permute-start | bytes 12296 | tf_op jit(solution)/shard_map/columns/ppermute | solution.py:429
  97.0 3.6 %collective-permute-start.5 = (f32[8,128]{1,0:T(8,128)S(1)}, f32[8,128]{1,0:T(8,128)S(1)}, u32[]{:S(2)}, u32[]{:S(2)}) collective-permute-start(f32[8,128]{1,0:T(8,128)S(1)} %final_estimate.1), channel_id=1, source_target_pairs={{0,64},{64,0},{128,192},{192,128},{1,65},{65,1},{129,193},{193,129... | collective-permute-start | bytes 12296 | tf_op jit(solution)/shard_map/columns/ppermute | solution.py:429

commit v4 on v3

--- a/solution.py
+++ b/solution.py
@@ -18,9 +18,12 @@
 DEPTHS = 96
 STRIP = 128
 OWN = 32
+WIDE = 256
 GROUP = 42
+GROUPS = 6
+BLOCKS = 16
 HALO = 5
-TILES = 32
+UNROLL = 16
 LEFT = 136
 EDGE = 8
 BASE = 176
@@ -66,7 +69,7 @@
     ro32, ro8 = spread_rows(CHAN), spread_rows(HID)
     ci32, ci8 = spread_cols(CHAN), spread_cols(HID)
     for b in range(3):
-        wf[b * CR : (b + 1) * CR, :] = banded([fw[3 * a + b] for a in range(3)], ro32, ci32).astype(BF16)
+        wf[:, b * CR : (b + 1) * CR] = banded([fw[3 * a + b] for a in range(3)], ro32, ci32).astype(BF16)
     for a in range(3):
         for e in range(3):
             taps = [9 * a + 3 * b + e for b in range(3)]
@@ -92,7 +95,7 @@
     return pl.pallas_call(
         weights_kernel,
         out_shape=(
-            jax.ShapeDtypeStruct((3 * CR, CR), BF16),
+            jax.ShapeDtypeStruct((CR, 3 * CR), BF16),
             jax.ShapeDtypeStruct((3 * HR, 3 * CR), BF16),
             jax.ShapeDtypeStruct((3 * HR, 3 * HR), BF16),
             jax.ShapeDtypeStruct((3 * ROWS, 3 * HR), BF16),
@@ -119,6 +122,21 @@
     edge[...] = packed.astype(BF16)
 
 
+def copy_kernel(x, y):
+    y[...] = x[...]
+
+
+def copied(x):
+    return pl.pallas_call(
+        copy_kernel,
+        out_shape=jax.ShapeDtypeStruct(x.shape, x.dtype),
+        in_specs=[VMEM],
+        out_specs=VMEM,
+        compiler_params=PARAMS,
+        name="own_strip",
+    )(x)
+
+
 def all_views(pos, parts):
     return pl.pallas_call(
         views_kernel,
@@ -133,50 +151,55 @@
     )(pos, *parts)
 
 
-def lane_places(width):
-    lane = iota((1, width), 1) & (STRIP - 1)
-    group = (lane >= GROUP).astype(I32) + (lane >= 2 * GROUP).astype(I32)
+def lane_places():
+    lane = iota((1, WIDE), 1)
+    group = sum((lane >= GROUP * g).astype(I32) for g in range(1, GROUPS))
     return lane, group, lane - GROUP * group - HALO
 
 
-def wrap_tiles(ref, size):
-    lane = iota((1, STRIP), 1)
-    last = ref[TILES * size : (TILES + 1) * size, :].astype(F32)
+def wrap_blocks(ref, size):
+    lane = iota((1, WIDE), 1)
+    last = ref[BLOCKS * size : (BLOCKS + 1) * size, :].astype(F32)
     first = ref[size : 2 * size, :].astype(F32)
     before = jnp.where(lane >= GROUP, pltpu.roll(last, GROUP, axis=1), 0.0)
-    after = jnp.where(lane < 2 * GROUP, pltpu.roll(first, STRIP - GROUP, axis=1), 0.0)
+    after = jnp.where(lane < (GROUPS - 1) * GROUP, pltpu.roll(first, WIDE - GROUP, axis=1), 0.0)
     ref[0:size, :] = before.astype(BF16)
-    ref[(TILES + 1) * size : (TILES + 2) * size, :] = after.astype(BF16)
-
-
-def own_mask():
-    lane, _, col = lane_places(STRIP)
-    return ((col >= 0) & (col < OWN)).astype(F32)
+    ref[(BLOCKS + 1) * size : (BLOCKS + 2) * size, :] = after.astype(BF16)
 
 
 def total_of(x):
     return jnp.sum(jnp.sum(x, axis=0, keepdims=True), axis=1, keepdims=True)
 
 
+def joined(z, rows):
+    return (
+        z[rows : 2 * rows]
+        + pltpu.roll(z[:rows], 1, axis=1)
+        + pltpu.roll(z[2 * rows :], WIDE - 1, axis=1)
+    )
+
+
 def conv_and_stats(w, ref, size, out, stats):
-    mask = own_mask()
+    _, _, col = lane_places()
+    mine = (col >= 0) & (col < OWN)
 
     def one(k, acc):
         rows = ref[pl.ds(pl.multiple_of(k * size, size), 3 * size), :]
-        z = mm(w[...], rows)
-        y = z[HR : 2 * HR] + pltpu.roll(z[:HR], 1, axis=1) + pltpu.roll(z[2 * HR :], STRIP - 1, axis=1)
+        y = joined(mm(w[...], rows), HR)
         out[pl.ds(pl.multiple_of(k * HR, HR), HR), :] = y
         return acc + y
 
-    acc = lax.fori_loop(0, TILES, one, jnp.zeros((HR, STRIP), F32), unroll=4) * mask
+    acc = lax.fori_loop(0, BLOCKS, one, jnp.zeros((HR, WIDE), F32), unroll=UNROLL)
+    acc = jnp.where(mine, acc, 0.0)
     means = [total_of(acc[ROWS * o : ROWS * (o + 1)]) * (1.0 / COUNT) for o in range(HID)]
-    mean = jnp.concatenate([jnp.broadcast_to(m, (ROWS, STRIP)) for m in means], axis=0)
+    mean = jnp.concatenate([jnp.broadcast_to(m, (ROWS, WIDE)) for m in means], axis=0)
 
     def two(k, acc):
-        dev = (out[pl.ds(pl.multiple_of(k * HR, HR), HR), :] - mean) * mask
+        dev = out[pl.ds(pl.multiple_of(k * HR, HR), HR), :] - mean
         return acc + dev * dev
 
-    acc = lax.fori_loop(0, TILES, two, jnp.zeros((HR, STRIP), F32), unroll=4)
+    acc = lax.fori_loop(0, BLOCKS, two, jnp.zeros((HR, WIDE), F32), unroll=2)
+    acc = jnp.where(mine, acc, 0.0)
     lane = iota((1, STRIP), 1)
     row = jnp.zeros((1, STRIP), F32)
     for o in range(HID):
@@ -198,11 +221,11 @@
     means, scales = [], []
     for o in range(HID):
         spread = pick(center, HID + o) * (1.0 / COUNT) + pick(between, o) * (1.0 / DEVICES)
-        means.append(jnp.broadcast_to(pick(center, o), (ROWS, STRIP)))
-        scales.append(jnp.broadcast_to(lax.rsqrt(spread + norm_eps), (ROWS, STRIP)))
+        means.append(jnp.broadcast_to(pick(center, o), (ROWS, WIDE)))
+        scales.append(jnp.broadcast_to(lax.rsqrt(spread + norm_eps), (ROWS, WIDE)))
     mean = jnp.concatenate(means, axis=0)
     scale = jnp.concatenate(scales, axis=0)
-    _, _, col = lane_places(STRIP)
+    _, _, col = lane_places()
     col = col + (STRIP * pos[1] + OWN * pos[0])
     inside = (col >= 0) & (col < STRIP * pos[2])
 
@@ -212,100 +235,98 @@
         act[pl.ds(pl.multiple_of((k + 1) * HR, HR), HR), :] = y.astype(BF16)
         return carry
 
-    lax.fori_loop(0, TILES, one, 0, unroll=4)
-    wrap_tiles(act, HR)
+    lax.fori_loop(0, BLOCKS, one, 0, unroll=2)
+    wrap_blocks(act, HR)
 
 
 def window_features(depth, every, left, edge, wf, feats):
     lane = iota((1, STRIP), 1)
     start = (OWN * depth + STRIP - EDGE) & (STRIP - 1)
-    back = STRIP - start
     first = depth == 0
 
     def one(v, carry):
         own = every[v].astype(F32)
         before = left[v].astype(F32)
-        far = pltpu.roll(edge[...].astype(F32), (3 * STRIP - EDGE * v - jnp.where(first, EDGE, 0)) & (STRIP - 1), axis=1)
+        turn = (3 * STRIP - EDGE * v - jnp.where(first, EDGE, 0)) & (STRIP - 1)
+        far = pltpu.roll(edge[...].astype(F32), turn, axis=1)
         a = jnp.where(first, far, before)
         b = jnp.where(first, before, own)
         c = jnp.where(first, own, far)
-        x = jnp.concatenate(
-            [
-                pltpu.roll(jnp.where(lane >= start, a, b), back, axis=1),
-                pltpu.roll(jnp.where(lane >= start, b, c), back, axis=1),
-            ],
-            axis=1,
-        ).astype(BF16)
-        y = mm(wf[...], x)
-        f = (
-            y[CR : 2 * CR]
-            + pltpu.roll(y[:CR], 1, axis=1)
-            + pltpu.roll(y[2 * CR :], 2 * STRIP - 1, axis=1)
-        )
-        feats[v] = f.astype(BF16)
+        taps = []
+        for at in (start - 1, start, start + 1):
+            one_half = pltpu.roll(jnp.where(lane >= at, a, b), STRIP - at, axis=1)
+            two_half = pltpu.roll(jnp.where(lane >= at, b, c), STRIP - at, axis=1)
+            taps.append(jnp.concatenate([one_half, two_half], axis=1).astype(BF16))
+        feats[v] = mm(wf[...], jnp.concatenate(taps, axis=0)).astype(BF16)
         return carry
 
-    lax.fori_loop(0, VIEWS, one, 0)
+    lax.fori_loop(0, VIEWS, one, 0, unroll=8)
 
 
 def volume_kernel(pos, shifts, frame, every, left, edge, wf, w1, out, stats, feats, even, odd, vol):
     depth = pos[0]
     base = STRIP * pos[1] + OWN * depth
-    wide = 2 * STRIP
-    lane = iota((1, wide), 1)
+    lane, group, col = lane_places()
     window_features(depth, every, left, edge, wf, feats)
     zero_view = pltpu.roll(feats[0].astype(F32), BASE - (LEFT - HALO), axis=1)
     own_lanes = (lane >= BASE) & (lane < BASE + GROUP)
     for v in range(1, VIEWS):
         feats[v] = jnp.where(own_lanes, zero_view, feats[v].astype(F32)).astype(BF16)
 
-    _, group, col = lane_places(wide)
-    half = lane >= STRIP
     glob = base + col
     valid = (glob >= 0) & (glob < STRIP * pos[2])
-    places = iota((BASE, wide), 0)
-    below = jnp.where(iota((wide - BASE, wide), 0) == col + HALO, -1.0, 0.0)
-
-    def move(kk, moved):
-        tally = jnp.ones((1, wide), F32)
+    places = iota((BASE, WIDE), 0).astype(F32).astype(BF16)
+    below = jnp.where(iota((WIDE - BASE, WIDE), 0) == col + HALO, -1.0, 0.0).astype(BF16)
+    ones = jnp.ones((BASE, WIDE), BF16)
+    none = jnp.zeros((BASE, WIDE), BF16)
+
+    def move(k, v, moved):
+        shift = shifts[v, k]
+        for g in range(1, GROUPS):
+            shift = jnp.where(group == g, shifts[v, BLOCKS * g + k], shift)
+        source = glob - shift
+        inside = (source >= frame[v, 0]) & (source < frame[v, 1])
+        index = jnp.where(inside, col - shift + LEFT, -1)
+        index = jnp.broadcast_to(index.astype(F32), (16, WIDE)).astype(BF16)
+        index = jnp.concatenate([index] * (BASE // 16), axis=0)
+        hot = jnp.where(places == index, ones, none)
+        mask = inside.astype(F32)
+        packed = jnp.broadcast_to(mask, (16, WIDE)).astype(BF16)
+        packed = jnp.concatenate([packed] * ((WIDE - BASE) // 16), axis=0)
+        hot = jnp.concatenate([hot, below * packed], axis=0)
+        moved[v - 1] = mm(feats[v], hot)
+        return mask
+
+    def spread(k, r, moved, inverse):
+        total = squares = None
+        for v in range(VIEWS - 1):
+            p = moved[v, r : r + 16, :]
+            total = p if total is None else total + p
+            squares = p * p if squares is None else squares + p * p
+        average = total * inverse
+        value = jnp.where(valid, squares * inverse - average * average, 0.0)
+        row = pl.multiple_of((k + 1) * CR + r, 16)
+        vol[pl.ds(row, 16), :] = jnp.maximum(value, 0.0).astype(BF16)
+
+    def both(k, into, moved, inverse):
+        ahead = jnp.minimum(k + 1, BLOCKS - 1)
+        tally = jnp.ones((1, WIDE), F32)
+        chunks = CR // 16
         for v in range(1, VIEWS):
-            at = [[shifts[v, TILES * j + 2 * kk + s] for j in range(3)] for s in range(2)]
-            one, two = (
-                jnp.where(group == 0, t[0], jnp.where(group == 1, t[1], t[2])) for t in at
-            )
-            shift = jnp.where(half, two, one)
-            source = glob - shift
-            inside = (source >= frame[v, 0]) & (source < frame[v, 1])
-            index = jnp.where(inside, col - shift + LEFT, -1)
-            hot = jnp.where(places == index, 1.0, 0.0).astype(BF16)
-            mask = inside.astype(F32)
-            hot = jnp.concatenate([hot, (below * mask).astype(BF16)], axis=0)
-            moved[v - 1] = mm(feats[v], hot)
-            tally = tally + mask
+            tally = tally + move(ahead, v, into)
+            for r in range(chunks * (v - 1) // (VIEWS - 1), chunks * v // (VIEWS - 1)):
+                spread(k, 16 * r, moved, inverse)
         return 1.0 / tally
 
-    def spread(kk, moved, inverse):
-        for r in range(0, CR, 16):
-            total = squares = None
-            for v in range(VIEWS - 1):
-                p = moved[v, r : r + 16, :]
-                total = p if total is None else total + p
-                squares = p * p if squares is None else squares + p * p
-            average = total * inverse
-            value = jnp.where(valid, squares * inverse - average * average, 0.0)
-            value = jnp.maximum(value, 0.0).astype(BF16)
-            for s in range(2):
-                row = pl.multiple_of((2 * kk + s + 1) * CR + r, 16)
-                vol[pl.ds(row, 16), :] = value[:, s * STRIP : (s + 1) * STRIP]
+    tally = jnp.ones((1, WIDE), F32)
+    for v in range(1, VIEWS):
+        tally = tally + move(0, v, even)
 
     def step(t, inverse):
-        spread(2 * t, even, inverse)
-        later = move(2 * t + 1, odd)
-        spread(2 * t + 1, odd, later)
-        return move(jnp.minimum(2 * t + 2, TILES // 2 - 1), even)
-
-    lax.fori_loop(0, TILES // 4, step, move(0, even))
-    wrap_tiles(vol, CR)
+        return both(2 * t + 1, even, odd, both(2 * t, odd, even, inverse))
+
+    lax.fori_loop(0, BLOCKS // 2, step, 1.0 / tally)
+    wrap_blocks(vol, CR)
     conv_and_stats(w1, vol, CR, out, stats)
 
 
@@ -313,16 +334,16 @@
     return pl.pallas_call(
         volume_kernel,
         out_shape=(
-            jax.ShapeDtypeStruct((TILES * HR, STRIP), F32),
+            jax.ShapeDtypeStruct((BLOCKS * HR, WIDE), F32),
             jax.ShapeDtypeStruct((DEVICES, STRIP), F32),
         ),
         in_specs=[SMEM] * 3 + [VMEM] * 5,
         out_specs=(VMEM,) * 2,
         scratch_shapes=[
-            pltpu.VMEM((VIEWS, CR, 2 * STRIP), BF16),
-            pltpu.VMEM((VIEWS - 1, CR, 2 * STRIP), F32),
-            pltpu.VMEM((VIEWS - 1, CR, 2 * STRIP), F32),
-            pltpu.VMEM(((TILES + 2) * CR, STRIP), BF16),
+            pltpu.VMEM((VIEWS, CR, WIDE), BF16),
+            pltpu.VMEM((VIEWS - 1, CR, WIDE), F32),
+            pltpu.VMEM((VIEWS - 1, CR, WIDE), F32),
+            pltpu.VMEM(((BLOCKS + 2) * CR, WIDE), BF16),
         ],
         compiler_params=PARAMS,
         name="cost_volume",
@@ -338,12 +359,12 @@
     return pl.pallas_call(
         middle_kernel,
         out_shape=(
-            jax.ShapeDtypeStruct((TILES * HR, STRIP), F32),
+            jax.ShapeDtypeStruct((BLOCKS * HR, WIDE), F32),
             jax.ShapeDtypeStruct((DEVICES, STRIP), F32),
         ),
         in_specs=[SMEM] + [VMEM] * 3,
         out_specs=(VMEM,) * 2,
-        scratch_shapes=[pltpu.VMEM(((TILES + 2) * HR, STRIP), BF16)],
+        scratch_shapes=[pltpu.VMEM(((BLOCKS + 2) * HR, WIDE), BF16)],
         compiler_params=PARAMS,
         name="second_conv",
     )(pos, stats, values, w2)
@@ -353,31 +374,30 @@
     normalized(pos, stats_in, values, act)
 
     def one(k, peak):
-        z = mm(w3[...], act[pl.ds(pl.multiple_of(k * HR, HR), 3 * HR), :])
-        y = (
-            z[ROWS : 2 * ROWS]
-            + pltpu.roll(z[:ROWS], 1, axis=1)
-            + pltpu.roll(z[2 * ROWS :], STRIP - 1, axis=1)
-        )
+        y = joined(mm(w3[...], act[pl.ds(pl.multiple_of(k * HR, HR), 3 * HR), :]), ROWS)
         score[k] = y
         return jnp.maximum(peak, y)
 
-    peak = lax.fori_loop(0, TILES, one, jnp.full((ROWS, STRIP), -jnp.inf, F32), unroll=4)
-    _, group, _ = lane_places(STRIP)
+    peak = lax.fori_loop(0, BLOCKS, one, jnp.full((ROWS, WIDE), -jnp.inf, F32), unroll=UNROLL)
+    _, group, _ = lane_places()
 
     def two(k, sums):
         e = jnp.exp(score[k] - peak)
-        value = (TILES * group + k).astype(F32) / (DEPTHS - 1)
+        value = (BLOCKS * group + k).astype(F32) / (DEPTHS - 1)
         return sums[0] + e, sums[1] + e * value
 
-    zero = jnp.zeros((ROWS, STRIP), F32)
-    total, weighted = lax.fori_loop(0, TILES, two, (zero, zero), unroll=4)
+    zero = jnp.zeros((ROWS, WIDE), F32)
+    total, weighted = lax.fori_loop(0, BLOCKS, two, (zero, zero), unroll=4)
 
     def turned(x):
-        return [x] + [pltpu.roll(x, STRIP - j * GROUP, axis=1) for j in (1, 2)]
+        return [x[:, :STRIP]] + [
+            pltpu.roll(x, WIDE - g * GROUP, axis=1)[:, :STRIP] for g in range(1, GROUPS)
+        ]
 
     peaks, totals, weights = turned(peak), turned(total), turned(weighted)
-    top = jnp.maximum(jnp.maximum(peaks[0], peaks[1]), peaks[2])
+    top = peaks[0]
+    for p in peaks[1:]:
+        top = jnp.maximum(top, p)
     scales = [jnp.exp(p - top) for p in peaks]
     whole = sum(t * s for t, s in zip(totals, scales))
     mean = sum(t * s for t, s in zip(weights, scales)) / whole
@@ -394,8 +414,8 @@
         in_specs=[SMEM] + [VMEM] * 3,
         out_specs=VMEM,
         scratch_shapes=[
-            pltpu.VMEM(((TILES + 2) * HR, STRIP), BF16),
-            pltpu.VMEM((TILES, ROWS, STRIP), F32),
+            pltpu.VMEM(((BLOCKS + 2) * HR, WIDE), BF16),
+            pltpu.VMEM((BLOCKS, ROWS, WIDE), F32),
         ],
         compiler_params=PARAMS,
         name="final_estimate",
@@ -411,7 +431,7 @@
     pos = pos.astype(I32)
     own = raw_views.reshape(2, CR, STRIP)
     with jax.named_scope("views"):
-        parts = [own] + [lax.ppermute(own, "depth", [(i, i ^ k) for i in range(4)]) for k in (1, 2, 3)]
+        parts = [copied(own)] + [lax.ppermute(own, "depth", [(i, i ^ k) for i in range(4)]) for k in (1, 2, 3)]
         every, edge = all_views(pos, parts)
     with jax.named_scope("strips"):
         cols = lax.axis_size("col")

time: 101 us -> 90.4 us (0.90)
  Pallas kernels: 30.7 us -> 20.4 us
    pallas_call x3 -> x4, Pallas kernels: 26.6 us -> 18 us  [the longest x1 11.8 us: cost_and_conv(): pl.pallas_call(volume_kernel, out_shape=(jax.ShapeDtypeStruct((BLOCKS * H...]
    pallas_call x1, Pallas kernels: 3.27 us -> 1.65 us  [final_estimate(): pl.pallas_call(last_kernel, out_shape=jax.ShapeDtypeStruct((ROWS, STRIP),...]
  transfers between devices with their start and end apart: 8 -> 8, of which waited for: 5 -> 5; matrix products, arithmetic and copies ran while one was open for 0% -> 0% of each run, Pallas kernels for 4% -> 5%
where the time goes in v4:
time: 90.4 us; the launch traced here: 90.2 us
  blocking collectives  49.4 us (55%)
  Pallas kernels  20.4 us (23%)
  starting transfers between devices  10.6 us (12%)
  waiting for transfers between devices  7.71 us (9%)
  local copies, waits for them, and re-layouts  1.31 us (1%)
    all_to_all x2, blocking collectives, everyones(): return lax.all_to_all(stats, ('depth', 'col'), 0, 0, tiled=True)  49.4 us
    pallas_call x1, Pallas kernels, cost_and_conv(): pl.pallas_call(volume_kernel, out_shape=(jax.ShapeDtypeStruct((BLOCKS * H...  11.8 us
    ppermute x3, waiting for transfers between devices, local(): lax.ppermute(own, 'depth', [(i, i ^ k) for i in range(4)])  4.68 us
    ppermute x3, starting transfers between devices, local(): lax.ppermute(own, 'depth', [(i, i ^ k) for i in range(4)])  4.34 us
    ppermute x3, starting transfers between devices, local(): lax.ppermute(part, 'depth', [(i, i ^ k) for i in range(4)])  4.12 us
    pallas_call x1, Pallas kernels, make_weights(): pl.pallas_call(weights_kernel, out_shape=(jax.ShapeDtypeStruct((CR, 3 * C...  4.07 us
    ppermute x3, waiting for transfers between devices, local(): lax.ppermute(part, 'depth', [(i, i ^ k) for i in range(4)])  3.03 us
    pallas_call x1, Pallas kernels, second_conv(): pl.pallas_call(middle_kernel, out_shape=(jax.ShapeDtypeStruct((BLOCKS * H...  2.07 us
  transfers between devices with their start and end apart: 8, of which 5 were waited for; matrix products, arithmetic and copies ran while one was open for 0% of the time, Pallas kernels for 5%

profile of v4, /device:TPU:2, one launch (start us, length us, event | category | flops | bytes accessed | tf_op | source)
XLA Modules:
  0.0 90.2 jit_solution(6377081054328201162)
XLA Ops:
  0.0 1.5 %collective-permute-start.2 = (bf16[2,256,128]{2,1,0:T(8,128)(2,1)}, bf16[2,256,128]{2,1,0:T(8,128)(2,1)S(1)}, u32[]{:S(2)}, u32[]{:S(2)}) collective-permute-start(bf16[2,256,128]{2,1,0:T(8,128)(2,1)} %bitcast.16), channel_id=1, source_target_pairs={{0,192},{64,128},{128,64},{192,0},{1,193},{65,129},{129,65},{193,1... | collective-permute-start | bytes 393224 | tf_op jit(solution)/shard_map/views/ppermute | solution.py:434
  1.5 2.8 %collective-permute-start.1 = (bf16[2,256,128]{2,1,0:T(8,128)(2,1)}, bf16[2,256,128]{2,1,0:T(8,128)(2,1)S(1)}, u32[]{:S(2)}, u32[]{:S(2)}) collective-permute-start(bf16[2,256,128]{2,1,0:T(8,128)(2,1)} %bitcast.17), channel_id=1, source_target_pairs={{0,128},{64,192},{128,0},{192,64},{1,129},{65,193},{129,1},{193,65... | collective-permute-start | bytes 393224 | tf_op jit(solution)/shard_map/views/ppermute | solution.py:434
  4.3 0.0 collective-permute-start
  4.3 0.0 copy-start
  4.3 1.0 %copy-done = bf16[2,32,8,128]{3,2,1,0:T(8,128)(2,1)S(1)} copy-done((bf16[2,32,8,128]{3,2,1,0:T(8,128)(2,1)S(1)}, bf16[2,32,8,128]{3,2,1,0:T(8,128)(2,1)}, u32[]{:S(2)}) %copy-start) | copy-done | bytes 131096
  5.3 0.1 pad_add_fusion.pos
  5.4 1.4 %collective-permute-done.2.r3 = bf16[2,256,128]{2,1,0:T(8,128)(2,1)S(1)} collective-permute-done((bf16[2,256,128]{2,1,0:T(8,128)(2,1)}, bf16[2,256,128]{2,1,0:T(8,128)(2,1)S(1)}, u32[]{:S(2)}, u32[]{:S(2)}) %collective-permute-start.2) | collective-permute-done | bytes 131104 | tf_op jit(solution)/shard_map/views/ppermute | solution.py:434
  6.8 2.8 %collective-permute-done.1.r2 = bf16[2,256,128]{2,1,0:T(8,128)(2,1)S(1)} collective-permute-done((bf16[2,256,128]{2,1,0:T(8,128)(2,1)}, bf16[2,256,128]{2,1,0:T(8,128)(2,1)S(1)}, u32[]{:S(2)}, u32[]{:S(2)}) %collective-permute-start.1) | collective-permute-done | bytes 131104 | tf_op jit(solution)/shard_map/views/ppermute | solution.py:434
  9.6 0.5 collective-permute-done.r1
  10.1 0.0 copy-start.6
  10.1 0.0 copy-start.5
  10.1 0.0 copy-start.4
  10.1 0.0 copy-start.3
  10.1 0.8 all_views.1
  10.9 0.0 copy-start.2
  10.9 1.5 %collective-permute-start.3 = (bf16[8,256,128]{2,1,0:T(8,128)(2,1)S(1)}, bf16[8,256,128]{2,1,0:T(8,128)(2,1)S(1)}, u32[]{:S(2)}, u32[]{:S(2)}) collective-permute-start(bf16[8,256,128]{2,1,0:T(8,128)(2,1)S(1)} %get-tuple-element.21.every), channel_id=1, source_target_pairs={{0,1},{1,2},{2,3},{3,4},{4,5},{5,6},{6,7},{7,8},{8,9},{9,10},{10,1... | collective-permute-start | bytes 1572872 | tf_op jit(solution)/shard_map/strips/ppermute | solution.py:439
  12.4 0.0 copy-done.6
  12.4 0.1 copy.16.frame
  12.5 0.0 copy-done.5
  12.5 0.1 copy.15.lw
  12.6 0.0 copy-done.4
  12.6 0.1 copy.14.mw
  12.7 0.7 collective-permute-start.4
  13.4 0.0 copy-done.3
  13.4 0.0 copy-done.2
  13.4 0.0 copy-start.1
  13.4 4.1 %banded_weights.1 = (bf16[256,768]{1,0:T(8,128)(2,1)S(1)}, bf16[192,768]{1,0:T(8,128)(2,1)S(1)}, bf16[192,192]{1,0:T(8,128)(2,1)S(1)}, bf16[24,192]{1,0:T(8,128)(2,1)S(1)}) custom-call(bf16[9,32,32]{2,1,0:T(8,128)(2,1)S(1)} %copy-done.2, bf16[27,8,32]{2,1,0:T(8,128)(2,1)S(1)} %copy-done.3, bf16[27,8,8]{2,1,0:T(8,128)(2,1)S(1)} %copy.14.mw, ...), custom_call_target="tpu_custom_call" | custom-call | flops 2000000000 | bytes 1000000 | tf_op jit(solution)/shard_map/banded_weights/pallas_call | solution.py:95
  17.5 0.0 collective-permute-done.4.edge
  17.5 0.0 collective-permute-done.3.left
  17.5 0.0 copy-done.1
  17.5 11.8 %cost_volume.1 = (f32[1024,256]{1,0:T(8,128)S(1)}, f32[256,128]{1,0:T(8,128)S(1)}) custom-call(s32[3]{0:T(128)S(1)} %pad_add_fusion.pos, s32[8,96]{1,0:T(8,128)S(1)} %copy-done.1, s32[8,2]{1,0:T(8,128)S(1)} %copy.16.frame, bf16[8,256,128]{2,1,0:T(8,128)(2,1)S(1)} %get-tuple-element.21.every, bf16[8,256,128]{2,1,0:T(8,128)(2,1)S(1)} %collective-permute-done.3.left, ...), custom_call_target="tpu_custom_call" | custom-call | tf_op jit(solution)/shard_map/cost_volume/pallas_call | solution.py:334
  29.3 31.1 %all_to_all.22 = f32[256,1,128]{2,1,0:T(1,128)S(1)} all-to-all(f32[256,1,128]{2,1,0:T(1,128)S(1)} %bitcast.20), channel_id=1, replica_groups=mesh['depth'=4,'col'=64] {'depth','col'}, dimensions={0} | all-to-all | bytes 262144 | tf_op jit(solution)/shard_map/all_to_all | solution.py:426
  60.4 2.1 %second_conv.1 = (f32[1024,256]{1,0:T(8,128)S(1)}, f32[256,128]{1,0:T(8,128)S(1)}) custom-call(s32[3]{0:T(128)S(1)} %pad_add_fusion.pos, f32[256,128]{1,0:T(8,128)S(1)} %bitcast.14, f32[1024,256]{1,0:T(8,128)S(1)} %get-tuple-element.30.values, bf16[192,192]{1,0:T(8,128)(2,1)S(1)} %get-tuple-element.31.w2), custom_call_target="tpu_custom_call" | custom-call | tf_op jit(solution)/shard_map/second_conv/pallas_call | solution.py:359
  62.5 18.3 %all_to_all.23 = f32[256,1,128]{2,1,0:T(1,128)S(1)} all-to-all(f32[256,1,128]{2,1,0:T(1,128)S(1)} %bitcast.21), channel_id=1, replica_groups=mesh['depth'=4,'col'=64] {'depth','col'}, dimensions={0} | all-to-all | bytes 262144 | tf_op jit(solution)/shard_map/all_to_all | solution.py:426
  80.8 1.6 %final_estimate.1 = f32[8,128]{1,0:T(8,128)S(1)} custom-call(s32[3]{0:T(128)S(1)} %pad_add_fusion.pos, f32[256,128]{1,0:T(8,128)S(1)} %bitcast.15, f32[1024,256]{1,0:T(8,128)S(1)} %get-tuple-element.33.values, bf16[24,192]{1,0:T(8,128)(2,1)S(1)} %get-tuple-element.34.w3), custom_call_target="tpu_custom_call" | custom-call | tf_op jit(solution)/shard_map/final_estimate/pallas_call | solution.py:411
  82.4 0.4 collective-permute-start.7
  82.8 3.1 %collective-permute-start.6 = (f32[8,128]{1,0:T(8,128)S(1)}, f32[8,128]{1,0:T(8,128)S(1)}, u32[]{:S(2)}, u32[]{:S(2)}) collective-permute-start(f32[8,128]{1,0:T(8,128)S(1)} %final_estimate.1), channel_id=1, source_target_pairs={{0,128},{64,192},{128,0},{192,64},{1,129},{65,193},{129,1},{193,65... | collective-permute-start | bytes 12296 | tf_op jit(solution)/shard_map/columns/ppermute | solution.py:449
  86.0 0.6 collective-permute-start.5
  86.6 0.0 collective-permute-done.7
  86.6 1.4 %collective-permute-done.6 = f32[8,128]{1,0:T(8,128)S(1)} collective-permute-done((f32[8,128]{1,0:T(8,128)S(1)}, f32[8,128]{1,0:T(8,128)S(1)}, u32[]{:S(2)}, u32[]{:S(2)}) %collective-permute-start.6) | collective-permute-done | bytes 4128 | tf_op jit(solution)/shard_map/columns/ppermute | solution.py:449
  88.0 1.6 %collective-permute-done.5 = f32[8,128]{1,0:T(8,128)S(1)} collective-permute-done((f32[8,128]{1,0:T(8,128)S(1)}, f32[8,128]{1,0:T(8,128)S(1)}, u32[]{:S(2)}, u32[]{:S(2)}) %collective-permute-start.5) | collective-permute-done | bytes 4128 | tf_op jit(solution)/shard_map/columns/ppermute | solution.py:449
  89.6 0.6 add_add_fusion
  (2 shorter events, 0.0 us)
Async XLA Ops:
  0.0 6.8 %collective-permute-start.2 = (bf16[2,256,128]{2,1,0:T(8,128)(2,1)}, bf16[2,256,128]{2,1,0:T(8,128)(2,1)S(1)}, u32[]{:S(2)}, u32[]{:S(2)}) collective-permute-start(bf16[2,256,128]{2,1,0:T(8,128)(2,1)} %bitcast.16), channel_id=1, source_target_pairs={{0,192},{64,128},{128,64},{192,0},{1,193},{65,129},{129,65},{193,1... | collective-permute-start | bytes 393224 | tf_op jit(solution)/shard_map/views/ppermute | solution.py:434
  1.5 8.1 %collective-permute-start.1 = (bf16[2,256,128]{2,1,0:T(8,128)(2,1)}, bf16[2,256,128]{2,1,0:T(8,128)(2,1)S(1)}, u32[]{:S(2)}, u32[]{:S(2)}) collective-permute-start(bf16[2,256,128]{2,1,0:T(8,128)(2,1)} %bitcast.17), channel_id=1, source_target_pairs={{0,128},{64,192},{128,0},{192,64},{1,129},{65,193},{129,1},{193,65... | collective-permute-start | bytes 393224 | tf_op jit(solution)/shard_map/views/ppermute | solution.py:434
  4.3 5.7 %collective-permute-start = (bf16[2,256,128]{2,1,0:T(8,128)(2,1)}, bf16[2,256,128]{2,1,0:T(8,128)(2,1)S(1)}, u32[]{:S(2)}, u32[]{:S(2)}) collective-permute-start(bf16[2,256,128]{2,1,0:T(8,128)(2,1)} %bitcast.18), channel_id=1, source_target_pairs={{0,64},{64,0},{128,192},{192,128},{1,65},{65,1},{129,193},{193,129... | collective-permute-start | bytes 393224 | tf_op jit(solution)/shard_map/views/ppermute | solution.py:434
  4.3 1.0 %copy-start = (bf16[2,32,8,128]{3,2,1,0:T(8,128)(2,1)S(1)}, bf16[2,32,8,128]{3,2,1,0:T(8,128)(2,1)}, u32[]{:S(2)}) copy-start(bf16[2,32,8,128]{3,2,1,0:T(8,128)(2,1)} %param.7) | copy-start | bytes 393220
  10.1 2.3 %copy-start.6 = (s32[8,2]{0,1:T(2,128)S(1)}, s32[8,2]{0,1:T(2,128)}, u32[]{:S(2)}) copy-start(s32[8,2]{0,1:T(2,128)} %param.10) | copy-start | bytes 196
  10.1 2.4 %copy-start.5 = (bf16[27,8]{0,1:T(8,128)(2,1)S(1)}, bf16[27,8]{0,1:T(8,128)(2,1)}, u32[]{:S(2)}) copy-start(bf16[27,8]{0,1:T(8,128)(2,1)} %param.13) | copy-start | bytes 1300
  10.1 2.5 %copy-start.4 = (bf16[27,8,8]{0,2,1:T(8,128)(2,1)S(1)}, bf16[27,8,8]{0,2,1:T(8,128)(2,1)}, u32[]{:S(2)}) copy-start(bf16[27,8,8]{0,2,1:T(8,128)(2,1)} %param.12) | copy-start | bytes 10372
  10.1 3.3 %copy-start.3 = (bf16[27,8,32]{2,1,0:T(8,128)(2,1)S(1)}, bf16[27,8,32]{2,1,0:T(8,128)(2,1)}, u32[]{:S(2)}) copy-start(bf16[27,8,32]{2,1,0:T(8,128)(2,1)} %cw) | copy-start | bytes 41476
  10.9 2.5 %copy-start.2 = (bf16[9,32,32]{2,1,0:T(8,128)(2,1)S(1)}, bf16[9,32,32]{2,1,0:T(8,128)(2,1)}, u32[]{:S(2)}) copy-start(bf16[9,32,32]{2,1,0:T(8,128)(2,1)} %fw) | copy-start | bytes 55300
  10.9 6.6 %collective-permute-start.3 = (bf16[8,256,128]{2,1,0:T(8,128)(2,1)S(1)}, bf16[8,256,128]{2,1,0:T(8,128)(2,1)S(1)}, u32[]{:S(2)}, u32[]{:S(2)}) collective-permute-start(bf16[8,256,128]{2,1,0:T(8,128)(2,1)S(1)} %get-tuple-element.21.every), channel_id=1, source_target_pairs={{0,1},{1,2},{2,3},{3,4},{4,5},{5,6},{6,7},{7,8},{8,9},{9,10},{10,1... | collective-permute-start | bytes 1572872 | tf_op jit(solution)/shard_map/strips/ppermute | solution.py:439
  12.7 4.8 %collective-permute-start.4 = (bf16[256,128]{1,0:T(8,128)(2,1)S(1)}, bf16[256,128]{1,0:T(8,128)(2,1)S(1)}, u32[]{:S(2)}, u32[]{:S(2)}) collective-permute-start(bf16[256,128]{1,0:T(8,128)(2,1)S(1)} %get-tuple-element.22), channel_id=1, source_target_pairs={{0,2},{1,3},{2,4},{3,5},{4,6},{5,7},{6,8},{7,9},{8,10},{9,11},{10,... | collective-permute-start | bytes 196616 | tf_op jit(solution)/shard_map/strips/ppermute | solution.py:440
  13.4 4.1 %copy-start.1 = (s32[8,96]{1,0:T(8,128)S(1)}, s32[8,96]{1,0:T(8,128)}, u32[]{:S(2)}) copy-start(s32[8,96]{1,0:T(8,128)} %shifts.1) | copy-start | bytes 9220
  82.4 4.1 %collective-permute-start.7 = (f32[8,128]{1,0:T(8,128)S(1)}, f32[8,128]{1,0:T(8,128)S(1)}, u32[]{:S(2)}, u32[]{:S(2)}) collective-permute-start(f32[8,128]{1,0:T(8,128)S(1)} %final_estimate.1), channel_id=1, source_target_pairs={{0,192},{64,128},{128,64},{192,0},{1,193},{65,129},{129,65},{193,1... | collective-permute-start | bytes 12296 | tf_op jit(solution)/shard_map/columns/ppermute | solution.py:449
  82.8 5.1 %collective-permute-start.6 = (f32[8,128]{1,0:T(8,128)S(1)}, f32[8,128]{1,0:T(8,128)S(1)}, u32[]{:S(2)}, u32[]{:S(2)}) collective-permute-start(f32[8,128]{1,0:T(8,128)S(1)} %final_estimate.1), channel_id=1, source_target_pairs={{0,128},{64,192},{128,0},{192,64},{1,129},{65,193},{129,1},{193,65... | collective-permute-start | bytes 12296 | tf_op jit(solution)/shard_map/columns/ppermute | solution.py:449
  86.0 3.6 %collective-permute-start.5 = (f32[8,128]{1,0:T(8,128)S(1)}, f32[8,128]{1,0:T(8,128)S(1)}, u32[]{:S(2)}, u32[]{:S(2)}) collective-permute-start(f32[8,128]{1,0:T(8,128)S(1)} %final_estimate.1), channel_id=1, source_target_pairs={{0,64},{64,0},{128,192},{192,128},{1,65},{65,1},{129,193},{193,129... | collective-permute-start | bytes 12296 | tf_op jit(solution)/shard_map/columns/ppermute | solution.py:449

commit v5 on v4

--- a/solution.py
+++ b/solution.py
@@ -53,14 +53,15 @@
     return (iota((count, 8 * count), 0) == (iota((count, 8 * count), 1) >> 3)).astype(F32).astype(BF16)
 
 
-def banded(taps, left, right):
+def bands(rows, cols):
+    off = (iota((rows, cols), 1) & 7) - (iota((rows, cols), 0) & 7)
+    return [off == b - 1 for b in range(3)]
+
+
+def banded(places, parts):
     total = None
-    for b, w in enumerate(taps):
-        t = w if left is None else mm(left, w).astype(BF16)
-        u = mm(t, right)
-        rows, cols = u.shape
-        band = ((iota((rows, cols), 1) & 7) - (iota((rows, cols), 0) & 7)) == (b - 1)
-        u = jnp.where(band, u, 0.0)
+    for at, u in zip(places, parts):
+        u = jnp.where(at, u, 0.0)
         total = u if total is None else total + u
     return total
 
@@ -68,27 +69,32 @@
 def weights_kernel(fw, cw, mw, lw, wf, w1, w2, w3):
     ro32, ro8 = spread_rows(CHAN), spread_rows(HID)
     ci32, ci8 = spread_cols(CHAN), spread_cols(HID)
+    feat, cost, mid, last = mm(fw[...], ci32), mm(cw[...], ci32), mm(mw[...], ci8), mm(lw[...], ci8)
+
+    def rows_of(left, wide, tap, count):
+        return mm(left, wide[count * tap : count * (tap + 1)].astype(BF16))
+
+    places = bands(CR, CR)
     for b in range(3):
-        wf[:, b * CR : (b + 1) * CR] = banded([fw[3 * a + b] for a in range(3)], ro32, ci32).astype(BF16)
+        parts = [rows_of(ro32, feat, 3 * a + b, CHAN) for a in range(3)]
+        wf[:, b * CR : (b + 1) * CR] = banded(places, parts).astype(BF16)
+    places = bands(HR, CR)
     for a in range(3):
         for e in range(3):
-            taps = [9 * a + 3 * b + e for b in range(3)]
-            w1[e * HR : (e + 1) * HR, a * CR : (a + 1) * CR] = banded(
-                [cw[t] for t in taps], ro8, ci32
-            ).astype(BF16)
-    second, last = [], []
+            parts = [rows_of(ro8, cost, 9 * a + 3 * b + e, HID) for b in range(3)]
+            w1[e * HR : (e + 1) * HR, a * CR : (a + 1) * CR] = banded(places, parts).astype(BF16)
+    places, few = bands(HR, HR), bands(ROWS, HR)
+    second, third = [], []
     for e in range(3):
         row2, row3 = [], []
         for a in range(3):
             taps = [9 * a + 3 * b + e for b in range(3)]
-            row2.append(banded([mw[t] for t in taps], ro8, ci8))
-            row3.append(
-                banded([jnp.broadcast_to(lw[t], (ROWS, HID)).astype(BF16) for t in taps], None, ci8)
-            )
+            row2.append(banded(places, [rows_of(ro8, mid, t, HID) for t in taps]))
+            row3.append(banded(few, [jnp.broadcast_to(last[t : t + 1], (ROWS, HR)) for t in taps]))
         second.append(jnp.concatenate(row2, axis=1))
-        last.append(jnp.concatenate(row3, axis=1))
+        third.append(jnp.concatenate(row3, axis=1))
     w2[...] = jnp.concatenate(second, axis=0).astype(BF16)
-    w3[...] = jnp.concatenate(last, axis=0).astype(BF16)
+    w3[...] = jnp.concatenate(third, axis=0).astype(BF16)
 
 
 def make_weights(feat_weight, cost_weight, mid_weight, final_weight):
@@ -105,7 +111,12 @@
         compiler_params=PARAMS,
         cost_estimate=pl.CostEstimate(flops=2_000_000_000, bytes_accessed=1_000_000, transcendentals=0),
         name="banded_weights",
-    )(feat_weight, cost_weight, mid_weight, final_weight.astype(F32).reshape(27, 1, HID))
+    )(
+        feat_weight.reshape(9 * CHAN, CHAN),
+        cost_weight.reshape(27 * HID, CHAN),
+        mid_weight.reshape(27 * HID, HID),
+        final_weight,
+    )
 
 
 def views_kernel(pos, r0, r1, r2, r3, every, edge):
@@ -179,15 +190,17 @@
     )
 
 
-def conv_and_stats(w, ref, size, out, stats):
+def conv_block(w, ref, size, out, k):
+    rows = ref[k * size : (k + 3) * size, :]
+    out[k * HR : (k + 1) * HR, :] = joined(mm(w[...], rows), HR)
+
+
+def channel_stats(out, stats):
     _, _, col = lane_places()
     mine = (col >= 0) & (col < OWN)
 
     def one(k, acc):
-        rows = ref[pl.ds(pl.multiple_of(k * size, size), 3 * size), :]
-        y = joined(mm(w[...], rows), HR)
-        out[pl.ds(pl.multiple_of(k * HR, HR), HR), :] = y
-        return acc + y
+        return acc + out[pl.ds(pl.multiple_of(k * HR, HR), HR), :]
 
     acc = lax.fori_loop(0, BLOCKS, one, jnp.zeros((HR, WIDE), F32), unroll=UNROLL)
     acc = jnp.where(mine, acc, 0.0)
@@ -198,7 +211,7 @@
         dev = out[pl.ds(pl.multiple_of(k * HR, HR), HR), :] - mean
         return acc + dev * dev
 
-    acc = lax.fori_loop(0, BLOCKS, two, jnp.zeros((HR, WIDE), F32), unroll=2)
+    acc = lax.fori_loop(0, BLOCKS, two, jnp.zeros((HR, WIDE), F32), unroll=UNROLL)
     acc = jnp.where(mine, acc, 0.0)
     lane = iota((1, STRIP), 1)
     row = jnp.zeros((1, STRIP), F32)
@@ -227,15 +240,15 @@
     scale = jnp.concatenate(scales, axis=0)
     _, _, col = lane_places()
     col = col + (STRIP * pos[1] + OWN * pos[0])
-    inside = (col >= 0) & (col < STRIP * pos[2])
+    scale = jnp.where((col >= 0) & (col < STRIP * pos[2]), scale, 0.0)
 
     def one(k, carry):
         x = values[pl.ds(pl.multiple_of(k * HR, HR), HR), :]
-        y = jnp.where(inside, jnp.maximum((x - mean) * scale, 0.0), 0.0)
+        y = jnp.maximum((x - mean) * scale, 0.0)
         act[pl.ds(pl.multiple_of((k + 1) * HR, HR), HR), :] = y.astype(BF16)
         return carry
 
-    lax.fori_loop(0, BLOCKS, one, 0, unroll=2)
+    lax.fori_loop(0, BLOCKS, one, 0, unroll=UNROLL)
     wrap_blocks(act, HR)
 
 
@@ -304,30 +317,29 @@
             total = p if total is None else total + p
             squares = p * p if squares is None else squares + p * p
         average = total * inverse
-        value = jnp.where(valid, squares * inverse - average * average, 0.0)
-        row = pl.multiple_of((k + 1) * CR + r, 16)
-        vol[pl.ds(row, 16), :] = jnp.maximum(value, 0.0).astype(BF16)
-
-    def both(k, into, moved, inverse):
-        ahead = jnp.minimum(k + 1, BLOCKS - 1)
+        value = squares * inverse - average * average
+        row = (k + 1) * CR + r
+        vol[row : row + 16, :] = jnp.maximum(value, 0.0).astype(BF16)
+
+    def gathered(k, moved):
         tally = jnp.ones((1, WIDE), F32)
-        chunks = CR // 16
         for v in range(1, VIEWS):
-            tally = tally + move(ahead, v, into)
-            for r in range(chunks * (v - 1) // (VIEWS - 1), chunks * v // (VIEWS - 1)):
-                spread(k, 16 * r, moved, inverse)
-        return 1.0 / tally
-
-    tally = jnp.ones((1, WIDE), F32)
-    for v in range(1, VIEWS):
-        tally = tally + move(0, v, even)
-
-    def step(t, inverse):
-        return both(2 * t + 1, even, odd, both(2 * t, odd, even, inverse))
-
-    lax.fori_loop(0, BLOCKS // 2, step, 1.0 / tally)
+            tally = tally + move(k, v, moved)
+        return jnp.where(valid, 1.0 / tally, 0.0)
+
+    inverse = gathered(0, even)
+    for k in range(BLOCKS):
+        here, there = (even, odd) if k % 2 == 0 else (odd, even)
+        later = gathered(k + 1, there) if k + 1 < BLOCKS else None
+        if k >= 3:
+            conv_block(w1, vol, CR, out, k - 2)
+        for r in range(CR // 16):
+            spread(k, 16 * r, here, inverse)
+        inverse = later
     wrap_blocks(vol, CR)
-    conv_and_stats(w1, vol, CR, out, stats)
+    for k in (0, BLOCKS - 2, BLOCKS - 1):
+        conv_block(w1, vol, CR, out, k)
+    channel_stats(out, stats)
 
 
 def cost_and_conv(pos, shifts, frame, every, left, edge, wf, w1):
@@ -352,7 +364,9 @@
 
 def middle_kernel(pos, stats_in, values, w2, out, stats, act):
     normalized(pos, stats_in, values, act)
-    conv_and_stats(w2, act, HR, out, stats)
+    for k in range(BLOCKS):
+        conv_block(w2, act, HR, out, k)
+    channel_stats(out, stats)
 
 
 def second_conv(pos, stats, values, w2):
@@ -387,7 +401,7 @@
         return sums[0] + e, sums[1] + e * value
 
     zero = jnp.zeros((ROWS, WIDE), F32)
-    total, weighted = lax.fori_loop(0, BLOCKS, two, (zero, zero), unroll=4)
+    total, weighted = lax.fori_loop(0, BLOCKS, two, (zero, zero), unroll=UNROLL)
 
     def turned(x):
         return [x[:, :STRIP]] + [
@@ -431,17 +445,15 @@
     pos = pos.astype(I32)
     own = raw_views.reshape(2, CR, STRIP)
     with jax.named_scope("views"):
+        wf, w1, w2, w3 = make_weights(feat_weight, cost_weight, mid_weight, final_weight)
         parts = [copied(own)] + [lax.ppermute(own, "depth", [(i, i ^ k) for i in range(4)]) for k in (1, 2, 3)]
-        every, edge = all_views(pos, parts)
+        wf, turned = lax.optimization_barrier((wf, pos))
+        every, edge = all_views(turned, parts)
     with jax.named_scope("strips"):
         cols = lax.axis_size("col")
         far = [(i, i + 2) for i in range(cols - 2)] + [(3 * cols + i, 3 * cols + i - 1) for i in range(1, cols)]
         left = lax.ppermute(every, "col", [(i, i + 1) for i in range(cols - 1)])
         edge = lax.ppermute(edge, ("depth", "col"), far)
-    *weights, every = lax.optimization_barrier(
-        (feat_weight, cost_weight, mid_weight, final_weight, every)
-    )
-    wf, w1, w2, w3 = make_weights(*weights)
     first, stats = cost_and_conv(pos, shifts, frame_range, every, left, edge, wf, w1)
     second, stats = second_conv(pos, everyones(stats), first, w2)
     part = final_estimate(pos, everyones(stats), second, w3)

time: 90.4 us -> 86.9 us (0.961)
  Pallas kernels: 20.4 us -> 14.1 us
  blocking collectives: 49.4 us -> 52.9 us
  waiting for transfers between devices: 7.71 us -> 5.92 us
  local copies, waits for them, and re-layouts: 1.31 us -> 2.54 us
    all_to_all x2, blocking collectives: 49.4 us -> 52.9 us  [everyones(): return lax.all_to_all(stats, ('depth', 'col'), 0, 0, tiled=True)]
    pallas_call x1, Pallas kernels: 4.07 us -> 1 us  [make_weights(): pl.pallas_call(weights_kernel, out_shape=(jax.ShapeDtypeStruct((CR, 3 * C...]
    pallas_call x1, Pallas kernels: 11.8 us -> 9.05 us  [cost_and_conv(): pl.pallas_call(volume_kernel, out_shape=(jax.ShapeDtypeStruct((BLOCKS * H...]
    ppermute x3, waiting for transfers between devices: 4.68 us -> 2.18 us  [local(): lax.ppermute(own, 'depth', [(i, i ^ k) for i in range(4)])]
    unnamed x15 -> x13, local copies, waits for them, and re-layouts: 1.08 us -> 2.54 us
  transfers between devices with their start and end apart: 8 -> 8, of which waited for: 5 -> 5; matrix products, arithmetic and copies ran while one was open for 0% -> 2% of each run, Pallas kernels for 5% -> 1%
where the time goes in v5:
time: 86.9 us; the launch traced here: 86.6 us
  blocking collectives  52.9 us (61%)
  Pallas kernels  14.1 us (16%)
  starting transfers between devices  10.4 us (12%)
  waiting for transfers between devices  5.92 us (7%)
  local copies, waits for them, and re-layouts  2.54 us (3%)
    all_to_all x2, blocking collectives, everyones(): return lax.all_to_all(stats, ('depth', 'col'), 0, 0, tiled=True)  52.9 us
    pallas_call x1, Pallas kernels, cost_and_conv(): pl.pallas_call(volume_kernel, out_shape=(jax.ShapeDtypeStruct((BLOCKS * H...  9.05 us
    ppermute x3, starting transfers between devices, local(): lax.ppermute(own, 'depth', [(i, i ^ k) for i in range(4)])  4.34 us
    ppermute x3, starting transfers between devices, local(): lax.ppermute(part, 'depth', [(i, i ^ k) for i in range(4)])  4.12 us
    ppermute x3, waiting for transfers between devices, local(): lax.ppermute(part, 'depth', [(i, i ^ k) for i in range(4)])  3.03 us
    unnamed x13, local copies, waits for them, and re-layouts  2.54 us
    ppermute x3, waiting for transfers between devices, local(): lax.ppermute(own, 'depth', [(i, i ^ k) for i in range(4)])  2.18 us
    pallas_call x1, Pallas kernels, second_conv(): pl.pallas_call(middle_kernel, out_shape=(jax.ShapeDtypeStruct((BLOCKS * H...  1.84 us
  transfers between devices with their start and end apart: 8, of which 5 were waited for; matrix products, arithmetic and copies ran while one was open for 2% of the time, Pallas kernels for 1%

profile of v5, /device:TPU:2, one launch (start us, length us, event | category | flops | bytes accessed | tf_op | source)
XLA Modules:
  0.0 86.6 jit_solution(2936590703677671500)
XLA Ops:
  0.0 0.0 copy-start.2
  0.0 1.5 %collective-permute-start.2 = (bf16[2,256,128]{2,1,0:T(8,128)(2,1)}, bf16[2,256,128]{2,1,0:T(8,128)(2,1)S(1)}, u32[]{:S(2)}, u32[]{:S(2)}) collective-permute-start(bf16[2,256,128]{2,1,0:T(8,128)(2,1)} %bitcast.16), channel_id=1, source_target_pairs={{0,192},{64,128},{128,64},{192,0},{1,193},{65,129},{129,65},{193,1... | collective-permute-start | bytes 393224 | tf_op jit(solution)/shard_map/views/ppermute | solution.py:449
  1.5 2.8 %collective-permute-start.1 = (bf16[2,256,128]{2,1,0:T(8,128)(2,1)}, bf16[2,256,128]{2,1,0:T(8,128)(2,1)S(1)}, u32[]{:S(2)}, u32[]{:S(2)}) collective-permute-start(bf16[2,256,128]{2,1,0:T(8,128)(2,1)} %bitcast.17), channel_id=1, source_target_pairs={{0,128},{64,192},{128,0},{192,64},{1,129},{65,193},{129,1},{193,65... | collective-permute-start | bytes 393224 | tf_op jit(solution)/shard_map/views/ppermute | solution.py:449
  4.3 0.0 collective-permute-start
  4.3 0.8 copy.12.lw
  5.1 0.9 copy.11
  6.0 0.0 copy-done.2
  6.0 0.0 copy-start.3
  6.0 0.8 copy-done.3
  6.8 0.0 copy-start
  6.8 1.0 %banded_weights.1 = (bf16[256,768]{1,0:T(8,128)(2,1)S(1)}, bf16[192,768]{1,0:T(8,128)(2,1)S(1)}, bf16[192,192]{1,0:T(8,128)(2,1)S(1)}, bf16[24,192]{1,0:T(8,128)(2,1)S(1)}) custom-call(bf16[288,32]{1,0:T(8,128)(2,1)S(1)} %bitcast.23, bf16[216,32]{1,0:T(8,128)(2,1)S(1)} %bitcast.24, bf16[216,8]{1,0:T(8,128)(2,1)S(1)} %bitcast.22, bf16[27,8]{1,0:T(8,128)(2,1)S(1)} %copy.12.lw), custom_call_target="tpu_custom_call" | custom-call | flops 2000000000 | bytes 1000000 | tf_op jit(solution)/shard_map/views/banded_weights/pallas_call | solution.py:101
  7.8 0.0 copy-done
  7.8 0.1 pad_add_fusion.pos
  7.9 0.0 collective-permute-done.2.r3
  7.9 1.7 %collective-permute-done.1.r2 = bf16[2,256,128]{2,1,0:T(8,128)(2,1)S(1)} collective-permute-done((bf16[2,256,128]{2,1,0:T(8,128)(2,1)}, bf16[2,256,128]{2,1,0:T(8,128)(2,1)S(1)}, u32[]{:S(2)}, u32[]{:S(2)}) %collective-permute-start.1) | collective-permute-done | bytes 131104 | tf_op jit(solution)/shard_map/views/ppermute | solution.py:449
  9.6 0.5 collective-permute-done.r1
  10.1 0.8 all_views.1
  10.9 0.0 copy-start.4
  10.9 0.0 copy-start.1
  10.9 1.3 %collective-permute-start.3 = (bf16[8,256,128]{2,1,0:T(8,128)(2,1)S(1)}, bf16[8,256,128]{2,1,0:T(8,128)(2,1)S(1)}, u32[]{:S(2)}, u32[]{:S(2)}) collective-permute-start(bf16[8,256,128]{2,1,0:T(8,128)(2,1)S(1)} %get-tuple-element.19.every), channel_id=1, source_target_pairs={{0,1},{1,2},{2,3},{3,4},{4,5},{5,6},{6,7},{7,8},{8,9},{9,10},{10,1... | collective-permute-start | bytes 1572872 | tf_op jit(solution)/shard_map/strips/ppermute | solution.py:455
  12.2 0.7 collective-permute-start.4
  12.9 0.0 copy-done.4
  12.9 0.1 copy.13.frame
  13.0 0.0 collective-permute-done.4.edge
  13.0 0.7 collective-permute-done.3.left
  13.7 0.0 copy-done.1
  13.7 9.0 %cost_volume.1 = (f32[1024,256]{1,0:T(8,128)S(1)}, f32[256,128]{1,0:T(8,128)S(1)}) custom-call(s32[3]{0:T(128)S(1)} %pad_add_fusion.pos, s32[8,96]{1,0:T(8,128)S(1)} %copy-done.1, s32[8,2]{1,0:T(8,128)S(1)} %copy.13.frame, bf16[8,256,128]{2,1,0:T(8,128)(2,1)S(1)} %get-tuple-element.19.every, bf16[8,256,128]{2,1,0:T(8,128)(2,1)S(1)} %collective-permute-done.3.left, ...), custom_call_target="tpu_custom_call" | custom-call | tf_op jit(solution)/shard_map/cost_volume/pallas_call | solution.py:346
  22.8 34.7 %all_to_all.22 = f32[256,1,128]{2,1,0:T(1,128)S(1)} all-to-all(f32[256,1,128]{2,1,0:T(1,128)S(1)} %bitcast.20), channel_id=1, replica_groups=mesh['depth'=4,'col'=64] {'depth','col'}, dimensions={0} | all-to-all | bytes 262144 | tf_op jit(solution)/shard_map/all_to_all | solution.py:440
  57.5 1.8 %second_conv.1 = (f32[1024,256]{1,0:T(8,128)S(1)}, f32[256,128]{1,0:T(8,128)S(1)}) custom-call(s32[3]{0:T(128)S(1)} %pad_add_fusion.pos, f32[256,128]{1,0:T(8,128)S(1)} %bitcast.14, f32[1024,256]{1,0:T(8,128)S(1)} %get-tuple-element.24.values, bf16[192,192]{1,0:T(8,128)(2,1)S(1)} %get-tuple-element.25.w2), custom_call_target="tpu_custom_call" | custom-call | tf_op jit(solution)/shard_map/second_conv/pallas_call | solution.py:373
  59.3 18.2 %all_to_all.23 = f32[256,1,128]{2,1,0:T(1,128)S(1)} all-to-all(f32[256,1,128]{2,1,0:T(1,128)S(1)} %bitcast.21), channel_id=1, replica_groups=mesh['depth'=4,'col'=64] {'depth','col'}, dimensions={0} | all-to-all | bytes 262144 | tf_op jit(solution)/shard_map/all_to_all | solution.py:440
  77.5 1.4 %final_estimate.1 = f32[8,128]{1,0:T(8,128)S(1)} custom-call(s32[3]{0:T(128)S(1)} %pad_add_fusion.pos, f32[256,128]{1,0:T(8,128)S(1)} %bitcast.15, f32[1024,256]{1,0:T(8,128)S(1)} %get-tuple-element.27.values, bf16[24,192]{1,0:T(8,128)(2,1)S(1)} %get-tuple-element.28.w3), custom_call_target="tpu_custom_call" | custom-call | tf_op jit(solution)/shard_map/final_estimate/pallas_call | solution.py:425
  78.9 0.4 collective-permute-start.7
  79.3 3.1 %collective-permute-start.6 = (f32[8,128]{1,0:T(8,128)S(1)}, f32[8,128]{1,0:T(8,128)S(1)}, u32[]{:S(2)}, u32[]{:S(2)}) collective-permute-start(f32[8,128]{1,0:T(8,128)S(1)} %final_estimate.1), channel_id=1, source_target_pairs={{0,128},{64,192},{128,0},{192,64},{1,129},{65,193},{129,1},{193,65... | collective-permute-start | bytes 12296 | tf_op jit(solution)/shard_map/columns/ppermute | solution.py:461
  82.4 0.6 collective-permute-start.5
  83.0 0.0 collective-permute-done.7
  83.0 1.4 %collective-permute-done.6 = f32[8,128]{1,0:T(8,128)S(1)} collective-permute-done((f32[8,128]{1,0:T(8,128)S(1)}, f32[8,128]{1,0:T(8,128)S(1)}, u32[]{:S(2)}, u32[]{:S(2)}) %collective-permute-start.6) | collective-permute-done | bytes 4128 | tf_op jit(solution)/shard_map/columns/ppermute | solution.py:461
  84.4 1.6 %collective-permute-done.5 = f32[8,128]{1,0:T(8,128)S(1)} collective-permute-done((f32[8,128]{1,0:T(8,128)S(1)}, f32[8,128]{1,0:T(8,128)S(1)}, u32[]{:S(2)}, u32[]{:S(2)}) %collective-permute-start.5) | collective-permute-done | bytes 4128 | tf_op jit(solution)/shard_map/columns/ppermute | solution.py:461
  86.0 0.6 add_add_fusion
  (1 shorter events, 0.0 us)
Async XLA Ops:
  0.0 6.0 %copy-start.2 = (bf16[9,32,32]{2,1,0:T(8,128)(2,1)S(1)}, bf16[9,32,32]{2,1,0:T(8,128)(2,1)}, u32[]{:S(2)}) copy-start(bf16[9,32,32]{2,1,0:T(8,128)(2,1)} %param.8) | copy-start | bytes 55300
  0.0 7.9 %collective-permute-start.2 = (bf16[2,256,128]{2,1,0:T(8,128)(2,1)}, bf16[2,256,128]{2,1,0:T(8,128)(2,1)S(1)}, u32[]{:S(2)}, u32[]{:S(2)}) collective-permute-start(bf16[2,256,128]{2,1,0:T(8,128)(2,1)} %bitcast.16), channel_id=1, source_target_pairs={{0,192},{64,128},{128,64},{192,0},{1,193},{65,129},{129,65},{193,1... | collective-permute-start | bytes 393224 | tf_op jit(solution)/shard_map/views/ppermute | solution.py:449
  1.5 8.1 %collective-permute-start.1 = (bf16[2,256,128]{2,1,0:T(8,128)(2,1)}, bf16[2,256,128]{2,1,0:T(8,128)(2,1)S(1)}, u32[]{:S(2)}, u32[]{:S(2)}) collective-permute-start(bf16[2,256,128]{2,1,0:T(8,128)(2,1)} %bitcast.17), channel_id=1, source_target_pairs={{0,128},{64,192},{128,0},{192,64},{1,129},{65,193},{129,1},{193,65... | collective-permute-start | bytes 393224 | tf_op jit(solution)/shard_map/views/ppermute | solution.py:449
  4.3 5.7 %collective-permute-start = (bf16[2,256,128]{2,1,0:T(8,128)(2,1)}, bf16[2,256,128]{2,1,0:T(8,128)(2,1)S(1)}, u32[]{:S(2)}, u32[]{:S(2)}) collective-permute-start(bf16[2,256,128]{2,1,0:T(8,128)(2,1)} %bitcast.18), channel_id=1, source_target_pairs={{0,64},{64,0},{128,192},{192,128},{1,65},{65,1},{129,193},{193,129... | collective-permute-start | bytes 393224 | tf_op jit(solution)/shard_map/views/ppermute | solution.py:449
  6.0 0.8 copy-start.3
  6.8 1.0 %copy-start = (bf16[2,32,8,128]{3,2,1,0:T(8,128)(2,1)S(1)}, bf16[2,32,8,128]{3,2,1,0:T(8,128)(2,1)}, u32[]{:S(2)}) copy-start(bf16[2,32,8,128]{3,2,1,0:T(8,128)(2,1)} %param.7) | copy-start | bytes 393220
  10.9 2.0 %copy-start.4 = (s32[8,2]{0,1:T(2,128)S(1)}, s32[8,2]{0,1:T(2,128)}, u32[]{:S(2)}) copy-start(s32[8,2]{0,1:T(2,128)} %param.10) | copy-start | bytes 196
  10.9 2.8 %copy-start.1 = (s32[8,96]{1,0:T(8,128)S(1)}, s32[8,96]{1,0:T(8,128)}, u32[]{:S(2)}) copy-start(s32[8,96]{1,0:T(8,128)} %shifts.1) | copy-start | bytes 9220
  10.9 2.8 %collective-permute-start.3 = (bf16[8,256,128]{2,1,0:T(8,128)(2,1)S(1)}, bf16[8,256,128]{2,1,0:T(8,128)(2,1)S(1)}, u32[]{:S(2)}, u32[]{:S(2)}) collective-permute-start(bf16[8,256,128]{2,1,0:T(8,128)(2,1)S(1)} %get-tuple-element.19.every), channel_id=1, source_target_pairs={{0,1},{1,2},{2,3},{3,4},{4,5},{5,6},{6,7},{7,8},{8,9},{9,10},{10,1... | collective-permute-start | bytes 1572872 | tf_op jit(solution)/shard_map/strips/ppermute | solution.py:455
  12.2 0.8 collective-permute-start.4
  78.9 4.1 %collective-permute-start.7 = (f32[8,128]{1,0:T(8,128)S(1)}, f32[8,128]{1,0:T(8,128)S(1)}, u32[]{:S(2)}, u32[]{:S(2)}) collective-permute-start(f32[8,128]{1,0:T(8,128)S(1)} %final_estimate.1), channel_id=1, source_target_pairs={{0,192},{64,128},{128,64},{192,0},{1,193},{65,129},{129,65},{193,1... | collective-permute-start | bytes 12296 | tf_op jit(solution)/shard_map/columns/ppermute | solution.py:461
  79.3 5.1 %collective-permute-start.6 = (f32[8,128]{1,0:T(8,128)S(1)}, f32[8,128]{1,0:T(8,128)S(1)}, u32[]{:S(2)}, u32[]{:S(2)}) collective-permute-start(f32[8,128]{1,0:T(8,128)S(1)} %final_estimate.1), channel_id=1, source_target_pairs={{0,128},{64,192},{128,0},{192,64},{1,129},{65,193},{129,1},{193,65... | collective-permute-start | bytes 12296 | tf_op jit(solution)/shard_map/columns/ppermute | solution.py:461
  82.4 3.6 %collective-permute-start.5 = (f32[8,128]{1,0:T(8,128)S(1)}, f32[8,128]{1,0:T(8,128)S(1)}, u32[]{:S(2)}, u32[]{:S(2)}) collective-permute-start(f32[8,128]{1,0:T(8,128)S(1)} %final_estimate.1), channel_id=1, source_target_pairs={{0,64},{64,0},{128,192},{192,128},{1,65},{65,1},{129,193},{193,129... | collective-permute-start | bytes 12296 | tf_op jit(solution)/shard_map/columns/ppermute | solution.py:461

commit v6 on v5

--- a/solution.py
+++ b/solution.py
@@ -119,13 +119,16 @@
     )
 
 
-def views_kernel(pos, r0, r1, r2, r3, every, edge):
+def views_kernel(pos, r0, r1, r2, r3, every):
     depth = pos[0]
     for k, r in enumerate((r0, r1, r2, r3)):
         for u in range(2):
             every[2 * (depth ^ k) + u] = r[u]
+
+
+def edges_kernel(pos, every, edge):
     lane = iota((1, STRIP), 1)
-    turn = jnp.where(depth == 0, EDGE, 0)
+    turn = jnp.where(pos[0] == 0, EDGE, 0)
     packed = jnp.zeros((CR, STRIP), F32)
     for v in range(VIEWS):
         x = pltpu.roll(every[v].astype(F32), turn + EDGE * v, axis=1)
@@ -133,6 +136,17 @@
     edge[...] = packed.astype(BF16)
 
 
+def edges(pos, every):
+    return pl.pallas_call(
+        edges_kernel,
+        out_shape=jax.ShapeDtypeStruct((CR, STRIP), BF16),
+        in_specs=[SMEM, VMEM],
+        out_specs=VMEM,
+        compiler_params=PARAMS,
+        name="edges",
+    )(pos, every)
+
+
 def copy_kernel(x, y):
     y[...] = x[...]
 
@@ -151,12 +165,9 @@
 def all_views(pos, parts):
     return pl.pallas_call(
         views_kernel,
-        out_shape=(
-            jax.ShapeDtypeStruct((VIEWS, CR, STRIP), BF16),
-            jax.ShapeDtypeStruct((CR, STRIP), BF16),
-        ),
+        out_shape=jax.ShapeDtypeStruct((VIEWS, CR, STRIP), BF16),
         in_specs=[SMEM] + [VMEM] * 4,
-        out_specs=(VMEM,) * 2,
+        out_specs=VMEM,
         compiler_params=PARAMS,
         name="all_views",
     )(pos, *parts)
@@ -330,12 +341,12 @@
     inverse = gathered(0, even)
     for k in range(BLOCKS):
         here, there = (even, odd) if k % 2 == 0 else (odd, even)
-        later = gathered(k + 1, there) if k + 1 < BLOCKS else None
+        for r in range(CR // 16):
+            spread(k, 16 * r, here, inverse)
+        if k + 1 < BLOCKS:
+            inverse = gathered(k + 1, there)
         if k >= 3:
             conv_block(w1, vol, CR, out, k - 2)
-        for r in range(CR // 16):
-            spread(k, 16 * r, here, inverse)
-        inverse = later
     wrap_blocks(vol, CR)
     for k in (0, BLOCKS - 2, BLOCKS - 1):
         conv_block(w1, vol, CR, out, k)
@@ -448,12 +459,12 @@
         wf, w1, w2, w3 = make_weights(feat_weight, cost_weight, mid_weight, final_weight)
         parts = [copied(own)] + [lax.ppermute(own, "depth", [(i, i ^ k) for i in range(4)]) for k in (1, 2, 3)]
         wf, turned = lax.optimization_barrier((wf, pos))
-        every, edge = all_views(turned, parts)
+        every = all_views(turned, parts)
     with jax.named_scope("strips"):
         cols = lax.axis_size("col")
         far = [(i, i + 2) for i in range(cols - 2)] + [(3 * cols + i, 3 * cols + i - 1) for i in range(1, cols)]
         left = lax.ppermute(every, "col", [(i, i + 1) for i in range(cols - 1)])
-        edge = lax.ppermute(edge, ("depth", "col"), far)
+        edge = lax.ppermute(edges(pos, every), ("depth", "col"), far)
     first, stats = cost_and_conv(pos, shifts, frame_range, every, left, edge, wf, w1)
     second, stats = second_conv(pos, everyones(stats), first, w2)
     part = final_estimate(pos, everyones(stats), second, w3)

time: 86.9 us -> 86.7 us (level)
  transfers between devices with their start and end apart: 8 -> 8, of which waited for: 5 -> 4; matrix products, arithmetic and copies ran while one was open for 2% -> 2% of each run, Pallas kernels for 1% -> 2%
where the time goes in v6:
time: 86.7 us; the launch traced here: 86.4 us
  blocking collectives  52.8 us (61%)
  Pallas kernels  14.6 us (17%)
  starting transfers between devices  10.4 us (12%)
  waiting for transfers between devices  5.21 us (6%)
  local copies, waits for them, and re-layouts  2.54 us (3%)
    all_to_all x2, blocking collectives, everyones(): return lax.all_to_all(stats, ('depth', 'col'), 0, 0, tiled=True)  52.8 us
    pallas_call x1, Pallas kernels, cost_and_conv(): pl.pallas_call(volume_kernel, out_shape=(jax.ShapeDtypeStruct((BLOCKS * H...  9.04 us
    ppermute x3, starting transfers between devices, local(): lax.ppermute(own, 'depth', [(i, i ^ k) for i in range(4)])  4.34 us
    ppermute x3, starting transfers between devices, local(): lax.ppermute(part, 'depth', [(i, i ^ k) for i in range(4)])  4.12 us
    ppermute x3, waiting for transfers between devices, local(): lax.ppermute(part, 'depth', [(i, i ^ k) for i in range(4)])  3.03 us
    unnamed x13, local copies, waits for them, and re-layouts  2.54 us
    ppermute x3, waiting for transfers between devices, local(): lax.ppermute(own, 'depth', [(i, i ^ k) for i in range(4)])  2.18 us
    pallas_call x1, Pallas kernels, second_conv(): pl.pallas_call(middle_kernel, out_shape=(jax.ShapeDtypeStruct((BLOCKS * H...  1.84 us
  transfers between devices with their start and end apart: 8, of which 4 were waited for; matrix products, arithmetic and copies ran while one was open for 2% of the time, Pallas kernels for 2%

profile of v6, /device:TPU:2, one launch (start us, length us, event | category | flops | bytes accessed | tf_op | source)
XLA Modules:
  0.0 86.4 jit_solution(17297484012552856981)
XLA Ops:
  0.0 0.0 copy-start.2
  0.0 1.5 %collective-permute-start.2 = (bf16[2,256,128]{2,1,0:T(8,128)(2,1)}, bf16[2,256,128]{2,1,0:T(8,128)(2,1)S(1)}, u32[]{:S(2)}, u32[]{:S(2)}) collective-permute-start(bf16[2,256,128]{2,1,0:T(8,128)(2,1)} %bitcast.16), channel_id=1, source_target_pairs={{0,192},{64,128},{128,64},{192,0},{1,193},{65,129},{129,65},{193,1... | collective-permute-start | bytes 393224 | tf_op jit(solution)/shard_map/views/ppermute | solution.py:460
  1.5 2.8 %collective-permute-start.1 = (bf16[2,256,128]{2,1,0:T(8,128)(2,1)}, bf16[2,256,128]{2,1,0:T(8,128)(2,1)S(1)}, u32[]{:S(2)}, u32[]{:S(2)}) collective-permute-start(bf16[2,256,128]{2,1,0:T(8,128)(2,1)} %bitcast.17), channel_id=1, source_target_pairs={{0,128},{64,192},{128,0},{192,64},{1,129},{65,193},{129,1},{193,65... | collective-permute-start | bytes 393224 | tf_op jit(solution)/shard_map/views/ppermute | solution.py:460
  4.3 0.0 collective-permute-start
  4.3 0.8 copy.12.lw
  5.1 0.9 copy.11
  6.0 0.0 copy-done.2
  6.0 0.0 copy-start.3
  6.0 0.8 copy-done.3
  6.8 0.0 copy-start
  6.8 1.0 %banded_weights.1 = (bf16[256,768]{1,0:T(8,128)(2,1)S(1)}, bf16[192,768]{1,0:T(8,128)(2,1)S(1)}, bf16[192,192]{1,0:T(8,128)(2,1)S(1)}, bf16[24,192]{1,0:T(8,128)(2,1)S(1)}) custom-call(bf16[288,32]{1,0:T(8,128)(2,1)S(1)} %bitcast.23, bf16[216,32]{1,0:T(8,128)(2,1)S(1)} %bitcast.24, bf16[216,8]{1,0:T(8,128)(2,1)S(1)} %bitcast.22, bf16[27,8]{1,0:T(8,128)(2,1)S(1)} %copy.12.lw), custom_call_target="tpu_custom_call" | custom-call | flops 2000000000 | bytes 1000000 | tf_op jit(solution)/shard_map/views/banded_weights/pallas_call | solution.py:101
  7.8 0.0 copy-done
  7.8 0.1 pad_add_fusion.pos
  7.9 0.0 collective-permute-done.2.r3
  7.9 1.7 %collective-permute-done.1.r2 = bf16[2,256,128]{2,1,0:T(8,128)(2,1)S(1)} collective-permute-done((bf16[2,256,128]{2,1,0:T(8,128)(2,1)}, bf16[2,256,128]{2,1,0:T(8,128)(2,1)S(1)}, u32[]{:S(2)}, u32[]{:S(2)}) %collective-permute-start.1) | collective-permute-done | bytes 131104 | tf_op jit(solution)/shard_map/views/ppermute | solution.py:460
  9.6 0.5 collective-permute-done.r1
  10.1 0.6 all_views.1.every
  10.7 0.0 copy-start.4
  10.7 1.3 %collective-permute-start.3 = (bf16[8,256,128]{2,1,0:T(8,128)(2,1)S(1)}, bf16[8,256,128]{2,1,0:T(8,128)(2,1)S(1)}, u32[]{:S(2)}, u32[]{:S(2)}) collective-permute-start(bf16[8,256,128]{2,1,0:T(8,128)(2,1)S(1)} %all_views.1.every), channel_id=1, source_target_pairs={{0,1},{1,2},{2,3},{3,4},{4,5},{5,6},{6,7},{7,8},{8,9},{9,10},{10,1... | collective-permute-start | bytes 1572872 | tf_op jit(solution)/shard_map/strips/ppermute | solution.py:466
  12.0 0.7 edges.1
  12.8 0.0 copy-start.1
  12.8 0.7 collective-permute-start.4
  13.5 0.0 copy-done.4
  13.5 0.1 copy.13.frame
  13.6 0.0 collective-permute-done.4.edge
  13.6 0.0 collective-permute-done.3.left
  13.6 0.0 copy-done.1
  13.6 9.0 %cost_volume.1 = (f32[1024,256]{1,0:T(8,128)S(1)}, f32[256,128]{1,0:T(8,128)S(1)}) custom-call(s32[3]{0:T(128)S(1)} %pad_add_fusion.pos, s32[8,96]{1,0:T(8,128)S(1)} %copy-done.1, s32[8,2]{1,0:T(8,128)S(1)} %copy.13.frame, bf16[8,256,128]{2,1,0:T(8,128)(2,1)S(1)} %all_views.1.every, bf16[8,256,128]{2,1,0:T(8,128)(2,1)S(1)} %collective-permute-done.3.left, ...), custom_call_target="tpu_custom_call" | custom-call | tf_op jit(solution)/shard_map/cost_volume/pallas_call | solution.py:357
  22.6 34.7 %all_to_all.22 = f32[256,1,128]{2,1,0:T(1,128)S(1)} all-to-all(f32[256,1,128]{2,1,0:T(1,128)S(1)} %bitcast.20), channel_id=1, replica_groups=mesh['depth'=4,'col'=64] {'depth','col'}, dimensions={0} | all-to-all | bytes 262144 | tf_op jit(solution)/shard_map/all_to_all | solution.py:451
  57.3 1.8 %second_conv.1 = (f32[1024,256]{1,0:T(8,128)S(1)}, f32[256,128]{1,0:T(8,128)S(1)}) custom-call(s32[3]{0:T(128)S(1)} %pad_add_fusion.pos, f32[256,128]{1,0:T(8,128)S(1)} %bitcast.14, f32[1024,256]{1,0:T(8,128)S(1)} %get-tuple-element.20.values, bf16[192,192]{1,0:T(8,128)(2,1)S(1)} %get-tuple-element.21.w2), custom_call_target="tpu_custom_call" | custom-call | tf_op jit(solution)/shard_map/second_conv/pallas_call | solution.py:384
  59.1 18.2 %all_to_all.23 = f32[256,1,128]{2,1,0:T(1,128)S(1)} all-to-all(f32[256,1,128]{2,1,0:T(1,128)S(1)} %bitcast.21), channel_id=1, replica_groups=mesh['depth'=4,'col'=64] {'depth','col'}, dimensions={0} | all-to-all | bytes 262144 | tf_op jit(solution)/shard_map/all_to_all | solution.py:451
  77.3 1.4 %final_estimate.1 = f32[8,128]{1,0:T(8,128)S(1)} custom-call(s32[3]{0:T(128)S(1)} %pad_add_fusion.pos, f32[256,128]{1,0:T(8,128)S(1)} %bitcast.15, f32[1024,256]{1,0:T(8,128)S(1)} %get-tuple-element.23.values, bf16[24,192]{1,0:T(8,128)(2,1)S(1)} %get-tuple-element.24.w3), custom_call_target="tpu_custom_call" | custom-call | tf_op jit(solution)/shard_map/final_estimate/pallas_call | solution.py:436
  78.7 0.4 collective-permute-start.7
  79.1 3.1 %collective-permute-start.6 = (f32[8,128]{1,0:T(8,128)S(1)}, f32[8,128]{1,0:T(8,128)S(1)}, u32[]{:S(2)}, u32[]{:S(2)}) collective-permute-start(f32[8,128]{1,0:T(8,128)S(1)} %final_estimate.1), channel_id=1, source_target_pairs={{0,128},{64,192},{128,0},{192,64},{1,129},{65,193},{129,1},{193,65... | collective-permute-start | bytes 12296 | tf_op jit(solution)/shard_map/columns/ppermute | solution.py:472
  82.2 0.6 collective-permute-start.5
  82.8 0.0 collective-permute-done.7
  82.8 1.4 %collective-permute-done.6 = f32[8,128]{1,0:T(8,128)S(1)} collective-permute-done((f32[8,128]{1,0:T(8,128)S(1)}, f32[8,128]{1,0:T(8,128)S(1)}, u32[]{:S(2)}, u32[]{:S(2)}) %collective-permute-start.6) | collective-permute-done | bytes 4128 | tf_op jit(solution)/shard_map/columns/ppermute | solution.py:472
  84.2 1.6 %collective-permute-done.5 = f32[8,128]{1,0:T(8,128)S(1)} collective-permute-done((f32[8,128]{1,0:T(8,128)S(1)}, f32[8,128]{1,0:T(8,128)S(1)}, u32[]{:S(2)}, u32[]{:S(2)}) %collective-permute-start.5) | collective-permute-done | bytes 4128 | tf_op jit(solution)/shard_map/columns/ppermute | solution.py:472
  85.8 0.6 add_add_fusion
  (1 shorter events, 0.0 us)
Async XLA Ops:
  0.0 6.0 %copy-start.2 = (bf16[9,32,32]{2,1,0:T(8,128)(2,1)S(1)}, bf16[9,32,32]{2,1,0:T(8,128)(2,1)}, u32[]{:S(2)}) copy-start(bf16[9,32,32]{2,1,0:T(8,128)(2,1)} %param.8) | copy-start | bytes 55300
  0.0 7.9 %collective-permute-start.2 = (bf16[2,256,128]{2,1,0:T(8,128)(2,1)}, bf16[2,256,128]{2,1,0:T(8,128)(2,1)S(1)}, u32[]{:S(2)}, u32[]{:S(2)}) collective-permute-start(bf16[2,256,128]{2,1,0:T(8,128)(2,1)} %bitcast.16), channel_id=1, source_target_pairs={{0,192},{64,128},{128,64},{192,0},{1,193},{65,129},{129,65},{193,1... | collective-permute-start | bytes 393224 | tf_op jit(solution)/shard_map/views/ppermute | solution.py:460
  1.5 8.1 %collective-permute-start.1 = (bf16[2,256,128]{2,1,0:T(8,128)(2,1)}, bf16[2,256,128]{2,1,0:T(8,128)(2,1)S(1)}, u32[]{:S(2)}, u32[]{:S(2)}) collective-permute-start(bf16[2,256,128]{2,1,0:T(8,128)(2,1)} %bitcast.17), channel_id=1, source_target_pairs={{0,128},{64,192},{128,0},{192,64},{1,129},{65,193},{129,1},{193,65... | collective-permute-start | bytes 393224 | tf_op jit(solution)/shard_map/views/ppermute | solution.py:460
  4.3 5.7 %collective-permute-start = (bf16[2,256,128]{2,1,0:T(8,128)(2,1)}, bf16[2,256,128]{2,1,0:T(8,128)(2,1)S(1)}, u32[]{:S(2)}, u32[]{:S(2)}) collective-permute-start(bf16[2,256,128]{2,1,0:T(8,128)(2,1)} %bitcast.18), channel_id=1, source_target_pairs={{0,64},{64,0},{128,192},{192,128},{1,65},{65,1},{129,193},{193,129... | collective-permute-start | bytes 393224 | tf_op jit(solution)/shard_map/views/ppermute | solution.py:460
  6.0 0.8 copy-start.3
  6.8 1.0 %copy-start = (bf16[2,32,8,128]{3,2,1,0:T(8,128)(2,1)S(1)}, bf16[2,32,8,128]{3,2,1,0:T(8,128)(2,1)}, u32[]{:S(2)}) copy-start(bf16[2,32,8,128]{3,2,1,0:T(8,128)(2,1)} %param.7) | copy-start | bytes 393220
  10.7 2.8 %copy-start.4 = (s32[8,2]{0,1:T(2,128)S(1)}, s32[8,2]{0,1:T(2,128)}, u32[]{:S(2)}) copy-start(s32[8,2]{0,1:T(2,128)} %param.10) | copy-start | bytes 196
  10.7 2.9 %collective-permute-start.3 = (bf16[8,256,128]{2,1,0:T(8,128)(2,1)S(1)}, bf16[8,256,128]{2,1,0:T(8,128)(2,1)S(1)}, u32[]{:S(2)}, u32[]{:S(2)}) collective-permute-start(bf16[8,256,128]{2,1,0:T(8,128)(2,1)S(1)} %all_views.1.every), channel_id=1, source_target_pairs={{0,1},{1,2},{2,3},{3,4},{4,5},{5,6},{6,7},{7,8},{8,9},{9,10},{10,1... | collective-permute-start | bytes 1572872 | tf_op jit(solution)/shard_map/strips/ppermute | solution.py:466
  12.8 0.8 copy-start.1
  12.8 0.8 collective-permute-start.4
  78.7 4.1 %collective-permute-start.7 = (f32[8,128]{1,0:T(8,128)S(1)}, f32[8,128]{1,0:T(8,128)S(1)}, u32[]{:S(2)}, u32[]{:S(2)}) collective-permute-start(f32[8,128]{1,0:T(8,128)S(1)} %final_estimate.1), channel_id=1, source_target_pairs={{0,192},{64,128},{128,64},{192,0},{1,193},{65,129},{129,65},{193,1... | collective-permute-start | bytes 12296 | tf_op jit(solution)/shard_map/columns/ppermute | solution.py:472
  79.1 5.1 %collective-permute-start.6 = (f32[8,128]{1,0:T(8,128)S(1)}, f32[8,128]{1,0:T(8,128)S(1)}, u32[]{:S(2)}, u32[]{:S(2)}) collective-permute-start(f32[8,128]{1,0:T(8,128)S(1)} %final_estimate.1), channel_id=1, source_target_pairs={{0,128},{64,192},{128,0},{192,64},{1,129},{65,193},{129,1},{193,65... | collective-permute-start | bytes 12296 | tf_op jit(solution)/shard_map/columns/ppermute | solution.py:472
  82.2 3.6 %collective-permute-start.5 = (f32[8,128]{1,0:T(8,128)S(1)}, f32[8,128]{1,0:T(8,128)S(1)}, u32[]{:S(2)}, u32[]{:S(2)}) collective-permute-start(f32[8,128]{1,0:T(8,128)S(1)} %final_estimate.1), channel_id=1, source_target_pairs={{0,64},{64,0},{128,192},{192,128},{1,65},{65,1},{129,193},{193,129... | collective-permute-start | bytes 12296 | tf_op jit(solution)/shard_map/columns/ppermute | solution.py:472

commit v7 on v6

--- a/solution.py
+++ b/solution.py
@@ -324,13 +324,13 @@
     def spread(k, r, moved, inverse):
         total = squares = None
         for v in range(VIEWS - 1):
-            p = moved[v, r : r + 16, :]
+            p = moved[v, r : r + 32, :]
             total = p if total is None else total + p
             squares = p * p if squares is None else squares + p * p
         average = total * inverse
         value = squares * inverse - average * average
         row = (k + 1) * CR + r
-        vol[row : row + 16, :] = jnp.maximum(value, 0.0).astype(BF16)
+        vol[row : row + 32, :] = jnp.maximum(value, 0.0).astype(BF16)
 
     def gathered(k, moved):
         tally = jnp.ones((1, WIDE), F32)
@@ -341,8 +341,8 @@
     inverse = gathered(0, even)
     for k in range(BLOCKS):
         here, there = (even, odd) if k % 2 == 0 else (odd, even)
-        for r in range(CR // 16):
-            spread(k, 16 * r, here, inverse)
+        for r in range(CR // 32):
+            spread(k, 32 * r, here, inverse)
         if k + 1 < BLOCKS:
             inverse = gathered(k + 1, there)
         if k >= 3:

time: 86.7 us -> 86.7 us (level)
  no operation moved by 1% of the time
where the time goes in v7:
time: 86.7 us; the launch traced here: 86.4 us
  blocking collectives  52.8 us (61%)
  Pallas kernels  14.6 us (17%)
  starting transfers between devices  10.4 us (12%)
  waiting for transfers between devices  5.21 us (6%)
  local copies, waits for them, and re-layouts  2.54 us (3%)
    all_to_all x2, blocking collectives, everyones(): return lax.all_to_all(stats, ('depth', 'col'), 0, 0, tiled=True)  52.8 us
    pallas_call x1, Pallas kernels, cost_and_conv(): pl.pallas_call(volume_kernel, out_shape=(jax.ShapeDtypeStruct((BLOCKS * H...  9.04 us
    ppermute x3, starting transfers between devices, local(): lax.ppermute(own, 'depth', [(i, i ^ k) for i in range(4)])  4.34 us
    ppermute x3, starting transfers between devices, local(): lax.ppermute(part, 'depth', [(i, i ^ k) for i in range(4)])  4.12 us
    ppermute x3, waiting for transfers between devices, local(): lax.ppermute(part, 'depth', [(i, i ^ k) for i in range(4)])  3.03 us
    unnamed x13, local copies, waits for them, and re-layouts  2.54 us
    ppermute x3, waiting for transfers between devices, local(): lax.ppermute(own, 'depth', [(i, i ^ k) for i in range(4)])  2.18 us
    pallas_call x1, Pallas kernels, second_conv(): pl.pallas_call(middle_kernel, out_shape=(jax.ShapeDtypeStruct((BLOCKS * H...  1.84 us
  transfers between devices with their start and end apart: 8, of which 4 were waited for; matrix products, arithmetic and copies ran while one was open for 2% of the time, Pallas kernels for 2%

profile of v7, /device:TPU:2, one launch (start us, length us, event | category | flops | bytes accessed | tf_op | source)
XLA Modules:
  0.0 86.4 jit_solution(17297484012552856981)
XLA Ops:
  0.0 0.0 copy-start.2
  0.0 1.5 %collective-permute-start.2 = (bf16[2,256,128]{2,1,0:T(8,128)(2,1)}, bf16[2,256,128]{2,1,0:T(8,128)(2,1)S(1)}, u32[]{:S(2)}, u32[]{:S(2)}) collective-permute-start(bf16[2,256,128]{2,1,0:T(8,128)(2,1)} %bitcast.16), channel_id=1, source_target_pairs={{0,192},{64,128},{128,64},{192,0},{1,193},{65,129},{129,65},{193,1... | collective-permute-start | bytes 393224 | tf_op jit(solution)/shard_map/views/ppermute | solution.py:460
  1.5 2.8 %collective-permute-start.1 = (bf16[2,256,128]{2,1,0:T(8,128)(2,1)}, bf16[2,256,128]{2,1,0:T(8,128)(2,1)S(1)}, u32[]{:S(2)}, u32[]{:S(2)}) collective-permute-start(bf16[2,256,128]{2,1,0:T(8,128)(2,1)} %bitcast.17), channel_id=1, source_target_pairs={{0,128},{64,192},{128,0},{192,64},{1,129},{65,193},{129,1},{193,65... | collective-permute-start | bytes 393224 | tf_op jit(solution)/shard_map/views/ppermute | solution.py:460
  4.3 0.0 collective-permute-start
  4.3 0.8 copy.12.lw
  5.1 0.9 copy.11
  6.0 0.0 copy-done.2
  6.0 0.0 copy-start.3
  6.0 0.8 copy-done.3
  6.8 0.0 copy-start
  6.8 1.0 %banded_weights.1 = (bf16[256,768]{1,0:T(8,128)(2,1)S(1)}, bf16[192,768]{1,0:T(8,128)(2,1)S(1)}, bf16[192,192]{1,0:T(8,128)(2,1)S(1)}, bf16[24,192]{1,0:T(8,128)(2,1)S(1)}) custom-call(bf16[288,32]{1,0:T(8,128)(2,1)S(1)} %bitcast.23, bf16[216,32]{1,0:T(8,128)(2,1)S(1)} %bitcast.24, bf16[216,8]{1,0:T(8,128)(2,1)S(1)} %bitcast.22, bf16[27,8]{1,0:T(8,128)(2,1)S(1)} %copy.12.lw), custom_call_target="tpu_custom_call" | custom-call | flops 2000000000 | bytes 1000000 | tf_op jit(solution)/shard_map/views/banded_weights/pallas_call | solution.py:101
  7.8 0.0 copy-done
  7.8 0.1 pad_add_fusion.pos
  7.9 0.0 collective-permute-done.2.r3
  7.9 1.7 %collective-permute-done.1.r2 = bf16[2,256,128]{2,1,0:T(8,128)(2,1)S(1)} collective-permute-done((bf16[2,256,128]{2,1,0:T(8,128)(2,1)}, bf16[2,256,128]{2,1,0:T(8,128)(2,1)S(1)}, u32[]{:S(2)}, u32[]{:S(2)}) %collective-permute-start.1) | collective-permute-done | bytes 131104 | tf_op jit(solution)/shard_map/views/ppermute | solution.py:460
  9.6 0.5 collective-permute-done.r1
  10.1 0.6 all_views.1.every
  10.7 0.0 copy-start.4
  10.7 1.3 %collective-permute-start.3 = (bf16[8,256,128]{2,1,0:T(8,128)(2,1)S(1)}, bf16[8,256,128]{2,1,0:T(8,128)(2,1)S(1)}, u32[]{:S(2)}, u32[]{:S(2)}) collective-permute-start(bf16[8,256,128]{2,1,0:T(8,128)(2,1)S(1)} %all_views.1.every), channel_id=1, source_target_pairs={{0,1},{1,2},{2,3},{3,4},{4,5},{5,6},{6,7},{7,8},{8,9},{9,10},{10,1... | collective-permute-start | bytes 1572872 | tf_op jit(solution)/shard_map/strips/ppermute | solution.py:466
  12.0 0.7 edges.1
  12.8 0.0 copy-start.1
  12.8 0.7 collective-permute-start.4
  13.5 0.0 copy-done.4
  13.5 0.1 copy.13.frame
  13.6 0.0 collective-permute-done.4.edge
  13.6 0.0 collective-permute-done.3.left
  13.6 0.0 copy-done.1
  13.6 9.0 %cost_volume.1 = (f32[1024,256]{1,0:T(8,128)S(1)}, f32[256,128]{1,0:T(8,128)S(1)}) custom-call(s32[3]{0:T(128)S(1)} %pad_add_fusion.pos, s32[8,96]{1,0:T(8,128)S(1)} %copy-done.1, s32[8,2]{1,0:T(8,128)S(1)} %copy.13.frame, bf16[8,256,128]{2,1,0:T(8,128)(2,1)S(1)} %all_views.1.every, bf16[8,256,128]{2,1,0:T(8,128)(2,1)S(1)} %collective-permute-done.3.left, ...), custom_call_target="tpu_custom_call" | custom-call | tf_op jit(solution)/shard_map/cost_volume/pallas_call | solution.py:357
  22.6 34.7 %all_to_all.22 = f32[256,1,128]{2,1,0:T(1,128)S(1)} all-to-all(f32[256,1,128]{2,1,0:T(1,128)S(1)} %bitcast.20), channel_id=1, replica_groups=mesh['depth'=4,'col'=64] {'depth','col'}, dimensions={0} | all-to-all | bytes 262144 | tf_op jit(solution)/shard_map/all_to_all | solution.py:451
  57.3 1.8 %second_conv.1 = (f32[1024,256]{1,0:T(8,128)S(1)}, f32[256,128]{1,0:T(8,128)S(1)}) custom-call(s32[3]{0:T(128)S(1)} %pad_add_fusion.pos, f32[256,128]{1,0:T(8,128)S(1)} %bitcast.14, f32[1024,256]{1,0:T(8,128)S(1)} %get-tuple-element.20.values, bf16[192,192]{1,0:T(8,128)(2,1)S(1)} %get-tuple-element.21.w2), custom_call_target="tpu_custom_call" | custom-call | tf_op jit(solution)/shard_map/second_conv/pallas_call | solution.py:384
  59.1 18.2 %all_to_all.23 = f32[256,1,128]{2,1,0:T(1,128)S(1)} all-to-all(f32[256,1,128]{2,1,0:T(1,128)S(1)} %bitcast.21), channel_id=1, replica_groups=mesh['depth'=4,'col'=64] {'depth','col'}, dimensions={0} | all-to-all | bytes 262144 | tf_op jit(solution)/shard_map/all_to_all | solution.py:451
  77.3 1.4 %final_estimate.1 = f32[8,128]{1,0:T(8,128)S(1)} custom-call(s32[3]{0:T(128)S(1)} %pad_add_fusion.pos, f32[256,128]{1,0:T(8,128)S(1)} %bitcast.15, f32[1024,256]{1,0:T(8,128)S(1)} %get-tuple-element.23.values, bf16[24,192]{1,0:T(8,128)(2,1)S(1)} %get-tuple-element.24.w3), custom_call_target="tpu_custom_call" | custom-call | tf_op jit(solution)/shard_map/final_estimate/pallas_call | solution.py:436
  78.7 0.4 collective-permute-start.7
  79.1 3.1 %collective-permute-start.6 = (f32[8,128]{1,0:T(8,128)S(1)}, f32[8,128]{1,0:T(8,128)S(1)}, u32[]{:S(2)}, u32[]{:S(2)}) collective-permute-start(f32[8,128]{1,0:T(8,128)S(1)} %final_estimate.1), channel_id=1, source_target_pairs={{0,128},{64,192},{128,0},{192,64},{1,129},{65,193},{129,1},{193,65... | collective-permute-start | bytes 12296 | tf_op jit(solution)/shard_map/columns/ppermute | solution.py:472
  82.2 0.6 collective-permute-start.5
  82.8 0.0 collective-permute-done.7
  82.8 1.4 %collective-permute-done.6 = f32[8,128]{1,0:T(8,128)S(1)} collective-permute-done((f32[8,128]{1,0:T(8,128)S(1)}, f32[8,128]{1,0:T(8,128)S(1)}, u32[]{:S(2)}, u32[]{:S(2)}) %collective-permute-start.6) | collective-permute-done | bytes 4128 | tf_op jit(solution)/shard_map/columns/ppermute | solution.py:472
  84.2 1.6 %collective-permute-done.5 = f32[8,128]{1,0:T(8,128)S(1)} collective-permute-done((f32[8,128]{1,0:T(8,128)S(1)}, f32[8,128]{1,0:T(8,128)S(1)}, u32[]{:S(2)}, u32[]{:S(2)}) %collective-permute-start.5) | collective-permute-done | bytes 4128 | tf_op jit(solution)/shard_map/columns/ppermute | solution.py:472
  85.8 0.6 add_add_fusion
  (1 shorter events, 0.0 us)
Async XLA Ops:
  0.0 6.0 %copy-start.2 = (bf16[9,32,32]{2,1,0:T(8,128)(2,1)S(1)}, bf16[9,32,32]{2,1,0:T(8,128)(2,1)}, u32[]{:S(2)}) copy-start(bf16[9,32,32]{2,1,0:T(8,128)(2,1)} %param.8) | copy-start | bytes 55300
  0.0 7.9 %collective-permute-start.2 = (bf16[2,256,128]{2,1,0:T(8,128)(2,1)}, bf16[2,256,128]{2,1,0:T(8,128)(2,1)S(1)}, u32[]{:S(2)}, u32[]{:S(2)}) collective-permute-start(bf16[2,256,128]{2,1,0:T(8,128)(2,1)} %bitcast.16), channel_id=1, source_target_pairs={{0,192},{64,128},{128,64},{192,0},{1,193},{65,129},{129,65},{193,1... | collective-permute-start | bytes 393224 | tf_op jit(solution)/shard_map/views/ppermute | solution.py:460
  1.5 8.1 %collective-permute-start.1 = (bf16[2,256,128]{2,1,0:T(8,128)(2,1)}, bf16[2,256,128]{2,1,0:T(8,128)(2,1)S(1)}, u32[]{:S(2)}, u32[]{:S(2)}) collective-permute-start(bf16[2,256,128]{2,1,0:T(8,128)(2,1)} %bitcast.17), channel_id=1, source_target_pairs={{0,128},{64,192},{128,0},{192,64},{1,129},{65,193},{129,1},{193,65... | collective-permute-start | bytes 393224 | tf_op jit(solution)/shard_map/views/ppermute | solution.py:460
  4.3 5.7 %collective-permute-start = (bf16[2,256,128]{2,1,0:T(8,128)(2,1)}, bf16[2,256,128]{2,1,0:T(8,128)(2,1)S(1)}, u32[]{:S(2)}, u32[]{:S(2)}) collective-permute-start(bf16[2,256,128]{2,1,0:T(8,128)(2,1)} %bitcast.18), channel_id=1, source_target_pairs={{0,64},{64,0},{128,192},{192,128},{1,65},{65,1},{129,193},{193,129... | collective-permute-start | bytes 393224 | tf_op jit(solution)/shard_map/views/ppermute | solution.py:460
  6.0 0.8 copy-start.3
  6.8 1.0 %copy-start = (bf16[2,32,8,128]{3,2,1,0:T(8,128)(2,1)S(1)}, bf16[2,32,8,128]{3,2,1,0:T(8,128)(2,1)}, u32[]{:S(2)}) copy-start(bf16[2,32,8,128]{3,2,1,0:T(8,128)(2,1)} %param.7) | copy-start | bytes 393220
  10.7 2.8 %copy-start.4 = (s32[8,2]{0,1:T(2,128)S(1)}, s32[8,2]{0,1:T(2,128)}, u32[]{:S(2)}) copy-start(s32[8,2]{0,1:T(2,128)} %param.10) | copy-start | bytes 196
  10.7 2.9 %collective-permute-start.3 = (bf16[8,256,128]{2,1,0:T(8,128)(2,1)S(1)}, bf16[8,256,128]{2,1,0:T(8,128)(2,1)S(1)}, u32[]{:S(2)}, u32[]{:S(2)}) collective-permute-start(bf16[8,256,128]{2,1,0:T(8,128)(2,1)S(1)} %all_views.1.every), channel_id=1, source_target_pairs={{0,1},{1,2},{2,3},{3,4},{4,5},{5,6},{6,7},{7,8},{8,9},{9,10},{10,1... | collective-permute-start | bytes 1572872 | tf_op jit(solution)/shard_map/strips/ppermute | solution.py:466
  12.8 0.8 copy-start.1
  12.8 0.8 collective-permute-start.4
  78.7 4.1 %collective-permute-start.7 = (f32[8,128]{1,0:T(8,128)S(1)}, f32[8,128]{1,0:T(8,128)S(1)}, u32[]{:S(2)}, u32[]{:S(2)}) collective-permute-start(f32[8,128]{1,0:T(8,128)S(1)} %final_estimate.1), channel_id=1, source_target_pairs={{0,192},{64,128},{128,64},{192,0},{1,193},{65,129},{129,65},{193,1... | collective-permute-start | bytes 12296 | tf_op jit(solution)/shard_map/columns/ppermute | solution.py:472
  79.1 5.1 %collective-permute-start.6 = (f32[8,128]{1,0:T(8,128)S(1)}, f32[8,128]{1,0:T(8,128)S(1)}, u32[]{:S(2)}, u32[]{:S(2)}) collective-permute-start(f32[8,128]{1,0:T(8,128)S(1)} %final_estimate.1), channel_id=1, source_target_pairs={{0,128},{64,192},{128,0},{192,64},{1,129},{65,193},{129,1},{193,65... | collective-permute-start | bytes 12296 | tf_op jit(solution)/shard_map/columns/ppermute | solution.py:472
  82.2 3.6 %collective-permute-start.5 = (f32[8,128]{1,0:T(8,128)S(1)}, f32[8,128]{1,0:T(8,128)S(1)}, u32[]{:S(2)}, u32[]{:S(2)}) collective-permute-start(f32[8,128]{1,0:T(8,128)S(1)} %final_estimate.1), channel_id=1, source_target_pairs={{0,64},{64,0},{128,192},{192,128},{1,65},{65,1},{129,193},{193,129... | collective-permute-start | bytes 12296 | tf_op jit(solution)/shard_map/columns/ppermute | solution.py:472
